TPU v7x, 512 devices: a whole 4x8x8 slice. The times are simulated.
512 devices in a mesh: expert: 128 (over y, z, core), dp: 4 (over x).
Axes of the slice: x: 4, y: 8, z: 8, core: 2. Of those that a mesh axis runs over, the one named last changes fastest.
Arguments:
- tokens: bfloat16 [16384, 2048], P('expert'), may hold values from -6 to 6
- routes: int32 [16384, 2], P('expert'), may hold values from 0 to 127, as said below
- route_weights: float32 [16384, 2], P('expert'), may hold values from 0.1 to 0.9
- loss_weights: float32 [16384], P('expert'), may hold values from 0.3 to 3
- gate_up: bfloat16 [128, 2, 768, 2048], P('expert', None, 'dp'), may hold values from -0.125 to 0.125
- down_weight: bfloat16 [128, 768, 2048], P('expert', 'dp'), may hold values from -0.21875 to 0.21875
Outputs:
- input_gradient: bfloat16 [16384, 2048], P('expert')
- projection_gradient: bfloat16 [128, 2, 768, 2048], P('expert', None, 'dp')
Inputs may be any that keep to these rules, and one draw needn't show every extreme that they name: `routes`: each row names 2 different experts. One expert, the same for all rows, is named by exactly 4 rows of every aligned block of 128 rows (the tokens of one index of expert); every other expert is named by at most 2 rows of such a block, and some expert by exactly 2 rows of every block.
All inputs are finite; a program needn't handle non-finite values.
Results may differ from a plain program's by a relative error of at most 0.018.
Values may be sent and summed in bfloat16 or wider, within the bound.
No kernel may reach another device: no remote copies, remote signals or barrier semaphores. Data moves between devices by JAX's collectives and lax.ppermute only.
A program may use at most 64 MiB of HBM per device.

v0:
```python
import jax
import jax.numpy as jnp
from jax import lax
from jax.sharding import PartitionSpec as P


def from_root(value, axis, source):
    kept = jnp.where(lax.axis_index(axis) == source, value, 0).astype(value.dtype)
    return lax.psum(kept, axis)


def swish_parts(preact):
    sigmoid_part = jax.nn.sigmoid(preact)
    return (preact * sigmoid_part, sigmoid_part * (1.0 + preact * (1.0 - sigmoid_part)))


def relocate(buffer):
    return lax.all_to_all(buffer, "expert", split_axis=0, concat_axis=0, tiled=True)


def quarter_total(first_term, second_term):
    return (
        lax.psum(first_term.astype(jnp.bfloat16), "dp").astype(jnp.float32),
        lax.psum(second_term.astype(jnp.bfloat16), "dp").astype(jnp.float32),
    )


def local_forward(row_block, weight_in, weight_out, quarter):
    projected = lax.dot_general(
        row_block, weight_in, (((1,), (1,)), ((), ())), preferred_element_type=jnp.float32
    )
    swish_value, _ = swish_parts(projected[:, :quarter])
    hidden = (swish_value * projected[:, quarter:]).astype(jnp.bfloat16)
    return (projected, jnp.dot(hidden, weight_out, preferred_element_type=jnp.float32))


def local_backward(row_block, cotangent, projected, weight_in, weight_out, quarter):
    swish_value, swish_slope = swish_parts(projected[:, :quarter])
    back_hidden = lax.dot_general(
        cotangent, weight_out, (((1,), (1,)), ((), ())), preferred_element_type=jnp.float32
    )
    grad_pre = jnp.concatenate(
        [back_hidden * projected[:, quarter:] * swish_slope, back_hidden * swish_value], axis=1
    ).astype(jnp.bfloat16)
    gradient = lax.dot_general(
        grad_pre, row_block, (((0,), (0,)), ((), ())), preferred_element_type=jnp.float32
    )
    input_part = jnp.dot(grad_pre, weight_in, preferred_element_type=jnp.float32)
    return (input_part, gradient)


def local(tokens, routes, route_weights, loss_weights, gate_up, down_weight):
    experts = lax.axis_size("expert")
    width = tokens.shape[1]
    local_tokens = tokens.shape[0]
    choices_per = routes.shape[1]
    quarter = down_weight.shape[1]
    assignments = local_tokens * choices_per
    hot_rows = 2 * assignments // experts
    capacity = (assignments - hot_rows + experts - 2) // (experts - 1)
    slots = experts * capacity
    flat_routes = routes.reshape(assignments)
    member = flat_routes[:, None] == lax.iota(jnp.int32, experts)[None, :]
    counts = jnp.sum(member.astype(jnp.int32), axis=0)
    busiest = jnp.argmax(counts)
    is_hot = flat_routes == busiest
    cold_member = (member & ~is_hot[:, None]).astype(jnp.bfloat16)
    positions = lax.iota(jnp.int32, assignments)
    earlier = (positions[None, :] < positions[:, None]).astype(jnp.bfloat16)
    rank_table = jnp.dot(earlier, cold_member, preferred_element_type=jnp.float32)
    cold_rank = jnp.sum(rank_table * cold_member.astype(jnp.float32), axis=1).astype(jnp.int32)
    hot_rank = jnp.dot(
        earlier, is_hot.astype(jnp.bfloat16), preferred_element_type=jnp.float32
    ).astype(jnp.int32)
    slot_index = jnp.where(is_hot, 0, flat_routes * capacity + cold_rank)
    hot_index = jnp.where(is_hot, hot_rank, 0)
    placement = (
        (lax.iota(jnp.int32, slots)[:, None] == slot_index[None, :]) & ~is_hot[None, :]
    ).astype(jnp.bfloat16)
    pick_hot = (
        (lax.iota(jnp.int32, hot_rows)[:, None] == hot_index[None, :]) & is_hot[None, :]
    ).astype(jnp.bfloat16)
    place_tokens = jnp.sum(placement.reshape(slots, local_tokens, choices_per), axis=2)
    hot_by_token = jnp.sum(pick_hot.reshape(hot_rows, local_tokens, choices_per), axis=2)
    outgoing = jnp.dot(place_tokens, tokens, preferred_element_type=jnp.float32).astype(
        jnp.bfloat16
    )
    hot_tokens = jnp.dot(hot_by_token, tokens, preferred_element_type=jnp.float32).astype(
        jnp.bfloat16
    )
    own_in = gate_up.reshape(2 * quarter, width)
    own_out = down_weight.reshape(quarter, width)
    shadow_in, shadow_out = (
        from_root(gate_up, "expert", busiest),
        from_root(down_weight, "expert", busiest),
    )
    spare_in = shadow_in.reshape(2 * quarter, width)
    spare_out = shadow_out.reshape(quarter, width)
    rows_in = relocate(outgoing.reshape(experts, capacity, width)).reshape(slots, width)
    cold_projected, cold_partial = local_forward(rows_in, own_in, own_out, quarter)
    hot_projected, hot_term = local_forward(hot_tokens, spare_in, spare_out, quarter)
    cold_sum, hot_sum = quarter_total(cold_partial, hot_term)
    cold_out = cold_sum.astype(jnp.bfloat16)
    hot_out = hot_sum.astype(jnp.bfloat16)
    returned = relocate(cold_out.reshape(experts, capacity, width)).reshape(slots, width)
    per_assign = jnp.where(is_hot[:, None], hot_out[hot_index], returned[slot_index])
    combined = jnp.sum(
        route_weights[:, :, None]
        * per_assign.reshape(local_tokens, choices_per, width).astype(jnp.float32),
        axis=1,
    )
    cotangent = (
        (loss_weights[:, None, None] * route_weights[:, :, None] * combined[:, None, :])
        .astype(jnp.bfloat16)
        .reshape(assignments, width)
    )
    cot_send = jnp.dot(placement, cotangent, preferred_element_type=jnp.float32).astype(
        jnp.bfloat16
    )
    cot_hot = jnp.dot(pick_hot, cotangent, preferred_element_type=jnp.float32).astype(jnp.bfloat16)
    cot_rows = relocate(cot_send.reshape(experts, capacity, width)).reshape(slots, width)
    cold_input, cold_grad = local_backward(
        rows_in, cot_rows, cold_projected, own_in, own_out, quarter
    )
    hot_input, hot_grad = local_backward(
        hot_tokens, cot_hot, hot_projected, spare_in, spare_out, quarter
    )
    cold_in_sum, hot_in_sum = quarter_total(cold_input, hot_input)
    cold_each = cold_in_sum.astype(jnp.bfloat16)
    hot_each = hot_in_sum.astype(jnp.bfloat16)
    returned_in = relocate(cold_each.reshape(experts, capacity, width)).reshape(slots, width)
    input_each = jnp.where(is_hot[:, None], hot_each[hot_index], returned_in[slot_index])
    input_gradient = jnp.sum(
        input_each.reshape(local_tokens, choices_per, width).astype(jnp.float32), axis=1
    ).astype(jnp.bfloat16)
    hot_share = lax.psum_scatter(hot_grad, "expert", scatter_dimension=1, tiled=True)
    hot_final = lax.all_gather(hot_share.astype(jnp.bfloat16), "expert", axis=1, tiled=True)
    is_owner = lax.axis_index("expert") == busiest
    projection_gradient = jnp.where(is_owner, hot_final, cold_grad.astype(jnp.bfloat16))
    return (input_gradient, projection_gradient.reshape(1, 2, quarter, width))


def solution(mesh):
    in_specs = (
        P("expert", None),
        P("expert", None),
        P("expert", None),
        P("expert"),
        P("expert", None, "dp", None),
        P("expert", "dp", None),
    )
    out_specs = (P("expert", None), P("expert", None, "dp", None))
    return jax.shard_map(local, mesh=mesh, in_specs=in_specs, out_specs=out_specs, check_vma=False)
```

profile of v0, /device:TPU:1, one launch (start us, length us, event | category | flops | bytes accessed | tf_op | source)
XLA Modules:
  0.0 681.1 jit_solution(4584187343061269848)
XLA Ops:
  8.1 0.8 copy.27
  9.1 0.7 iota_reduce_fusion
  9.8 0.6 fusion.39
  10.4 0.6 fusion.38
  12.2 0.7 reshape.179
  12.9 48.8 %all_to_all.20 = bf16[128,2,2048]{2,1,0:T(2,128)(2,1)} all-to-all(bf16[128,2,2048]{2,1,0:T(2,128)(2,1)S(1)} %reshape.179), channel_id=1, replica_groups=mesh['expert'=128,'dp'=4] {'expert'}, dimensions={0} | all-to-all | bytes 2097152 | tf_op jit(solution)/shard_map/all_to_all | solution.py:18
  61.7 1.6 reshape.180
  63.4 0.7 fusion.43
  64.1 0.7 copy-done.12
  64.9 1.5 convolution_convert_fusion.4
  66.3 2.5 reshape.183
  69.5 1.2 broadcast_select_fusion.2
  70.8 47.4 %all-reduce.5.cloned.1.call-done = bf16[128,2,2048]{2,1,0:T(2,128)(2,1)} async-done(((bf16[128,2,2048]{2,1,0:T(2,128)(2,1)}), bf16[128,2,2048]{2,1,0:T(2,128)(2,1)}) %all-reduce.5.cloned.1.call-update) | async-done | bytes 1048592 | tf_op jit(solution)/shard_map/psum | solution.py:23
  118.1 16.1 %all-to-all-start.1 = ((bf16[128,2,2048]{2,1,0:T(2,128)(2,1)}), bf16[128,2,2048]{2,1,0:T(2,128)(2,1)}, u32[]{:S(2)}, u32[]{:S(2)}) async-start(bf16[128,2,2048]{2,1,0:T(2,128)(2,1)} %all-reduce.5.cloned.1.call-done), calls=%async_computation.1 | async-start | bytes 2097152 | tf_op jit(solution)/shard_map/all_to_all | solution.py:18
  134.3 0.9 select_bitcast_fusion
  136.8 203.5 %all-reduce.9.cloned.1.call-done = (bf16[384,2048]{1,0:T(8,128)(2,1)}, bf16[192,2048]{1,0:T(8,128)(2,1)}) async-done(((bf16[384,2048]{1,0:T(8,128)(2,1)}, bf16[192,2048]{1,0:T(8,128)(2,1)}), (bf16[384,2048]{1,0:T(8,128)(2,1)}, bf16[192,2048]{1,0:T(8,128)(2,1)})) %all-reduce.9.cloned.1.call-update) | async-done | bytes 2359312 | tf_op jit(solution)/shard_map/psum | solution.py:9
  340.4 2.0 fusion.42
  342.6 13.1 %psum.44 = bf16[4,2048]{1,0:T(4,128)(2,1)S(1)} all-reduce(bf16[4,2048]{1,0:T(4,128)(2,1)S(1)} %convolution_convert_fusion.7), channel_id=1, replica_groups=mesh['expert'=128,'dp'=4] {'dp'}, use_global_device_ids=true, to_apply=%region_5.6 | all-reduce | flops 8192 | bytes 32768 | tf_op jit(solution)/shard_map/psum | solution.py:24
  355.7 1.4 gather_fusion
  357.1 0.7 gather.21
  357.8 1.5 reshape.184
  359.3 2.3 gather_fusion.1
  361.7 1.7 gather.23
  363.4 5.2 multiply_reduce_fusion
  368.6 2.5 mul.121
  371.2 2.7 mul.122
  373.9 0.5 multiply_convert_fusion.6
  374.5 2.3 fusion.32
  376.8 1.5 convolution_convert_fusion.3
  378.3 1.7 reshape.185
  380.1 44.8 %all_to_all.21 = bf16[128,2,2048]{2,1,0:T(2,128)(2,1)S(1)} all-to-all(bf16[128,2,2048]{2,1,0:T(2,128)(2,1)S(1)} %reshape.185), channel_id=1, replica_groups=mesh['expert'=128,'dp'=4] {'expert'}, dimensions={0} | all-to-all | bytes 2097152 | tf_op jit(solution)/shard_map/all_to_all | solution.py:18
  425.3 0.7 copy-done.9
  426.0 1.6 multiply_convert_fusion.2
  427.6 0.7 convolution_convert_fusion.1
  428.4 1.5 reshape.187
  430.0 142.3 %reduce-scatter.2.cloned.1.call-done = f32[384,16]{0,1:T(8,128)} async-done(((f32[384,2048]{0,1:T(8,128)}), f32[384,16]{0,1:T(8,128)}) %reduce-scatter.2.cloned.1.call-update) | async-done | bytes 24592 | tf_op jit(solution)/shard_map/reduce_scatter | solution.py:136
  572.3 1.3 convert_element_type.127
  573.7 14.7 %all-to-all-start.3 = ((bf16[128,2,2048]{2,1,0:T(2,128)(2,1)}), bf16[128,2,2048]{2,1,0:T(2,128)(2,1)S(1)}, u32[]{:S(2)}, u32[]{:S(2)}) async-start(bf16[128,2,2048]{2,1,0:T(2,128)(2,1)} %all-reduce.7.cloned.1.call-done), calls=%async_computation.3 | async-start | bytes 2097152 | tf_op jit(solution)/shard_map/all_to_all | solution.py:18
  588.8 14.4 %psum.46 = bf16[4,2048]{1,0:T(4,128)(2,1)S(1)} all-reduce(bf16[4,2048]{1,0:T(4,128)(2,1)S(1)} %convolution_convert_fusion.5), channel_id=1, replica_groups=mesh['expert'=128,'dp'=4] {'dp'}, use_global_device_ids=true, to_apply=%region_10.11 | all-reduce | flops 8192 | bytes 32768 | tf_op jit(solution)/shard_map/psum | solution.py:24
  603.2 1.5 gather_fusion.2
  604.7 1.5 gather.25
  606.2 12.8 %all-to-all-done.3 = bf16[128,2,2048]{2,1,0:T(2,128)(2,1)S(1)} async-done(((bf16[128,2,2048]{2,1,0:T(2,128)(2,1)}), bf16[128,2,2048]{2,1,0:T(2,128)(2,1)S(1)}, u32[]{:S(2)}, u32[]{:S(2)}) %all-to-all-start.3) | async-done | bytes 1048608 | tf_op jit(solution)/shard_map/all_to_all | solution.py:18
  619.4 1.5 gather_fusion.3
  620.9 1.5 gather.27
  622.4 4.9 fusion.3
  627.3 43.7 %all-gather.2.cloned.1.call-done = bf16[384,2048]{0,1:T(8,128)(2,1)} async-done(((bf16[384,16]{0,1:T(8,128)(2,1)}), bf16[384,2048]{0,1:T(8,128)(2,1)}) %all-gather.2.cloned.1.call-update) | async-done | bytes 1572880 | tf_op jit(solution)/shard_map/all_gather | solution.py:137
  671.0 0.8 fusion
  671.8 1.6 copy.38
  (83 shorter events, 4.7 us)
Async XLA Ops:
  8.0 3.7 copy-start
  8.0 110.1 %all-reduce.5.cloned.1.call-start = ((), (), s32[]{:S(2)}) async-start(), calls=%async_computation.5 | async-start | bytes 2097152 | tf_op jit(solution)/shard_map/psum | solution.py:23
  61.7 1.7 copy-start.1
  63.3 3.1 copy-start.3
  63.3 1.6 copy-start.7
  64.1 0.7 copy-start.12
  70.8 63.6 %copy-start.8 = (bf16[1,192,2048]{2,1,0:T(8,128)(2,1)S(1)}, bf16[1,192,2048]{2,1,0:T(8,128)(2,1)}, u32[]{:S(2)}) copy-start(bf16[1,192,2048]{2,1,0:T(8,128)(2,1)} %param.11) | copy-start | bytes 2359300
  118.1 239.7 %all-to-all-start.1 = ((bf16[128,2,2048]{2,1,0:T(2,128)(2,1)}), bf16[128,2,2048]{2,1,0:T(2,128)(2,1)}, u32[]{:S(2)}, u32[]{:S(2)}) async-start(bf16[128,2,2048]{2,1,0:T(2,128)(2,1)} %all-reduce.5.cloned.1.call-done), calls=%async_computation.1 | async-start | bytes 2097152 | tf_op jit(solution)/shard_map/all_to_all | solution.py:18
  134.3 206.1 %all-reduce.9.cloned.1.call-start = ((), (), s32[]{:S(2)}) async-start(), calls=%async_computation.9 | async-start | bytes 4718592 | tf_op jit(solution)/shard_map/psum | solution.py:9
  135.3 0.9 copy-start.19
  135.3 1.0 copy-start.20
  135.3 437.0 %reduce-scatter.2.cloned.1.call-start = ((), (), s32[]{:S(2)}) async-start(), calls=%async_computation.7 | async-start | bytes 3170304 | tf_op jit(solution)/shard_map/reduce_scatter | solution.py:136
  136.6 219.2 %copy-start.18 = (s32[1024]{0:T(1024)}, s32[1024]{0:T(1024)S(1)}, u32[]{:S(2)}) copy-start(s32[1024]{0:T(1024)S(1)} %pad_clamp_fusion.1) | copy-start | bytes 12292
  136.6 222.7 %copy-start.17 = (s32[1024]{0:T(1024)}, s32[1024]{0:T(1024)S(1)}, u32[]{:S(2)}) copy-start(s32[1024]{0:T(1024)S(1)} %pad_clamp_fusion) | copy-start | bytes 12292
  340.4 2.0 copy-start.6
  374.4 2.3 copy-start.13
  374.4 2.3 copy-start.15
  376.8 196.9 %all-reduce.7.cloned.1.call-start = ((), (), s32[]{:S(2)}) async-start(), calls=%async_computation.6 | async-start | bytes 2097152 | tf_op jit(solution)/shard_map/psum | solution.py:23
  424.9 1.1 copy-start.9
  426.0 1.6 copy-start.2
  427.6 2.3 copy-start.10
  429.9 158.5 %copy-start.5 = (bf16[384,2048]{1,0:T(8,128)(2,1)S(1)}, bf16[384,2048]{1,0:T(8,128)(2,1)}, u32[]{:S(2)}) copy-start(bf16[384,2048]{1,0:T(8,128)(2,1)} %get-tuple-element.6) | copy-start | bytes 4718596
  429.9 158.5 %copy-start.14 = (bf16[4,192]{1,0:T(4,128)(2,1)S(1)}, bf16[4,192]{1,0:T(4,128)(2,1)}, u32[]{:S(2)}) copy-start(bf16[4,192]{1,0:T(4,128)(2,1)} %copy-done.13) | copy-start | bytes 4612
  429.9 158.5 %copy-start.16 = (bf16[4,192]{1,0:T(4,128)(2,1)S(1)}, bf16[4,192]{1,0:T(4,128)(2,1)}, u32[]{:S(2)}) copy-start(bf16[4,192]{1,0:T(4,128)(2,1)} %copy-done.15) | copy-start | bytes 4612
  429.9 241.1 %all-gather.2.cloned.1.call-start = ((), (), s32[]{:S(2)}) async-start(), calls=%async_computation.8 | async-start | bytes 1585152 | tf_op jit(solution)/shard_map/all_gather | solution.py:137
  573.7 45.3 %all-to-all-start.3 = ((bf16[128,2,2048]{2,1,0:T(2,128)(2,1)}), bf16[128,2,2048]{2,1,0:T(2,128)(2,1)S(1)}, u32[]{:S(2)}, u32[]{:S(2)}) async-start(bf16[128,2,2048]{2,1,0:T(2,128)(2,1)} %all-reduce.7.cloned.1.call-done), calls=%async_computation.3 | async-start | bytes 2097152 | tf_op jit(solution)/shard_map/all_to_all | solution.py:18
  622.4 48.6 %copy-start.4 = (bf16[256,2048]{1,0:T(8,128)(2,1)S(1)}, bf16[256,2048]{1,0:T(8,128)(2,1)}, u32[]{:S(2)}) copy-start(bf16[256,2048]{1,0:T(8,128)(2,1)} %copy-done.3) | copy-start | bytes 3145732
  622.4 48.6 %copy-start.11 = (bf16[256,192]{1,0:T(8,128)(2,1)S(1)}, bf16[256,192]{1,0:T(8,128)(2,1)}, u32[]{:S(2)}) copy-start(bf16[256,192]{1,0:T(8,128)(2,1)} %copy-done.10) | copy-start | bytes 294916
Sparse Core Ops, SparseCore 0:
  69.0 49.0 all-reduce.4
  430.1 46.9 all-reduce.6
Sparse Core Ops, SparseCore 1:
  138.7 201.6 all-reduce.8
  376.9 195.4 reduce-scatter.1
  575.4 95.6 all-gather.1
where the time goes:
time: 682 us; the launch traced here: 681 us
  waiting for transfers between devices  450 us (66%)
  blocking collectives  121 us (18%)
  local copies, waits for them, and re-layouts  33.3 us (5%)
  starting transfers between devices  31.1 us (5%)
  between operations  16.7 us (2%)
  other arithmetic  15.8 us (2%)
  matrix products  13.2 us (2%)
    psum x1, waiting for transfers between devices, from_root(): return lax.psum(kept, axis)  204 us
    reduce_scatter x1, waiting for transfers between devices, local(): lax.psum_scatter(hot_grad, 'expert', scatter_dimension=1, tiled=True)  142 us
    all_to_all x2, blocking collectives, relocate(): lax.all_to_all(buffer, 'expert', split_axis=0, concat_axis=0, tiled=True)  93.6 us
    psum x2, waiting for transfers between devices, quarter_total(): lax.psum(first_term.astype(jnp.bfloat16), 'dp').astype(jnp.float32)  47.4 us
    all_gather x1, waiting for transfers between devices, local(): lax.all_gather(hot_share.astype(jnp.bfloat16), 'expert', axis=1, tiled=True)  43.7 us
    all_to_all x2, starting transfers between devices, relocate(): lax.all_to_all(buffer, 'expert', split_axis=0, concat_axis=0, tiled=True)  30.8 us
    psum x2, blocking collectives, quarter_total(): lax.psum(second_term.astype(jnp.bfloat16), 'dp').astype(jnp.float32)  27.5 us
  transfers between devices with their start and end apart: 7, of which 5 were waited for; matrix products, arithmetic and copies ran while one was open for 4% of the time, Pallas kernels for 0%

commit v1 on v0

v1 whole, which is shorter than its diff:
```python
import jax
import jax.numpy as jnp
from jax import lax
from jax.experimental import pallas as pl
from jax.experimental.pallas import tpu as pltpu
from jax.sharding import PartitionSpec as P

BF = jnp.bfloat16
F32 = jnp.float32
SLOTS = 4
VMEM_BYTES = 48 * 1024 * 1024


def swish_parts(preact):
    sigmoid_part = jax.nn.sigmoid(preact)
    return (preact * sigmoid_part, sigmoid_part * (1.0 + preact * (1.0 - sigmoid_part)))


def over_experts(rows):
    return lax.all_to_all(rows, "expert", split_axis=0, concat_axis=0, tiled=True)


def over_dp(blocks):
    return lax.all_to_all(blocks, "dp", split_axis=0, concat_axis=0, tiled=True)


def gather_columns(block):
    parts = lax.axis_size("dp")
    return over_dp(jnp.broadcast_to(block[None], (parts,) + block.shape))


def dot_t(a, b):
    return lax.dot_general(a, b, (((1,), (1,)), ((), ())), preferred_element_type=F32)


def forward_kernel(rows_ref, win_ref, wout_ref, part_ref, proj_ref):
    parts, _, cols = rows_ref.shape
    quarter = wout_ref.shape[0]
    projected = dot_t(rows_ref[0], win_ref[:, :cols])
    for q in range(1, parts):
        projected += dot_t(rows_ref[q], win_ref[:, q * cols : (q + 1) * cols])
    proj_ref[...] = projected
    swish_value, _ = swish_parts(projected[:, :quarter])
    hidden = (swish_value * projected[:, quarter:]).astype(BF)
    for q in range(parts):
        part_ref[q] = jnp.dot(
            hidden, wout_ref[:, q * cols : (q + 1) * cols], preferred_element_type=F32
        ).astype(BF)


def backward_kernel(rows_ref, cot_ref, proj_ref, win_ref, wout_ref, part_ref, grad_ref):
    parts, _, cols = rows_ref.shape
    quarter = wout_ref.shape[0]
    back_hidden = dot_t(cot_ref[0], wout_ref[:, :cols])
    for q in range(1, parts):
        back_hidden += dot_t(cot_ref[q], wout_ref[:, q * cols : (q + 1) * cols])
    projected = proj_ref[...]
    swish_value, swish_slope = swish_parts(projected[:, :quarter])
    grad_pre = jnp.concatenate(
        [back_hidden * projected[:, quarter:] * swish_slope, back_hidden * swish_value], axis=1
    ).astype(BF)
    for q in range(parts):
        span = slice(q * cols, (q + 1) * cols)
        part_ref[q] = jnp.dot(grad_pre, win_ref[:, span], preferred_element_type=F32).astype(BF)
        grad_ref[:, span] = lax.dot_general(
            grad_pre, rows_ref[q], (((0,), (0,)), ((), ())), preferred_element_type=F32
        ).astype(BF)


def local(tokens, routes, route_weights, loss_weights, gate_up, down_weight):
    experts = lax.axis_size("expert")
    parts = lax.axis_size("dp")
    width = tokens.shape[1]
    cols = width // parts
    local_tokens = tokens.shape[0]
    choices = routes.shape[1]
    quarter = down_weight.shape[1]
    assignments = local_tokens * choices
    slots = experts * SLOTS
    params = pltpu.CompilerParams(vmem_limit_bytes=VMEM_BYTES)
    own_in = gate_up.reshape(2 * quarter, width)
    own_out = down_weight.reshape(quarter, width)

    flat = routes.T.reshape(assignments)
    member = (flat[:, None] == lax.iota(jnp.int32, experts)[None, :]).astype(BF)
    positions = lax.iota(jnp.int32, assignments)
    earlier = (positions[None, :] < positions[:, None]).astype(BF)
    rank_table = jnp.dot(earlier, member, preferred_element_type=F32)
    rank = jnp.sum(rank_table * member.astype(F32), axis=1).astype(jnp.int32)
    slot_index = (flat * SLOTS + rank).reshape(choices, local_tokens)
    slot_ids = lax.iota(jnp.int32, slots)
    place = (slot_ids[None, :, None] == slot_index[:, None, :]).astype(BF)
    pick = (slot_index[:, :, None] == slot_ids[None, None, :]).astype(BF)

    mine = lax.dynamic_slice(
        tokens, (jnp.int32(0), lax.axis_index("dp") * cols), (local_tokens, cols)
    )
    outgoing = jnp.dot(place[0] + place[1], mine, preferred_element_type=F32).astype(BF)
    rows = gather_columns(over_experts(outgoing))

    partial, projected = pl.pallas_call(
        forward_kernel,
        out_shape=(
            jax.ShapeDtypeStruct((parts, slots, cols), BF),
            jax.ShapeDtypeStruct((slots, 2 * quarter), F32),
        ),
        compiler_params=params,
    )(rows, own_in, own_out)
    expert_out = jnp.sum(over_dp(partial).astype(F32), axis=0).astype(BF)
    returned = over_experts(expert_out)

    combined = sum(
        route_weights[:, k : k + 1] * jnp.dot(pick[k], returned, preferred_element_type=F32)
        for k in range(choices)
    )
    cot_send = sum(
        jnp.dot(
            place[k],
            (loss_weights[:, None] * route_weights[:, k : k + 1] * combined).astype(BF),
            preferred_element_type=F32,
        )
        for k in range(choices)
    ).astype(BF)
    cot = gather_columns(over_experts(cot_send))

    input_partial, gradient = pl.pallas_call(
        backward_kernel,
        out_shape=(
            jax.ShapeDtypeStruct((parts, slots, cols), BF),
            jax.ShapeDtypeStruct((2 * quarter, width), BF),
        ),
        compiler_params=params,
    )(rows, cot, projected, own_in, own_out)
    input_each = jnp.sum(over_dp(input_partial).astype(F32), axis=0).astype(BF)
    returned_in = over_experts(input_each)
    input_quarter = jnp.dot(
        pick[0] + pick[1], returned_in, preferred_element_type=F32
    ).astype(BF)
    gathered = gather_columns(input_quarter)
    input_gradient = jnp.swapaxes(gathered, 0, 1).reshape(local_tokens, width)
    return (input_gradient, gradient.reshape(1, 2, quarter, width))


def solution(mesh):
    in_specs = (
        P("expert", None),
        P("expert", None),
        P("expert", None),
        P("expert"),
        P("expert", None, "dp", None),
        P("expert", "dp", None),
    )
    out_specs = (P("expert", None), P("expert", None, "dp", None))
    return jax.shard_map(local, mesh=mesh, in_specs=in_specs, out_specs=out_specs, check_vma=False)
```

time: 682 us -> 274 us (0.40)
  the two profiles are of different devices: /device:TPU:1 before, /device:TPU:8 now
where the time goes in v1:
time: 274 us; the launch traced here: 273 us
  blocking collectives  217 us (79%)
  waiting for transfers between devices  17.8 us (6%)
  Pallas kernels  10.7 us (4%)
  starting transfers between devices  8.47 us (3%)
  local copies, waits for them, and re-layouts  7.46 us (3%)
  other arithmetic  5.81 us (2%)
  matrix products  5.02 us (2%)
    all_to_all x5, blocking collectives, over_dp(): return lax.all_to_all(blocks, 'dp', split_axis=0, concat_axis=0, tiled=True)  125 us
    all_to_all x3, blocking collectives, over_experts(): lax.all_to_all(rows, 'expert', split_axis=0, concat_axis=0, tiled=True)  92.6 us
    all_to_all x1, waiting for transfers between devices, over_experts(): lax.all_to_all(rows, 'expert', split_axis=0, concat_axis=0, tiled=True)  17.8 us
    all_to_all x1, starting transfers between devices, over_experts(): lax.all_to_all(rows, 'expert', split_axis=0, concat_axis=0, tiled=True)  8.47 us
    pallas_call x1, Pallas kernels, local(): pl.pallas_call(backward_kernel, out_shape=(jax.ShapeDtypeStruct((parts, s...  7.18 us
  transfers between devices with their start and end apart: 1, of which 1 were waited for; matrix products, arithmetic and copies ran while one was open for 1% of the time, Pallas kernels for 0%

profile of v1, /device:TPU:8, one launch (start us, length us, event | category | flops | bytes accessed | tf_op | source)
XLA Modules:
  0.0 273.5 jit_solution(4575999953587592366)
XLA Ops:
  0.6 0.0 copy-start
  0.6 1.0 fusion.2
  1.6 0.7 bitcast_add_fusion
  2.3 0.1 iota_compare_fusion
  2.4 0.0 copy-done
  2.5 0.3 convolution_convert_fusion
  2.8 0.1 all_to_all.43
  2.9 37.5 %all_to_all.67 = bf16[128,4,512]{2,1,0:T(4,128)(2,1)S(1)} all-to-all(bf16[128,4,512]{2,1,0:T(4,128)(2,1)S(1)} %all_to_all.43), channel_id=1, replica_groups=mesh['expert'=128,'dp'=4] {'expert'}, dimensions={0} | all-to-all | bytes 1048576 | tf_op jit(solution)/shard_map/all_to_all | solution.py:20
  40.4 0.1 broadcast_in_dim.12
  40.5 0.2 broadcast_in_dim.13
  40.7 0.0 copy-start.1
  40.7 0.0 copy-start.2
  40.7 29.7 %all_to_all.68.rows_ref = bf16[4,512,512]{2,1,0:T(8,128)(2,1)} all-to-all(bf16[4,512,512]{2,1,0:T(8,128)(2,1)S(1)} %broadcast_in_dim.13), channel_id=1, replica_groups=mesh['expert'=128,'dp'=4] {'dp'}, dimensions={0} | all-to-all | bytes 4194304 | tf_op jit(solution)/shard_map/all_to_all | solution.py:24
  70.4 0.0 copy-done.1
  70.4 0.0 copy-done.2
  70.4 3.5 %shard_map.77 = (bf16[4,512,512]{2,1,0:T(8,128)(2,1)S(1)}, f32[512,384]{1,0:T(8,128)S(1)}) custom-call(bf16[4,512,512]{2,1,0:T(8,128)(2,1)} %all_to_all.68.rows_ref, bf16[384,2048]{1,0:T(8,128)(2,1)S(1)} %bitcast.50, bf16[192,2048]{1,0:T(8,128)(2,1)S(1)} %bitcast.52), custom_call_target="tpu_custom_call" | custom-call | tf_op jit(solution)/shard_map/pallas_call | solution.py:101
  73.9 0.0 copy-start.3
  73.9 0.9 copy-done.3
  74.8 27.7 %all_to_all.69 = bf16[4,512,512]{2,1,0:T(8,128)(2,1)} all-to-all(bf16[4,512,512]{2,1,0:T(8,128)(2,1)S(1)} %get-tuple-element.6), channel_id=1, replica_groups=mesh['expert'=128,'dp'=4] {'dp'}, dimensions={0} | all-to-all | bytes 4194304 | tf_op jit(solution)/shard_map/all_to_all | solution.py:24
  102.5 2.2 reduce_sum.34
  104.7 0.9 all_to_all.47
  105.6 8.5 %all-to-all-start.3 = ((bf16[128,4,512]{2,1,0:T(4,128)(2,1)}), bf16[128,4,512]{2,1,0:T(4,128)(2,1)}, u32[]{:S(2)}, u32[]{:S(2)}) async-start(bf16[128,4,512]{2,1,0:T(4,128)(2,1)} %all_to_all.47), calls=%async_computation.3 | async-start | bytes 1048576 | tf_op jit(solution)/shard_map/all_to_all | solution.py:20
  114.1 1.3 fusion.18
  115.3 0.9 fusion.15
  116.2 17.8 %all-to-all-done.3 = bf16[128,4,512]{2,1,0:T(4,128)(2,1)} async-done(((bf16[128,4,512]{2,1,0:T(4,128)(2,1)}), bf16[128,4,512]{2,1,0:T(4,128)(2,1)}, u32[]{:S(2)}, u32[]{:S(2)}) %all-to-all-start.3) | async-done | bytes 524320 | tf_op jit(solution)/shard_map/all_to_all | solution.py:20
  134.0 1.2 all_to_all.49
  135.2 1.0 convolution_multiply_fusion.1
  136.2 1.0 fusion.1
  137.2 0.4 fusion.3
  137.6 1.2 fusion
  138.7 1.2 all_to_all.50
  139.9 26.9 %all_to_all.70 = bf16[128,4,512]{2,1,0:T(4,128)(2,1)} all-to-all(bf16[128,4,512]{2,1,0:T(4,128)(2,1)S(1)} %all_to_all.50), channel_id=1, replica_groups=mesh['expert'=128,'dp'=4] {'expert'}, dimensions={0} | all-to-all | bytes 1048576 | tf_op jit(solution)/shard_map/all_to_all | solution.py:20
  166.7 1.2 broadcast_in_dim.15
  167.9 0.2 broadcast_in_dim.16
  168.1 0.0 copy-start.4
  168.1 29.0 %all_to_all.71.cot_ref = bf16[4,512,512]{2,1,0:T(8,128)(2,1)} all-to-all(bf16[4,512,512]{2,1,0:T(8,128)(2,1)S(1)} %broadcast_in_dim.16), channel_id=1, replica_groups=mesh['expert'=128,'dp'=4] {'dp'}, dimensions={0} | all-to-all | bytes 4194304 | tf_op jit(solution)/shard_map/all_to_all | solution.py:24
  197.1 0.0 copy-done.4
  197.1 7.2 %shard_map.78 = (bf16[4,512,512]{2,1,0:T(8,128)(2,1)S(1)}, bf16[384,2048]{1,0:T(8,128)(2,1)}) custom-call(bf16[4,512,512]{2,1,0:T(8,128)(2,1)} %all_to_all.68.rows_ref, bf16[4,512,512]{2,1,0:T(8,128)(2,1)} %all_to_all.71.cot_ref, f32[512,384]{1,0:T(8,128)S(1)} %copy-done.4, bf16[384,2048]{1,0:T(8,128)(2,1)S(1)} %bitcast.51, bf16[192,2048]{1,0:T(8,128)(2,1)S(1)} %bitcast.53), custom_call_target="tpu_custom_call" | custom-call | tf_op jit(solution)/shard_map/pallas_call | solution.py:126
  204.3 27.2 %all_to_all.72 = bf16[4,512,512]{2,1,0:T(8,128)(2,1)S(1)} all-to-all(bf16[4,512,512]{2,1,0:T(8,128)(2,1)S(1)} %get-tuple-element.8), channel_id=1, replica_groups=mesh['expert'=128,'dp'=4] {'dp'}, dimensions={0} | all-to-all | bytes 4194304 | tf_op jit(solution)/shard_map/all_to_all | solution.py:24
  231.5 0.6 reduce_sum.35
  232.1 0.1 all_to_all.54
  232.2 28.3 %all_to_all.73 = bf16[128,4,512]{2,1,0:T(4,128)(2,1)S(1)} all-to-all(bf16[128,4,512]{2,1,0:T(4,128)(2,1)S(1)} %all_to_all.54), channel_id=1, replica_groups=mesh['expert'=128,'dp'=4] {'expert'}, dimensions={0} | all-to-all | bytes 1048576 | tf_op jit(solution)/shard_map/all_to_all | solution.py:20
  260.5 0.1 all_to_all.56
  260.7 0.0 copy-done.5
  260.7 0.2 convolution_convert_fusion.1
  261.0 11.2 %all_to_all.74 = bf16[4,128,512]{2,1,0:T(8,128)(2,1)S(1)} all-to-all(bf16[4,128,512]{2,1,0:T(8,128)(2,1)S(1)} %broadcast_in_dim.17), channel_id=1, replica_groups=mesh['expert'=128,'dp'=4] {'dp'}, dimensions={0} | all-to-all | bytes 1048576 | tf_op jit(solution)/shard_map/all_to_all | solution.py:24
  272.2 0.3 copy.8
  272.4 1.0 copy.9
  (2 shorter events, 0.0 us)
Async XLA Ops:
  0.6 1.8 copy-start
  40.7 29.7 %copy-start.1 = (bf16[1,2,192,2048]{3,2,1,0:T(8,128)(2,1)S(1)}, bf16[1,2,192,2048]{3,2,1,0:T(8,128)(2,1)}, u32[]{:S(2)}) copy-start(bf16[1,2,192,2048]{3,2,1,0:T(8,128)(2,1)} %param.10) | copy-start | bytes 4718596
  40.7 29.7 %copy-start.2 = (bf16[1,192,2048]{2,1,0:T(8,128)(2,1)S(1)}, bf16[1,192,2048]{2,1,0:T(8,128)(2,1)}, u32[]{:S(2)}) copy-start(bf16[1,192,2048]{2,1,0:T(8,128)(2,1)} %param.11) | copy-start | bytes 2359300
  73.9 0.9 copy-start.3
  105.6 28.4 %all-to-all-start.3 = ((bf16[128,4,512]{2,1,0:T(4,128)(2,1)}), bf16[128,4,512]{2,1,0:T(4,128)(2,1)}, u32[]{:S(2)}, u32[]{:S(2)}) async-start(bf16[128,4,512]{2,1,0:T(4,128)(2,1)} %all_to_all.47), calls=%async_computation.3 | async-start | bytes 1048576 | tf_op jit(solution)/shard_map/all_to_all | solution.py:20
  168.1 29.0 %copy-start.4 = (f32[512,384]{1,0:T(8,128)S(1)}, f32[512,384]{1,0:T(8,128)}, u32[]{:S(2)}) copy-start(f32[512,384]{1,0:T(8,128)} %copy-done.3) | copy-start | bytes 2359300
  232.1 28.6 %copy-start.5 = (bf16[2,128,512]{2,1,0:T(8,128)(2,1)S(1)}, bf16[2,128,512]{2,1,0:T(8,128)(2,1)}, u32[]{:S(2)}) copy-start(bf16[2,128,512]{2,1,0:T(8,128)(2,1)} %get-tuple-element.14) | copy-start | bytes 786436

commit v2 on v1

v2 whole, which is shorter than its diff:
```python
import functools

import jax
import jax.numpy as jnp
from jax import lax
from jax.experimental import pallas as pl
from jax.experimental.pallas import tpu as pltpu
from jax.sharding import PartitionSpec as P

BF = jnp.bfloat16
F32 = jnp.float32
SLOTS = 3
LANES = 128
VMEM_BYTES = 48 * 1024 * 1024
VMEM = pl.BlockSpec(memory_space=pltpu.VMEM)
SMEM = pl.BlockSpec(memory_space=pltpu.SMEM)


def swish_parts(preact):
    sigmoid_part = jax.nn.sigmoid(preact)
    return (preact * sigmoid_part, sigmoid_part * (1.0 + preact * (1.0 - sigmoid_part)))


def over_experts(rows):
    count, cols = rows.shape
    experts = lax.axis_size("expert")
    blocks = rows.reshape(experts, count // experts, cols // LANES, LANES)
    moved = lax.all_to_all(blocks, "expert", split_axis=0, concat_axis=0, tiled=True)
    return moved.reshape(count, cols)


def shift_dp(block, step):
    parts = lax.axis_size("dp")
    return lax.ppermute(block, "dp", [(i, (i + step) % parts) for i in range(parts)])


def gather_dp(block):
    return [block] + [shift_dp(block, k) for k in range(1, lax.axis_size("dp"))]


def scatter_sum_dp(blocks):
    total = blocks[0].astype(F32)
    for moved in [shift_dp(blocks[k], k) for k in range(1, len(blocks))]:
        total = total + moved.astype(F32)
    return total.astype(BF)


def swap_cores(value):
    experts = lax.axis_size("expert")
    return lax.ppermute(value, "expert", [(i, i ^ 1) for i in range(experts)])


def mm(a, b):
    return jnp.dot(a, b, preferred_element_type=F32)


def mm_t(a, b):
    return lax.dot_general(a, b, (((1,), (1,)), ((), ())), preferred_element_type=F32)


def t_mm(a, b):
    return lax.dot_general(a, b, (((0,), (0,)), ((), ())), preferred_element_type=F32)


def span_of(where_ref, step, cols, parts):
    block = lax.rem(where_ref[0] + (step + parts), parts)
    return pl.ds(pl.multiple_of(block * cols, cols), cols)


def extra_rows(shape):
    return lax.rem(lax.broadcasted_iota(jnp.int32, shape, 0), SLOTS) == SLOTS - 1


def contract(blocks, weight_ref, where_ref):
    parts = len(blocks)
    cols = blocks[0].shape[1]
    total = None
    for k in range(parts):
        term = mm_t(blocks[k][...], weight_ref[:, span_of(where_ref, -k, cols, parts)])
        total = term if total is None else total + term
    return total


def expand(value, weight_ref, other_ref, where_ref, outs):
    parts = len(outs)
    cols = outs[0].shape[1]

    @pl.when(where_ref[1] == 0)
    def _():
        for k in range(parts):
            span = span_of(where_ref, k, cols, parts)
            outs[k][...] = mm(value, weight_ref[:, span]).astype(BF)

    @pl.when(where_ref[1] != 0)
    def _():
        extra = extra_rows(value.shape)
        mine = jnp.where(extra, jnp.zeros_like(value), value)
        theirs = jnp.where(extra, value, jnp.zeros_like(value))
        for k in range(parts):
            span = span_of(where_ref, k, cols, parts)
            outs[k][...] = (mm(mine, weight_ref[:, span]) + mm(theirs, other_ref[:, span])).astype(
                BF
            )


def forward_kernel(parts, where_ref, *refs):
    rows = refs[:parts]
    win_ref, wout_ref, other_in_ref, other_out_ref = refs[parts : parts + 4]
    outs = refs[parts + 4 : 2 * parts + 4]
    proj_ref = refs[2 * parts + 4]
    quarter = wout_ref.shape[0]
    proj_ref[...] = contract(rows, win_ref, where_ref)

    @pl.when(where_ref[1] != 0)
    def _():
        other = contract(rows, other_in_ref, where_ref)
        proj_ref[...] = jnp.where(extra_rows(other.shape), other, proj_ref[...])

    projected = proj_ref[...]
    swish_value, _ = swish_parts(projected[:, :quarter])
    hidden = (swish_value * projected[:, quarter:]).astype(BF)
    expand(hidden, wout_ref, other_out_ref, where_ref, outs)


def backward_kernel(parts, where_ref, *refs):
    cots = refs[:parts]
    proj_ref, win_ref, wout_ref, other_in_ref, other_out_ref = refs[parts : parts + 5]
    outs = refs[parts + 5 : 2 * parts + 5]
    grad_pre_ref, back_ref = refs[2 * parts + 5 :]
    quarter = wout_ref.shape[0]
    back_ref[...] = contract(cots, wout_ref, where_ref)

    @pl.when(where_ref[1] != 0)
    def _():
        other = contract(cots, other_out_ref, where_ref)
        back_ref[...] = jnp.where(extra_rows(other.shape), other, back_ref[...])

    back_hidden = back_ref[...]
    projected = proj_ref[...]
    swish_value, swish_slope = swish_parts(projected[:, :quarter])
    grad_pre = jnp.concatenate(
        [back_hidden * projected[:, quarter:] * swish_slope, back_hidden * swish_value], axis=1
    ).astype(BF)
    grad_pre_ref[...] = grad_pre
    expand(grad_pre, win_ref, other_in_ref, where_ref, outs)


def other_gradient_kernel(parts, where_ref, *refs):
    rows = refs[:parts]
    grad_pre_ref, out_ref = refs[parts:]
    cols = rows[0].shape[1]

    @pl.when(where_ref[1] == 0)
    def _():
        out_ref[...] = jnp.zeros_like(out_ref)

    @pl.when(where_ref[1] != 0)
    def _():
        grad_pre = grad_pre_ref[...]
        theirs = jnp.where(extra_rows(grad_pre.shape), grad_pre, jnp.zeros_like(grad_pre))
        for k in range(parts):
            span = span_of(where_ref, -k, cols, parts)
            out_ref[:, span] = t_mm(theirs, rows[k][...]).astype(BF)


def gradient_kernel(parts, where_ref, *refs):
    rows = refs[:parts]
    grad_pre_ref, other_ref, out_ref = refs[parts:]
    cols = rows[0].shape[1]
    grad_pre = grad_pre_ref[...]
    skip = extra_rows(grad_pre.shape) & (where_ref[1] != 0)
    mine = jnp.where(skip, jnp.zeros_like(grad_pre), grad_pre)
    for k in range(parts):
        span = span_of(where_ref, -k, cols, parts)
        out_ref[:, span] = (t_mm(mine, rows[k][...]) + other_ref[:, span].astype(F32)).astype(BF)


def one_hot(slot_ref, k, slots):
    shape = (slot_ref.shape[0], slots)
    return (lax.broadcasted_iota(jnp.int32, shape, 1) == slot_ref[:, k : k + 1]).astype(BF)


def send_kernel(slot_ref, tokens_ref, out_ref):
    slots = out_ref.shape[0]
    both = sum(one_hot(slot_ref, k, slots) for k in range(slot_ref.shape[1]))
    out_ref[...] = t_mm(both, tokens_ref[...]).astype(BF)


def combine_kernel(slot_ref, route_weight_ref, loss_weight_ref, returned_ref, out_ref):
    slots = out_ref.shape[0]
    choices = slot_ref.shape[1]
    picks = [one_hot(slot_ref, k, slots) for k in range(choices)]
    weights = [route_weight_ref[:, k : k + 1] for k in range(choices)]
    returned = returned_ref[...]
    combined = sum(weights[k] * mm(picks[k], returned) for k in range(choices))
    loss = loss_weight_ref[...]
    out_ref[...] = sum(
        t_mm(picks[k], (loss * weights[k] * combined).astype(BF)) for k in range(choices)
    ).astype(BF)


def collect_kernel(slot_ref, returned_ref, out_ref):
    slots = returned_ref.shape[0]
    both = sum(one_hot(slot_ref, k, slots) for k in range(slot_ref.shape[1]))
    out_ref[...] = mm(both, returned_ref[...]).astype(BF)


def join_kernel(parts, where_ref, *refs):
    out_ref = refs[parts]
    cols = refs[0].shape[1]
    for k in range(parts):
        out_ref[:, span_of(where_ref, -k, cols, parts)] = refs[k][...]


def call(kernel, outs, args, scalars=1, scratch=()):
    return pl.pallas_call(
        kernel,
        out_shape=outs,
        in_specs=[SMEM] * scalars + [VMEM] * (len(args) - scalars),
        out_specs=jax.tree.map(lambda _: VMEM, outs),
        scratch_shapes=list(scratch),
        compiler_params=pltpu.CompilerParams(vmem_limit_bytes=VMEM_BYTES),
    )(*args)


def local(tokens, routes, route_weights, loss_weights, gate_up, down_weight):
    experts = lax.axis_size("expert")
    parts = lax.axis_size("dp")
    part = lax.axis_index("dp")
    index = lax.axis_index("expert")
    local_tokens, width = tokens.shape
    cols = width // parts
    choices = routes.shape[1]
    quarter = down_weight.shape[1]
    assignments = local_tokens * choices
    slots = experts * SLOTS
    own_in = gate_up.reshape(2 * quarter, width)
    own_out = down_weight.reshape(quarter, width)

    flat = routes.reshape(assignments)
    member = (flat[:, None] == lax.iota(jnp.int32, experts)[None, :]).astype(BF)
    busiest = jnp.argmax(jnp.sum(member.astype(F32), axis=0)).astype(jnp.int32)
    positions = lax.iota(jnp.int32, assignments)
    earlier = (positions[None, :] < positions[:, None]).astype(BF)
    rank = jnp.sum(mm(earlier, member) * member.astype(F32), axis=1).astype(jnp.int32)
    slot = jnp.where(
        rank == SLOTS, (flat ^ 1) * SLOTS + SLOTS - 1, flat * SLOTS + rank
    ).reshape(local_tokens, choices)
    where = jnp.stack([part, ((index ^ 1) == busiest).astype(jnp.int32)]).astype(jnp.int32)

    block = jax.ShapeDtypeStruct((slots, cols), BF)
    mine = lax.dynamic_slice(tokens, (jnp.int32(0), part * cols), (local_tokens, cols))
    outgoing = call(send_kernel, block, (slot, mine), scalars=0)
    rows = gather_dp(over_experts(outgoing))
    other_in, other_out = swap_cores(own_in), swap_cores(own_out)

    *partial, projected = call(
        functools.partial(forward_kernel, parts),
        [block] * parts + [jax.ShapeDtypeStruct((slots, 2 * quarter), F32)],
        (where, *rows, own_in, own_out, other_in, other_out),
    )
    returned = over_experts(scatter_sum_dp(partial))

    cot_send = call(
        combine_kernel,
        block,
        (slot, route_weights, loss_weights.reshape(local_tokens, 1), returned),
        scalars=0,
    )
    cots = gather_dp(over_experts(cot_send))

    *input_partial, grad_pre = call(
        functools.partial(backward_kernel, parts),
        [block] * parts + [jax.ShapeDtypeStruct((slots, 2 * quarter), BF)],
        (where, *cots, projected, own_in, own_out, other_in, other_out),
        scratch=[pltpu.VMEM((slots, quarter), F32)],
    )
    returned_in = over_experts(scatter_sum_dp(input_partial))

    whole_gradient = jax.ShapeDtypeStruct((2 * quarter, width), BF)
    lent = call(
        functools.partial(other_gradient_kernel, parts), whole_gradient, (where, *rows, grad_pre)
    )
    gradient = call(
        functools.partial(gradient_kernel, parts),
        whole_gradient,
        (where, *rows, grad_pre, swap_cores(lent)),
    )

    collected = call(
        collect_kernel,
        jax.ShapeDtypeStruct((local_tokens, cols), BF),
        (slot, returned_in),
        scalars=0,
    )
    input_gradient = call(
        functools.partial(join_kernel, parts),
        jax.ShapeDtypeStruct((local_tokens, width), BF),
        (where, *gather_dp(collected)),
    )
    return (input_gradient, gradient.reshape(1, 2, quarter, width))


def solution(mesh):
    in_specs = (
        P("expert", None),
        P("expert", None),
        P("expert", None),
        P("expert"),
        P("expert", None, "dp", None),
        P("expert", "dp", None),
    )
    out_specs = (P("expert", None), P("expert", None, "dp", None))
    return jax.shard_map(local, mesh=mesh, in_specs=in_specs, out_specs=out_specs, check_vma=False)
```

time: 274 us -> 249 us (0.909)
  blocking collectives: 217 us -> 48.2 us
  waiting for transfers between devices: 17.8 us -> 98.4 us
  starting transfers between devices: 8.47 us -> 76.9 us
  Pallas kernels: 10.7 us -> 15.9 us
  matrix products: 5.02 us -> 0.24 us
  other arithmetic: 5.81 us -> 1.95 us
    all_to_all x8 -> x2, blocking collectives: 217 us -> 48.2 us  [over_experts(): lax.all_to_all(blocks, 'expert', split_axis=0, concat_axis=0, tiled=True)]
    ppermute x0 -> x18, waiting for transfers between devices: none -> 65.7 us  [the longest x15 65.7 us: shift_dp(): lax.ppermute(block, 'dp', [(i, (i + step) % parts) for i in range(parts)])]
    ppermute x0 -> x18, starting transfers between devices: none -> 52.9 us  [the longest x15 46.9 us: shift_dp(): lax.ppermute(block, 'dp', [(i, (i + step) % parts) for i in range(parts)])]
    all_to_all x1 -> x2, starting transfers between devices: 8.47 us -> 23.9 us  [over_experts(): lax.all_to_all(blocks, 'expert', split_axis=0, concat_axis=0, tiled=True)]
    all_to_all x1 -> x2, waiting for transfers between devices: 17.8 us -> 32.7 us  [over_experts(): lax.all_to_all(blocks, 'expert', split_axis=0, concat_axis=0, tiled=True)]
    pallas_call x2 -> x8, Pallas kernels: 10.7 us -> 15.9 us  [call(): pl.pallas_call(kernel, out_shape=outs, in_specs=[SMEM] * scalars + [VMEM]...]
    dot_general x7 -> x1, matrix products: 5.02 us -> 0.24 us  [mm(): return jnp.dot(a, b, preferred_element_type=F32)]
    all_to_all x7 -> x0, local copies, waits for them, and re-layouts: 3.89 us -> none  [the longest x6 3.62 us: over_experts(): lax.all_to_all(rows, 'expert', split_axis=0, concat_axis=0, tiled=True)]
  transfers between devices with their start and end apart: 1 -> 20, of which waited for: 1 -> 13; matrix products, arithmetic and copies ran while one was open for 1% -> 2% of each run, Pallas kernels for 0% -> 2%
where the time goes in v2:
time: 249 us; the launch traced here: 248 us
  waiting for transfers between devices  98.4 us (40%)
  starting transfers between devices  76.9 us (31%)
  blocking collectives  48.2 us (19%)
  Pallas kernels  15.9 us (6%)
  local copies, waits for them, and re-layouts  5.1 us (2%)
    ppermute x15, waiting for transfers between devices, shift_dp(): lax.ppermute(block, 'dp', [(i, (i + step) % parts) for i in range(parts)])  65.7 us
    all_to_all x2, blocking collectives, over_experts(): lax.all_to_all(blocks, 'expert', split_axis=0, concat_axis=0, tiled=True)  48.2 us
    ppermute x15, starting transfers between devices, shift_dp(): lax.ppermute(block, 'dp', [(i, (i + step) % parts) for i in range(parts)])  46.9 us
    all_to_all x2, waiting for transfers between devices, over_experts(): lax.all_to_all(blocks, 'expert', split_axis=0, concat_axis=0, tiled=True)  32.7 us
    all_to_all x2, starting transfers between devices, over_experts(): lax.all_to_all(blocks, 'expert', split_axis=0, concat_axis=0, tiled=True)  23.9 us
    pallas_call x8, Pallas kernels, call(): pl.pallas_call(kernel, out_shape=outs, in_specs=[SMEM] * scalars + [VMEM]...  15.9 us
    ppermute x3, starting transfers between devices, swap_cores(): return lax.ppermute(value, 'expert', [(i, i ^ 1) for i in range(experts)])  6.02 us
  transfers between devices with their start and end apart: 20, of which 13 were waited for; matrix products, arithmetic and copies ran while one was open for 2% of the time, Pallas kernels for 2%

profile of v2, /device:TPU:8, one launch (start us, length us, event | category | flops | bytes accessed | tf_op | source)
XLA Modules:
  0.0 248.3 jit_solution(16111776621613461817)
XLA Ops:
  0.6 2.1 collective-permute-start.3
  2.7 0.7 broadcast_multiply_fusion
  3.4 0.8 copy.13
  5.3 0.8 reshape.46
  6.1 17.5 %all-to-all-start = ((bf16[128,3,4,128]{3,2,1,0:T(4,128)(2,1)}), bf16[128,3,4,128]{3,2,1,0:T(4,128)(2,1)S(1)}, u32[]{:S(2)}, u32[]{:S(2)}) async-start(bf16[128,3,4,128]{3,2,1,0:T(4,128)(2,1)} %reshape.46), calls=%async_computation | async-start | bytes 786432 | tf_op jit(solution)/shard_map/all_to_all | solution.py:28
  23.6 2.1 collective-permute-start.4
  25.7 15.5 %all-to-all-done = bf16[128,3,4,128]{3,2,1,0:T(4,128)(2,1)S(1)} async-done(((bf16[128,3,4,128]{3,2,1,0:T(4,128)(2,1)}), bf16[128,3,4,128]{3,2,1,0:T(4,128)(2,1)S(1)}, u32[]{:S(2)}, u32[]{:S(2)}) %all-to-all-start) | async-done | bytes 393248 | tf_op jit(solution)/shard_map/all_to_all | solution.py:28
  41.2 4.7 %collective-permute-start.2 = (bf16[384,512]{1,0:T(8,128)(2,1)S(1)}, bf16[384,512]{1,0:T(8,128)(2,1)S(1)}, u32[]{:S(2)}, u32[]{:S(2)}) collective-permute-start(bf16[384,512]{1,0:T(8,128)(2,1)S(1)} %bitcast.26), channel_id=1, source_target_pairs={{0,3},{1,0},{2,1},{3,2},{4,7},{5,4},{6,5},{7,6},{8,11},{9,8},{10,9... | collective-permute-start | bytes 1179656 | tf_op jit(solution)/shard_map/ppermute | solution.py:34
  45.9 2.7 %collective-permute-start.1 = (bf16[384,512]{1,0:T(8,128)(2,1)S(1)}, bf16[384,512]{1,0:T(8,128)(2,1)S(1)}, u32[]{:S(2)}, u32[]{:S(2)}) collective-permute-start(bf16[384,512]{1,0:T(8,128)(2,1)S(1)} %bitcast.27), channel_id=1, source_target_pairs={{0,2},{1,3},{2,0},{3,1},{4,6},{5,7},{6,4},{7,5},{8,10},{9,11},{10,... | collective-permute-start | bytes 1179656 | tf_op jit(solution)/shard_map/ppermute | solution.py:34
  48.6 2.8 %collective-permute-start = (bf16[384,512]{1,0:T(8,128)(2,1)S(1)}, bf16[384,512]{1,0:T(8,128)(2,1)S(1)}, u32[]{:S(2)}, u32[]{:S(2)}) collective-permute-start(bf16[384,512]{1,0:T(8,128)(2,1)S(1)} %bitcast.28), channel_id=1, source_target_pairs={{0,1},{1,2},{2,3},{3,0},{4,5},{5,6},{6,7},{7,4},{8,9},{9,10},{10,1... | collective-permute-start | bytes 1179656 | tf_op jit(solution)/shard_map/ppermute | solution.py:34
  51.5 0.7 iota_reduce_fusion
  52.9 9.0 %collective-permute-done.2.refs_3_ = bf16[384,512]{1,0:T(8,128)(2,1)S(1)} collective-permute-done((bf16[384,512]{1,0:T(8,128)(2,1)S(1)}, bf16[384,512]{1,0:T(8,128)(2,1)S(1)}, u32[]{:S(2)}, u32[]{:S(2)}) %collective-permute-start.2) | collective-permute-done | bytes 393248 | tf_op jit(solution)/shard_map/ppermute | solution.py:34
  62.0 5.6 %collective-permute-done.refs_1_ = bf16[384,512]{1,0:T(8,128)(2,1)S(1)} collective-permute-done((bf16[384,512]{1,0:T(8,128)(2,1)S(1)}, bf16[384,512]{1,0:T(8,128)(2,1)S(1)}, u32[]{:S(2)}, u32[]{:S(2)}) %collective-permute-start) | collective-permute-done | bytes 393248 | tf_op jit(solution)/shard_map/ppermute | solution.py:34
  67.5 3.8 %shard_map.78 = (bf16[384,512]{1,0:T(8,128)(2,1)S(1)}, bf16[384,512]{1,0:T(8,128)(2,1)S(1)}, bf16[384,512]{1,0:T(8,128)(2,1)S(1)}, bf16[384,512]{1,0:T(8,128)(2,1)S(1)}, f32[384,384]{1,0:T(8,128)S(1)}) custom-call(s32[2]{0:T(128)S(1)} %pad_add_fusion.where_ref, bf16[384,512]{1,0:T(8,128)(2,1)S(1)} %bitcast.29, ...), custom_call_target="tpu_custom_call" | custom-call | tf_op jit(solution)/shard_map/pallas_call | solution.py:216
  71.4 0.8 copy-done.2
  72.2 1.9 collective-permute-start.5
  74.1 4.0 %collective-permute-start.6 = (bf16[384,512]{1,0:T(8,128)(2,1)S(1)}, bf16[384,512]{1,0:T(8,128)(2,1)S(1)}, u32[]{:S(2)}, u32[]{:S(2)}) collective-permute-start(bf16[384,512]{1,0:T(8,128)(2,1)S(1)} %get-tuple-element.16), channel_id=1, source_target_pairs={{0,2},{1,3},{2,0},{3,1},{4,6},{5,7},{6,4},{7,5},{8,10},{9,11},{10,... | collective-permute-start | bytes 1179656 | tf_op jit(solution)/shard_map/ppermute | solution.py:34
  78.1 3.3 %collective-permute-start.7 = (bf16[384,512]{1,0:T(8,128)(2,1)S(1)}, bf16[384,512]{1,0:T(8,128)(2,1)S(1)}, u32[]{:S(2)}, u32[]{:S(2)}) collective-permute-start(bf16[384,512]{1,0:T(8,128)(2,1)S(1)} %get-tuple-element.17), channel_id=1, source_target_pairs={{0,3},{1,0},{2,1},{3,2},{4,7},{5,4},{6,5},{7,6},{8,11},{9,8},{10,9... | collective-permute-start | bytes 1179656 | tf_op jit(solution)/shard_map/ppermute | solution.py:34
  81.4 13.4 %collective-permute-done.5 = bf16[384,512]{1,0:T(8,128)(2,1)S(1)} collective-permute-done((bf16[384,512]{1,0:T(8,128)(2,1)S(1)}, bf16[384,512]{1,0:T(8,128)(2,1)S(1)}, u32[]{:S(2)}, u32[]{:S(2)}) %collective-permute-start.5) | collective-permute-done | bytes 393248 | tf_op jit(solution)/shard_map/ppermute | solution.py:34
  94.8 2.5 %collective-permute-done.7 = bf16[384,512]{1,0:T(8,128)(2,1)S(1)} collective-permute-done((bf16[384,512]{1,0:T(8,128)(2,1)S(1)}, bf16[384,512]{1,0:T(8,128)(2,1)S(1)}, u32[]{:S(2)}, u32[]{:S(2)}) %collective-permute-start.7) | collective-permute-done | bytes 393248 | tf_op jit(solution)/shard_map/ppermute | solution.py:34
  97.5 0.8 reshape.50
  98.3 6.5 %all-to-all-start.1 = ((bf16[128,3,4,128]{3,2,1,0:T(4,128)(2,1)}), bf16[128,3,4,128]{3,2,1,0:T(4,128)(2,1)S(1)}, u32[]{:S(2)}, u32[]{:S(2)}) async-start(bf16[128,3,4,128]{3,2,1,0:T(4,128)(2,1)} %reshape.50), calls=%async_computation.1 | async-start | bytes 786432 | tf_op jit(solution)/shard_map/all_to_all | solution.py:28
  105.0 17.3 %all-to-all-done.1 = bf16[128,3,4,128]{3,2,1,0:T(4,128)(2,1)S(1)} async-done(((bf16[128,3,4,128]{3,2,1,0:T(4,128)(2,1)}), bf16[128,3,4,128]{3,2,1,0:T(4,128)(2,1)S(1)}, u32[]{:S(2)}, u32[]{:S(2)}) %all-to-all-start.1) | async-done | bytes 393248 | tf_op jit(solution)/shard_map/all_to_all | solution.py:28
  122.4 0.7 shard_map.79
  123.1 0.8 reshape.52
  123.9 24.4 %all_to_all.20 = bf16[128,3,4,128]{3,2,1,0:T(4,128)(2,1)S(1)} all-to-all(bf16[128,3,4,128]{3,2,1,0:T(4,128)(2,1)} %reshape.52), channel_id=1, replica_groups=mesh['expert'=128,'dp'=4] {'expert'}, dimensions={0} | all-to-all | bytes 786432 | tf_op jit(solution)/shard_map/all_to_all | solution.py:28
  148.4 4.5 %collective-permute-start.10 = (bf16[384,512]{1,0:T(8,128)(2,1)S(1)}, bf16[384,512]{1,0:T(8,128)(2,1)S(1)}, u32[]{:S(2)}, u32[]{:S(2)}) collective-permute-start(bf16[384,512]{1,0:T(8,128)(2,1)S(1)} %bitcast.37), channel_id=1, source_target_pairs={{0,3},{1,0},{2,1},{3,2},{4,7},{5,4},{6,5},{7,6},{8,11},{9,8},{10,9... | collective-permute-start | bytes 1179656 | tf_op jit(solution)/shard_map/ppermute | solution.py:34
  153.0 1.9 collective-permute-start.9
  154.9 2.9 %collective-permute-start.8 = (bf16[384,512]{1,0:T(8,128)(2,1)S(1)}, bf16[384,512]{1,0:T(8,128)(2,1)S(1)}, u32[]{:S(2)}, u32[]{:S(2)}) collective-permute-start(bf16[384,512]{1,0:T(8,128)(2,1)S(1)} %bitcast.39), channel_id=1, source_target_pairs={{0,1},{1,2},{2,3},{3,0},{4,5},{5,6},{6,7},{7,4},{8,9},{9,10},{10,1... | collective-permute-start | bytes 1179656 | tf_op jit(solution)/shard_map/ppermute | solution.py:34
  157.8 11.2 %collective-permute-done.10.refs_3_ = bf16[384,512]{1,0:T(8,128)(2,1)S(1)} collective-permute-done((bf16[384,512]{1,0:T(8,128)(2,1)S(1)}, bf16[384,512]{1,0:T(8,128)(2,1)S(1)}, u32[]{:S(2)}, u32[]{:S(2)}) %collective-permute-start.10) | collective-permute-done | bytes 393248 | tf_op jit(solution)/shard_map/ppermute | solution.py:34
  169.0 5.6 %collective-permute-done.8.refs_1_ = bf16[384,512]{1,0:T(8,128)(2,1)S(1)} collective-permute-done((bf16[384,512]{1,0:T(8,128)(2,1)S(1)}, bf16[384,512]{1,0:T(8,128)(2,1)S(1)}, u32[]{:S(2)}, u32[]{:S(2)}) %collective-permute-start.8) | collective-permute-done | bytes 393248 | tf_op jit(solution)/shard_map/ppermute | solution.py:34
  174.6 3.9 %shard_map.80 = (bf16[384,512]{1,0:T(8,128)(2,1)S(1)}, bf16[384,512]{1,0:T(8,128)(2,1)S(1)}, bf16[384,512]{1,0:T(8,128)(2,1)S(1)}, bf16[384,512]{1,0:T(8,128)(2,1)S(1)}, bf16[384,384]{1,0:T(8,128)(2,1)S(1)}) custom-call(s32[2]{0:T(128)S(1)} %pad_add_fusion.where_ref, bf16[384,512]{1,0:T(8,128)(2,1)S(1)} %bitcast.40, ...), custom_call_target="tpu_custom_call" | custom-call | tf_op jit(solution)/shard_map/pallas_call | solution.py:216
  178.5 1.9 collective-permute-start.11
  180.5 4.0 %collective-permute-start.12 = (bf16[384,512]{1,0:T(8,128)(2,1)S(1)}, bf16[384,512]{1,0:T(8,128)(2,1)S(1)}, u32[]{:S(2)}, u32[]{:S(2)}) collective-permute-start(bf16[384,512]{1,0:T(8,128)(2,1)S(1)} %get-tuple-element.21), channel_id=1, source_target_pairs={{0,2},{1,3},{2,0},{3,1},{4,6},{5,7},{6,4},{7,5},{8,10},{9,11},{10,... | collective-permute-start | bytes 1179656 | tf_op jit(solution)/shard_map/ppermute | solution.py:34
  184.4 3.1 %collective-permute-start.13 = (bf16[384,512]{1,0:T(8,128)(2,1)S(1)}, bf16[384,512]{1,0:T(8,128)(2,1)S(1)}, u32[]{:S(2)}, u32[]{:S(2)}) collective-permute-start(bf16[384,512]{1,0:T(8,128)(2,1)S(1)} %get-tuple-element.22), channel_id=1, source_target_pairs={{0,3},{1,0},{2,1},{3,2},{4,7},{5,4},{6,5},{7,6},{8,11},{9,8},{10,9... | collective-permute-start | bytes 1179656 | tf_op jit(solution)/shard_map/ppermute | solution.py:34
  187.5 1.8 shard_map.83
  189.3 1.9 collective-permute-start.17
  191.2 9.9 %collective-permute-done.11 = bf16[384,512]{1,0:T(8,128)(2,1)S(1)} collective-permute-done((bf16[384,512]{1,0:T(8,128)(2,1)S(1)}, bf16[384,512]{1,0:T(8,128)(2,1)S(1)}, u32[]{:S(2)}, u32[]{:S(2)}) %collective-permute-start.11) | collective-permute-done | bytes 393248 | tf_op jit(solution)/shard_map/ppermute | solution.py:34
  201.1 2.5 %collective-permute-done.13 = bf16[384,512]{1,0:T(8,128)(2,1)S(1)} collective-permute-done((bf16[384,512]{1,0:T(8,128)(2,1)S(1)}, bf16[384,512]{1,0:T(8,128)(2,1)S(1)}, u32[]{:S(2)}, u32[]{:S(2)}) %collective-permute-start.13) | collective-permute-done | bytes 393248 | tf_op jit(solution)/shard_map/ppermute | solution.py:34
  203.9 23.8 %all_to_all.21 = bf16[128,3,4,128]{3,2,1,0:T(4,128)(2,1)S(1)} all-to-all(bf16[128,3,4,128]{3,2,1,0:T(4,128)(2,1)S(1)} %reshape.54), channel_id=1, replica_groups=mesh['expert'=128,'dp'=4] {'expert'}, dimensions={0} | all-to-all | bytes 786432 | tf_op jit(solution)/shard_map/all_to_all | solution.py:28
  228.1 4.5 %collective-permute-start.16 = (bf16[128,512]{1,0:T(8,128)(2,1)S(1)}, bf16[128,512]{1,0:T(8,128)(2,1)S(1)}, u32[]{:S(2)}, u32[]{:S(2)}) collective-permute-start(bf16[128,512]{1,0:T(8,128)(2,1)S(1)} %shard_map.81.refs_0_), channel_id=1, source_target_pairs={{0,3},{1,0},{2,1},{3,2},{4,7},{5,4},{6,5},{7,6},{8,11},{9,8},{10,9... | collective-permute-start | bytes 393224 | tf_op jit(solution)/shard_map/ppermute | solution.py:34
  232.6 1.9 collective-permute-start.15
  234.6 2.8 %collective-permute-start.14 = (bf16[128,512]{1,0:T(8,128)(2,1)S(1)}, bf16[128,512]{1,0:T(8,128)(2,1)S(1)}, u32[]{:S(2)}, u32[]{:S(2)}) collective-permute-start(bf16[128,512]{1,0:T(8,128)(2,1)S(1)} %shard_map.81.refs_0_), channel_id=1, source_target_pairs={{0,1},{1,2},{2,3},{3,0},{4,5},{5,6},{6,7},{7,4},{8,9},{9,10},{10,1... | collective-permute-start | bytes 393224 | tf_op jit(solution)/shard_map/ppermute | solution.py:34
  237.3 0.6 collective-permute-done.16.refs_3_
  237.9 4.3 %collective-permute-done.15.refs_2_ = bf16[128,512]{1,0:T(8,128)(2,1)S(1)} collective-permute-done((bf16[128,512]{1,0:T(8,128)(2,1)S(1)}, bf16[128,512]{1,0:T(8,128)(2,1)S(1)}, u32[]{:S(2)}, u32[]{:S(2)}) %collective-permute-start.15) | collective-permute-done | bytes 131104 | tf_op jit(solution)/shard_map/ppermute | solution.py:34
  242.3 1.0 collective-permute-done.14.refs_1_
  243.3 1.4 shard_map.82
  244.7 3.6 %shard_map.84 = bf16[384,2048]{1,0:T(8,128)(2,1)} custom-call(s32[2]{0:T(128)S(1)} %pad_add_fusion.where_ref, bf16[384,512]{1,0:T(8,128)(2,1)S(1)} %bitcast.31, bf16[384,512]{1,0:T(8,128)(2,1)S(1)} %collective-permute-done.refs_1_, bf16[384,512]{1,0:T(8,128)(2,1)S(1)} %collective-permute-done.1.refs_2_, bf16[384,512]{1,0:T(8,128)(2,1)S(1)} %collective-permute-done.2.refs_3_, ...), custom_call_target="tpu_custom_call" | custom-call | tf_op jit(solution)/shard_map/pallas_call | solution.py:216
  (38 shorter events, 2.5 us)
Async XLA Ops:
  0.6 4.2 %copy-start = (bf16[128,2048]{1,0:T(8,128)(2,1)S(1)}, bf16[128,2048]{1,0:T(8,128)(2,1)}, u32[]{:S(2)}) copy-start(bf16[128,2048]{1,0:T(8,128)(2,1)} %param.6) | copy-start | bytes 1572868
  0.6 66.9 %collective-permute-start.3 = (bf16[384,2048]{1,0:T(8,128)(2,1)}, bf16[384,2048]{1,0:T(8,128)(2,1)}, u32[]{:S(2)}, u32[]{:S(2)}) collective-permute-start(bf16[384,2048]{1,0:T(8,128)(2,1)} %bitcast.41), channel_id=1, source_target_pairs={{0,4},{4,0},{8,12},{12,8},{16,20},{20,16},{24,28},{28,24},{32,36},... | collective-permute-start | bytes 4718600 | tf_op jit(solution)/shard_map/ppermute | solution.py:50
  4.2 19.4 %copy-start.1 = (bf16[1,192,2048]{2,1,0:T(8,128)(2,1)S(1)}, bf16[1,192,2048]{2,1,0:T(8,128)(2,1)}, u32[]{:S(2)}) copy-start(bf16[1,192,2048]{2,1,0:T(8,128)(2,1)} %param.11) | copy-start | bytes 2359300
  6.1 35.0 %all-to-all-start = ((bf16[128,3,4,128]{3,2,1,0:T(4,128)(2,1)}), bf16[128,3,4,128]{3,2,1,0:T(4,128)(2,1)S(1)}, u32[]{:S(2)}, u32[]{:S(2)}) async-start(bf16[128,3,4,128]{3,2,1,0:T(4,128)(2,1)} %reshape.46), calls=%async_computation | async-start | bytes 786432 | tf_op jit(solution)/shard_map/all_to_all | solution.py:28
  23.6 29.3 %collective-permute-start.4 = (bf16[192,2048]{1,0:T(8,128)(2,1)S(1)}, bf16[192,2048]{1,0:T(8,128)(2,1)}, u32[]{:S(2)}, u32[]{:S(2)}) collective-permute-start(bf16[192,2048]{1,0:T(8,128)(2,1)S(1)} %bitcast.32), channel_id=1, source_target_pairs={{0,4},{4,0},{8,12},{12,8},{16,20},{20,16},{24,28},{28,24},{32,36},... | collective-permute-start | bytes 2359304 | tf_op jit(solution)/shard_map/ppermute | solution.py:50
  41.2 20.7 %collective-permute-start.2 = (bf16[384,512]{1,0:T(8,128)(2,1)S(1)}, bf16[384,512]{1,0:T(8,128)(2,1)S(1)}, u32[]{:S(2)}, u32[]{:S(2)}) collective-permute-start(bf16[384,512]{1,0:T(8,128)(2,1)S(1)} %bitcast.26), channel_id=1, source_target_pairs={{0,3},{1,0},{2,1},{3,2},{4,7},{5,4},{6,5},{7,6},{8,11},{9,8},{10,9... | collective-permute-start | bytes 1179656 | tf_op jit(solution)/shard_map/ppermute | solution.py:34
  45.9 16.1 %collective-permute-start.1 = (bf16[384,512]{1,0:T(8,128)(2,1)S(1)}, bf16[384,512]{1,0:T(8,128)(2,1)S(1)}, u32[]{:S(2)}, u32[]{:S(2)}) collective-permute-start(bf16[384,512]{1,0:T(8,128)(2,1)S(1)} %bitcast.27), channel_id=1, source_target_pairs={{0,2},{1,3},{2,0},{3,1},{4,6},{5,7},{6,4},{7,5},{8,10},{9,11},{10,... | collective-permute-start | bytes 1179656 | tf_op jit(solution)/shard_map/ppermute | solution.py:34
  48.6 18.9 %collective-permute-start = (bf16[384,512]{1,0:T(8,128)(2,1)S(1)}, bf16[384,512]{1,0:T(8,128)(2,1)S(1)}, u32[]{:S(2)}, u32[]{:S(2)}) collective-permute-start(bf16[384,512]{1,0:T(8,128)(2,1)S(1)} %bitcast.28), channel_id=1, source_target_pairs={{0,1},{1,2},{2,3},{3,0},{4,5},{5,6},{6,7},{7,4},{8,9},{9,10},{10,1... | collective-permute-start | bytes 1179656 | tf_op jit(solution)/shard_map/ppermute | solution.py:34
  71.4 0.8 copy-start.2
  72.2 22.6 %collective-permute-start.5 = (bf16[384,512]{1,0:T(8,128)(2,1)S(1)}, bf16[384,512]{1,0:T(8,128)(2,1)S(1)}, u32[]{:S(2)}, u32[]{:S(2)}) collective-permute-start(bf16[384,512]{1,0:T(8,128)(2,1)S(1)} %get-tuple-element.15), channel_id=1, source_target_pairs={{0,1},{1,2},{2,3},{3,0},{4,5},{5,6},{6,7},{7,4},{8,9},{9,10},{10,1... | collective-permute-start | bytes 1179656 | tf_op jit(solution)/shard_map/ppermute | solution.py:34
  74.1 20.6 %collective-permute-start.6 = (bf16[384,512]{1,0:T(8,128)(2,1)S(1)}, bf16[384,512]{1,0:T(8,128)(2,1)S(1)}, u32[]{:S(2)}, u32[]{:S(2)}) collective-permute-start(bf16[384,512]{1,0:T(8,128)(2,1)S(1)} %get-tuple-element.16), channel_id=1, source_target_pairs={{0,2},{1,3},{2,0},{3,1},{4,6},{5,7},{6,4},{7,5},{8,10},{9,11},{10,... | collective-permute-start | bytes 1179656 | tf_op jit(solution)/shard_map/ppermute | solution.py:34
  78.1 19.2 %collective-permute-start.7 = (bf16[384,512]{1,0:T(8,128)(2,1)S(1)}, bf16[384,512]{1,0:T(8,128)(2,1)S(1)}, u32[]{:S(2)}, u32[]{:S(2)}) collective-permute-start(bf16[384,512]{1,0:T(8,128)(2,1)S(1)} %get-tuple-element.17), channel_id=1, source_target_pairs={{0,3},{1,0},{2,1},{3,2},{4,7},{5,4},{6,5},{7,6},{8,11},{9,8},{10,9... | collective-permute-start | bytes 1179656 | tf_op jit(solution)/shard_map/ppermute | solution.py:34
  97.3 7.5 %copy-start.4 = (f32[128,2]{0,1:T(2,128)S(1)}, f32[128,2]{0,1:T(2,128)}, u32[]{:S(2)}) copy-start(f32[128,2]{0,1:T(2,128)} %param.8) | copy-start | bytes 3076
  97.3 7.6 %copy-start.5 = (f32[128]{0:T(128)S(1)}, f32[128]{0:T(128)}, u32[]{:S(2)}) copy-start(f32[128]{0:T(128)} %param.9) | copy-start | bytes 1540
  98.3 24.0 %all-to-all-start.1 = ((bf16[128,3,4,128]{3,2,1,0:T(4,128)(2,1)}), bf16[128,3,4,128]{3,2,1,0:T(4,128)(2,1)S(1)}, u32[]{:S(2)}, u32[]{:S(2)}) async-start(bf16[128,3,4,128]{3,2,1,0:T(4,128)(2,1)} %reshape.50), calls=%async_computation.1 | async-start | bytes 786432 | tf_op jit(solution)/shard_map/all_to_all | solution.py:28
  123.9 50.7 %copy-start.3 = (f32[384,384]{1,0:T(8,128)S(1)}, f32[384,384]{1,0:T(8,128)}, u32[]{:S(2)}) copy-start(f32[384,384]{1,0:T(8,128)} %copy-done.2) | copy-start | bytes 1769476
  148.4 20.6 %collective-permute-start.10 = (bf16[384,512]{1,0:T(8,128)(2,1)S(1)}, bf16[384,512]{1,0:T(8,128)(2,1)S(1)}, u32[]{:S(2)}, u32[]{:S(2)}) collective-permute-start(bf16[384,512]{1,0:T(8,128)(2,1)S(1)} %bitcast.37), channel_id=1, source_target_pairs={{0,3},{1,0},{2,1},{3,2},{4,7},{5,4},{6,5},{7,6},{8,11},{9,8},{10,9... | collective-permute-start | bytes 1179656 | tf_op jit(solution)/shard_map/ppermute | solution.py:34
  153.0 16.1 %collective-permute-start.9 = (bf16[384,512]{1,0:T(8,128)(2,1)S(1)}, bf16[384,512]{1,0:T(8,128)(2,1)S(1)}, u32[]{:S(2)}, u32[]{:S(2)}) collective-permute-start(bf16[384,512]{1,0:T(8,128)(2,1)S(1)} %bitcast.38), channel_id=1, source_target_pairs={{0,2},{1,3},{2,0},{3,1},{4,6},{5,7},{6,4},{7,5},{8,10},{9,11},{10,... | collective-permute-start | bytes 1179656 | tf_op jit(solution)/shard_map/ppermute | solution.py:34
  154.9 19.7 %collective-permute-start.8 = (bf16[384,512]{1,0:T(8,128)(2,1)S(1)}, bf16[384,512]{1,0:T(8,128)(2,1)S(1)}, u32[]{:S(2)}, u32[]{:S(2)}) collective-permute-start(bf16[384,512]{1,0:T(8,128)(2,1)S(1)} %bitcast.39), channel_id=1, source_target_pairs={{0,1},{1,2},{2,3},{3,0},{4,5},{5,6},{6,7},{7,4},{8,9},{9,10},{10,1... | collective-permute-start | bytes 1179656 | tf_op jit(solution)/shard_map/ppermute | solution.py:34
  178.5 22.6 %collective-permute-start.11 = (bf16[384,512]{1,0:T(8,128)(2,1)S(1)}, bf16[384,512]{1,0:T(8,128)(2,1)S(1)}, u32[]{:S(2)}, u32[]{:S(2)}) collective-permute-start(bf16[384,512]{1,0:T(8,128)(2,1)S(1)} %get-tuple-element.20), channel_id=1, source_target_pairs={{0,1},{1,2},{2,3},{3,0},{4,5},{5,6},{6,7},{7,4},{8,9},{9,10},{10,1... | collective-permute-start | bytes 1179656 | tf_op jit(solution)/shard_map/ppermute | solution.py:34
  180.5 20.6 %collective-permute-start.12 = (bf16[384,512]{1,0:T(8,128)(2,1)S(1)}, bf16[384,512]{1,0:T(8,128)(2,1)S(1)}, u32[]{:S(2)}, u32[]{:S(2)}) collective-permute-start(bf16[384,512]{1,0:T(8,128)(2,1)S(1)} %get-tuple-element.21), channel_id=1, source_target_pairs={{0,2},{1,3},{2,0},{3,1},{4,6},{5,7},{6,4},{7,5},{8,10},{9,11},{10,... | collective-permute-start | bytes 1179656 | tf_op jit(solution)/shard_map/ppermute | solution.py:34
  184.4 19.2 %collective-permute-start.13 = (bf16[384,512]{1,0:T(8,128)(2,1)S(1)}, bf16[384,512]{1,0:T(8,128)(2,1)S(1)}, u32[]{:S(2)}, u32[]{:S(2)}) collective-permute-start(bf16[384,512]{1,0:T(8,128)(2,1)S(1)} %get-tuple-element.22), channel_id=1, source_target_pairs={{0,3},{1,0},{2,1},{3,2},{4,7},{5,4},{6,5},{7,6},{8,11},{9,8},{10,9... | collective-permute-start | bytes 1179656 | tf_op jit(solution)/shard_map/ppermute | solution.py:34
  189.3 55.3 %collective-permute-start.17 = (bf16[384,2048]{1,0:T(8,128)(2,1)}, bf16[384,2048]{1,0:T(8,128)(2,1)}, u32[]{:S(2)}, u32[]{:S(2)}) collective-permute-start(bf16[384,2048]{1,0:T(8,128)(2,1)} %shard_map.83), channel_id=1, source_target_pairs={{0,4},{4,0},{8,12},{12,8},{16,20},{20,16},{24,28},{28,24},{32,36},... | collective-permute-start | bytes 4718600 | tf_op jit(solution)/shard_map/ppermute | solution.py:50
  228.1 9.9 %collective-permute-start.16 = (bf16[128,512]{1,0:T(8,128)(2,1)S(1)}, bf16[128,512]{1,0:T(8,128)(2,1)S(1)}, u32[]{:S(2)}, u32[]{:S(2)}) collective-permute-start(bf16[128,512]{1,0:T(8,128)(2,1)S(1)} %shard_map.81.refs_0_), channel_id=1, source_target_pairs={{0,3},{1,0},{2,1},{3,2},{4,7},{5,4},{6,5},{7,6},{8,11},{9,8},{10,9... | collective-permute-start | bytes 393224 | tf_op jit(solution)/shard_map/ppermute | solution.py:34
  232.6 9.6 %collective-permute-start.15 = (bf16[128,512]{1,0:T(8,128)(2,1)S(1)}, bf16[128,512]{1,0:T(8,128)(2,1)S(1)}, u32[]{:S(2)}, u32[]{:S(2)}) collective-permute-start(bf16[128,512]{1,0:T(8,128)(2,1)S(1)} %shard_map.81.refs_0_), channel_id=1, source_target_pairs={{0,2},{1,3},{2,0},{3,1},{4,6},{5,7},{6,4},{7,5},{8,10},{9,11},{10,... | collective-permute-start | bytes 393224 | tf_op jit(solution)/shard_map/ppermute | solution.py:34
  234.6 8.7 %collective-permute-start.14 = (bf16[128,512]{1,0:T(8,128)(2,1)S(1)}, bf16[128,512]{1,0:T(8,128)(2,1)S(1)}, u32[]{:S(2)}, u32[]{:S(2)}) collective-permute-start(bf16[128,512]{1,0:T(8,128)(2,1)S(1)} %shard_map.81.refs_0_), channel_id=1, source_target_pairs={{0,1},{1,2},{2,3},{3,0},{4,5},{5,6},{6,7},{7,4},{8,9},{9,10},{10,1... | collective-permute-start | bytes 393224 | tf_op jit(solution)/shard_map/ppermute | solution.py:34

commit v3 on v1

v3 whole, which is shorter than its diff:
```python
import functools

import jax
import jax.numpy as jnp
from jax import lax
from jax.experimental import pallas as pl
from jax.experimental.pallas import tpu as pltpu
from jax.sharding import PartitionSpec as P

BF = jnp.bfloat16
F32 = jnp.float32
CORES = 2
SLOTS = 3
LANES = 128
VMEM_BYTES = 20 * 1024 * 1024
VMEM = pl.BlockSpec(memory_space=pltpu.VMEM)
SMEM = pl.BlockSpec(memory_space=pltpu.SMEM)
ANY = pl.BlockSpec(memory_space=pl.ANY)


def swish_parts(preact):
    sigmoid_part = jax.nn.sigmoid(preact)
    return (preact * sigmoid_part, sigmoid_part * (1.0 + preact * (1.0 - sigmoid_part)))


def over_chips(rows):
    count, cols = rows.shape
    experts = lax.axis_size("expert")
    chips = experts // CORES
    moved = lax.all_to_all(
        rows.reshape(chips, CORES * SLOTS, cols // LANES, LANES),
        "expert",
        split_axis=0,
        concat_axis=0,
        tiled=True,
        axis_index_groups=[list(range(core, experts, CORES)) for core in range(CORES)],
    )
    return moved.reshape(count, cols)


def over_dp(blocks):
    return lax.all_to_all(blocks, "dp", split_axis=0, concat_axis=0, tiled=True)


def gather_dp(block):
    return over_dp(jnp.broadcast_to(block[None], (lax.axis_size("dp"),) + block.shape))


def sum_dp(blocks):
    moved = over_dp(blocks)
    total = moved[0].astype(F32)
    for q in range(1, moved.shape[0]):
        total = total + moved[q].astype(F32)
    return total.astype(BF)


def swap_cores(value):
    experts = lax.axis_size("expert")
    return lax.ppermute(value, "expert", [(i, i ^ 1) for i in range(experts)])


def mm(a, b):
    return jnp.dot(a, b, preferred_element_type=F32)


def mm_t(a, b):
    return lax.dot_general(a, b, (((1,), (1,)), ((), ())), preferred_element_type=F32)


def t_mm(a, b):
    return lax.dot_general(a, b, (((0,), (0,)), ((), ())), preferred_element_type=F32)


def column_blocks(ref):
    parts, _, cols = ref.shape
    return [(q, slice(q * cols, (q + 1) * cols)) for q in range(parts)]


def rows_of_core(where_ref, shape, core):
    row = lax.broadcasted_iota(jnp.int32, shape, 0)
    at = (lax.rem(row, CORES * SLOTS) >= SLOTS).astype(jnp.int32)
    hot_core = jnp.where(where_ref[1] == 1, where_ref[0], 1 - where_ref[0])
    lent = (lax.rem(row, SLOTS) == SLOTS - 1) & (where_ref[1] != 0)
    return jnp.where(lent, hot_core, at) == core


def contract(blocks_ref, own_ref, other_ref, where_ref):
    def product(weight_ref):
        return sum(mm_t(blocks_ref[q], weight_ref[:, span]) for q, span in column_blocks(blocks_ref))

    own = product(own_ref)
    return jnp.where(rows_of_core(where_ref, own.shape, where_ref[0]), own, product(other_ref))


def expand(value, own_ref, other_ref, where_ref, out_ref):
    owned = rows_of_core(where_ref, value.shape, where_ref[0])
    mine = jnp.where(owned, value, jnp.zeros_like(value))
    theirs = jnp.where(owned, jnp.zeros_like(value), value)
    for q, span in column_blocks(out_ref):
        out_ref[q] = (mm(mine, own_ref[:, span]) + mm(theirs, other_ref[:, span])).astype(BF)


def forward_kernel(
    where_ref, rows_ref, in_ref, out_ref, other_in_ref, other_out_ref, partial_ref, proj_ref
):
    quarter = out_ref.shape[0]
    projected = contract(rows_ref, in_ref, other_in_ref, where_ref)
    proj_ref[...] = projected
    swish_value, _ = swish_parts(projected[:, :quarter])
    hidden = (swish_value * projected[:, quarter:]).astype(BF)
    expand(hidden, out_ref, other_out_ref, where_ref, partial_ref)


def backward_kernel(
    where_ref, cot_ref, proj_ref, in_ref, out_ref, other_in_ref, other_out_ref, partial_ref, pre_ref
):
    quarter = out_ref.shape[0]
    back_hidden = contract(cot_ref, out_ref, other_out_ref, where_ref)
    projected = proj_ref[...]
    swish_value, swish_slope = swish_parts(projected[:, :quarter])
    grad_pre = jnp.concatenate(
        [back_hidden * projected[:, quarter:] * swish_slope, back_hidden * swish_value], axis=1
    ).astype(BF)
    pre_ref[...] = grad_pre
    expand(grad_pre, in_ref, other_in_ref, where_ref, partial_ref)


def lent_gradient_kernel(where_ref, rows_ref, pre_ref, out_ref):
    pre = pre_ref[...]
    owned = rows_of_core(where_ref, pre.shape, where_ref[0])
    theirs = jnp.where(owned, jnp.zeros_like(pre), pre)
    for q, span in column_blocks(rows_ref):
        out_ref[:, span] = t_mm(theirs, rows_ref[q]).astype(BF)


def gradient_kernel(where_ref, rows_ref, pre_ref, lent_ref, out_ref):
    pre = pre_ref[...]
    owned = rows_of_core(where_ref, pre.shape, where_ref[0])
    mine = jnp.where(owned, pre, jnp.zeros_like(pre))
    for q, span in column_blocks(rows_ref):
        out_ref[:, span] = (t_mm(mine, rows_ref[q]) + lent_ref[:, span].astype(F32)).astype(BF)


def places(slot_ref, slots):
    shape = (slots, slot_ref.shape[1])
    row = lax.broadcasted_iota(jnp.int32, shape, 0)
    return [(row == slot_ref[k : k + 1, :]).astype(BF) for k in range(slot_ref.shape[0])]


def send_kernel(experts, routes_ref, tokens_ref, slot_ref, busiest_ref, out_ref):
    choices, local_tokens = routes_ref.shape
    square = (local_tokens, local_tokens)
    earlier = (
        lax.broadcasted_iota(jnp.int32, square, 0) < lax.broadcasted_iota(jnp.int32, square, 1)
    ).astype(BF)
    ids = lax.broadcasted_iota(jnp.int32, (experts, local_tokens), 0)
    counts = jnp.zeros((experts, 1), F32)
    for k in range(choices):
        expert = routes_ref[k : k + 1, :]
        member = ids == expert
        before = mm(member.astype(BF), earlier) + counts
        rank = jnp.sum(jnp.where(member, before, 0.0), axis=0, keepdims=True).astype(jnp.int32)
        counts += jnp.sum(member.astype(F32), axis=1, keepdims=True)
        slot_ref[k : k + 1, :] = jnp.where(
            rank == SLOTS, (expert ^ 1) * SLOTS + SLOTS - 1, expert * SLOTS + rank
        )
    most = jnp.max(counts, axis=0, keepdims=True)
    ids = lax.broadcasted_iota(jnp.int32, counts.shape, 0).astype(F32)
    busiest = jnp.sum(jnp.where(counts == most, ids, 0.0), axis=0, keepdims=True)
    busiest_ref[...] = busiest.astype(jnp.int32)
    both = sum(places(slot_ref, out_ref.shape[0]))
    out_ref[...] = mm(both, tokens_ref[...]).astype(BF)


def combine_kernel(slot_ref, route_weight_ref, loss_weight_ref, returned_ref, out_ref):
    place = places(slot_ref, out_ref.shape[0])
    choices = len(place)
    weights = [route_weight_ref[:, k : k + 1] for k in range(choices)]
    returned = returned_ref[...]
    combined = sum(weights[k] * t_mm(place[k], returned) for k in range(choices))
    loss = loss_weight_ref[...]
    out_ref[...] = sum(
        mm(place[k], (loss * weights[k] * combined).astype(BF)) for k in range(choices)
    ).astype(BF)


def collect_kernel(slot_ref, returned_ref, out_ref):
    both = sum(places(slot_ref, returned_ref.shape[0]))
    collected = t_mm(both, returned_ref[...]).astype(BF)
    for q in range(out_ref.shape[0]):
        out_ref[q] = collected


def join_kernel(parts_ref, _, out_ref):
    for q, span in column_blocks(parts_ref):
        out_ref[:, span] = parts_ref[q]


def call(kernel, outs, args, scalars=0, after=()):
    return pl.pallas_call(
        kernel,
        out_shape=outs,
        in_specs=[SMEM] * scalars + [VMEM] * (len(args) - scalars) + [ANY] * len(after),
        out_specs=jax.tree.map(lambda _: VMEM, outs),
        compiler_params=pltpu.CompilerParams(vmem_limit_bytes=VMEM_BYTES),
    )(*args, *after)


def local(tokens, routes, route_weights, loss_weights, gate_up, down_weight):
    experts = lax.axis_size("expert")
    parts = lax.axis_size("dp")
    index = lax.axis_index("expert")
    local_tokens, width = tokens.shape
    cols = width // parts
    choices = routes.shape[1]
    quarter = down_weight.shape[1]
    slots = experts * SLOTS
    own_in = gate_up.reshape(2 * quarter, width)
    own_out = down_weight.reshape(quarter, width)

    def out(*shape, dtype=BF):
        return jax.ShapeDtypeStruct(shape, dtype)

    mine = lax.dynamic_slice(
        tokens, (jnp.int32(0), lax.axis_index("dp") * cols), (local_tokens, cols)
    )
    slot, busiest, outgoing = call(
        functools.partial(send_kernel, experts),
        [out(choices, local_tokens, dtype=jnp.int32), out(1, 1, dtype=jnp.int32), out(slots, cols)],
        (routes.T, mine),
    )
    busiest = busiest[0, 0]
    hot = jnp.where(busiest == index, 1, jnp.where(busiest == (index ^ 1), 2, 0))
    where = jnp.stack([index & 1, hot]).astype(jnp.int32)

    other_in, other_out = swap_cores(own_in), swap_cores(own_out)
    weights = (own_in, own_out, other_in, other_out)
    rows = gather_dp(over_chips(outgoing))
    partial, projected = call(
        forward_kernel,
        [out(parts, slots, cols), out(slots, 2 * quarter, dtype=F32)],
        (where, rows, *weights),
        scalars=1,
    )
    returned = over_chips(sum_dp(partial))
    cot_send = call(
        combine_kernel,
        out(slots, cols),
        (slot, route_weights, loss_weights.reshape(local_tokens, 1), returned),
    )
    cot = gather_dp(over_chips(cot_send))
    input_partial, grad_pre = call(
        backward_kernel,
        [out(parts, slots, cols), out(slots, 2 * quarter)],
        (where, cot, projected, *weights),
        scalars=1,
    )
    lent = call(
        lent_gradient_kernel, out(2 * quarter, width), (where, rows, grad_pre), scalars=1
    )
    gradient = call(
        gradient_kernel,
        out(2 * quarter, width),
        (where, rows, grad_pre, swap_cores(lent)),
        scalars=1,
    )
    returned_in = over_chips(sum_dp(input_partial))
    collected = call(
        collect_kernel, out(parts, local_tokens, cols), (slot, returned_in)
    )
    input_gradient = call(
        join_kernel,
        out(local_tokens, width),
        (over_dp(collected),),
        after=(gradient,),
    )
    return (input_gradient, gradient.reshape(1, 2, quarter, width))


def solution(mesh):
    in_specs = (
        P("expert", None),
        P("expert", None),
        P("expert", None),
        P("expert"),
        P("expert", None, "dp", None),
        P("expert", "dp", None),
    )
    out_specs = (P("expert", None), P("expert", None, "dp", None))
    return jax.shard_map(local, mesh=mesh, in_specs=in_specs, out_specs=out_specs, check_vma=False)
```

time: 274 us -> 215 us (0.78)
  the two profiles are of different devices: /device:TPU:8 before, /device:TPU:16 now
where the time goes in v3:
time: 215 us
  blocking collectives  80.2 us (37%)
  waiting for transfers between devices  60.3 us (28%)
  starting transfers between devices  42 us (20%)
  Pallas kernels  19.5 us (9%)
  local copies, waits for them, and re-layouts  8.74 us (4%)
    all_to_all x2, blocking collectives, over_dp(): return lax.all_to_all(blocks, 'dp', split_axis=0, concat_axis=0, tiled=True)  40.1 us
    all_to_all x2, blocking collectives, over_chips(): lax.all_to_all(rows.reshape(chips, CORES * SLOTS, cols // LANES, LANES),...  40.1 us
    all_to_all x3, waiting for transfers between devices, over_dp(): return lax.all_to_all(blocks, 'dp', split_axis=0, concat_axis=0, tiled=True)  30.5 us
    all_to_all x2, waiting for transfers between devices, over_chips(): lax.all_to_all(rows.reshape(chips, CORES * SLOTS, cols // LANES, LANES),...  28.6 us
    all_to_all x2, starting transfers between devices, over_chips(): lax.all_to_all(rows.reshape(chips, CORES * SLOTS, cols // LANES, LANES),...  24 us
    pallas_call x8, Pallas kernels, call(): pl.pallas_call(kernel, out_shape=outs, in_specs=[SMEM] * scalars + [VMEM]...  19.5 us
    all_to_all x3, starting transfers between devices, over_dp(): return lax.all_to_all(blocks, 'dp', split_axis=0, concat_axis=0, tiled=True)  12.2 us
    ppermute x3, starting transfers between devices, swap_cores(): return lax.ppermute(value, 'expert', [(i, i ^ 1) for i in range(experts)])  5.74 us
  transfers between devices with their start and end apart: 8, of which 6 were waited for; matrix products, arithmetic and copies ran while one was open for 2% of the time, Pallas kernels for 3%

profile of v3, /device:TPU:16, one launch (start us, length us, event | category | flops | bytes accessed | tf_op | source)
XLA Modules:
  0.0 214.5 jit_solution(7864576523458190426)
XLA Ops:
  0.6 0.0 copy-start
  0.6 1.0 copy-done
  1.7 0.0 copy-start.6
  1.7 0.7 copy-done.6
  2.4 0.7 shard_map.77
  3.1 0.8 reshape.57
  3.9 16.5 %all-to-all-start = ((bf16[64,6,4,128]{3,2,1,0:T(4,128)(2,1)}), bf16[64,6,4,128]{3,2,1,0:T(4,128)(2,1)S(1)}, u32[]{:S(2)}, u32[]{:S(2)}) async-start(bf16[64,6,4,128]{3,2,1,0:T(4,128)(2,1)} %reshape.57), calls=%async_computation | async-start | bytes 786432 | tf_op jit(solution)/shard_map/all_to_all | solution.py:30
  20.4 1.9 collective-permute-start
  22.3 14.7 %all-to-all-done = bf16[64,6,4,128]{3,2,1,0:T(4,128)(2,1)S(1)} async-done(((bf16[64,6,4,128]{3,2,1,0:T(4,128)(2,1)}), bf16[64,6,4,128]{3,2,1,0:T(4,128)(2,1)S(1)}, u32[]{:S(2)}, u32[]{:S(2)}) %all-to-all-start) | async-done | bytes 393248 | tf_op jit(solution)/shard_map/all_to_all | solution.py:30
  37.0 0.1 copy.21
  37.1 1.3 broadcast_in_dim.15
  38.4 4.4 %all-to-all-start.1 = ((bf16[4,384,512]{2,1,0:T(8,128)(2,1)}), bf16[4,384,512]{2,1,0:T(8,128)(2,1)S(1)}, u32[]{:S(2)}, u32[]{:S(2)}) async-start(bf16[4,384,512]{2,1,0:T(8,128)(2,1)} %broadcast_in_dim.15), calls=%async_computation.1 | async-start | bytes 3145728 | tf_op jit(solution)/shard_map/all_to_all | solution.py:42
  42.8 1.9 collective-permute-start.1
  45.9 0.1 pad_add_fusion.where_ref
  45.9 1.2 collective-permute-done.1.other_out_ref
  47.1 14.7 %all-to-all-done.1.rows_ref = bf16[4,384,512]{2,1,0:T(8,128)(2,1)S(1)} async-done(((bf16[4,384,512]{2,1,0:T(8,128)(2,1)}), bf16[4,384,512]{2,1,0:T(8,128)(2,1)S(1)}, u32[]{:S(2)}, u32[]{:S(2)}) %all-to-all-start.1) | async-done | bytes 1572896 | tf_op jit(solution)/shard_map/all_to_all | solution.py:42
  61.8 4.9 %shard_map.78 = (bf16[4,384,512]{2,1,0:T(8,128)(2,1)S(1)}, f32[384,384]{1,0:T(8,128)S(1)}) custom-call(s32[2]{0:T(128)S(1)} %pad_add_fusion.where_ref, bf16[4,384,512]{2,1,0:T(8,128)(2,1)S(1)} %all-to-all-done.1.rows_ref, bf16[384,2048]{1,0:T(8,128)(2,1)} %bitcast.5.in_ref, bf16[192,2048]{1,0:T(8,128)(2,1)S(1)} %bitcast.30, ...), custom_call_target="tpu_custom_call" | custom-call | tf_op jit(solution)/shard_map/pallas_call | solution.py:200
  66.7 20.5 %all_to_all.45 = bf16[4,384,512]{2,1,0:T(8,128)(2,1)S(1)} all-to-all(bf16[4,384,512]{2,1,0:T(8,128)(2,1)S(1)} %get-tuple-element.12), channel_id=1, replica_groups=mesh['expert'=128,'dp'=4] {'dp'}, dimensions={0} | all-to-all | bytes 3145728 | tf_op jit(solution)/shard_map/all_to_all | solution.py:42
  87.2 0.2 add_convert_fusion.1
  87.4 0.8 add.41
  88.3 7.6 %all-to-all-start.3 = ((bf16[64,6,4,128]{3,2,1,0:T(4,128)(2,1)}), bf16[64,6,4,128]{3,2,1,0:T(4,128)(2,1)S(1)}, u32[]{:S(2)}, u32[]{:S(2)}) async-start(bf16[64,6,4,128]{3,2,1,0:T(4,128)(2,1)} %add.41), calls=%async_computation.3 | async-start | bytes 786432 | tf_op jit(solution)/shard_map/all_to_all | solution.py:30
  95.9 0.1 copy.8.route_weight_ref
  96.0 0.1 copy.9.loss_weight_ref
  96.1 13.9 %all-to-all-done.3 = bf16[64,6,4,128]{3,2,1,0:T(4,128)(2,1)S(1)} async-done(((bf16[64,6,4,128]{3,2,1,0:T(4,128)(2,1)}), bf16[64,6,4,128]{3,2,1,0:T(4,128)(2,1)S(1)}, u32[]{:S(2)}, u32[]{:S(2)}) %all-to-all-start.3) | async-done | bytes 393248 | tf_op jit(solution)/shard_map/all_to_all | solution.py:30
  110.0 0.1 copy.20
  110.0 0.7 shard_map.79
  110.7 0.8 reshape.61
  111.6 19.3 %all_to_all.46 = bf16[64,6,4,128]{3,2,1,0:T(4,128)(2,1)S(1)} all-to-all(bf16[64,6,4,128]{3,2,1,0:T(4,128)(2,1)} %reshape.61), channel_id=1, replica_groups={{0,8,16,24,32,40,48,56,64,72,80,88,96,104,112,120,128,136,144,152,160,1..., dimensions={0} | all-to-all | bytes 786432 | tf_op jit(solution)/shard_map/all_to_all | solution.py:30
  130.9 0.1 copy.19
  130.9 0.1 broadcast_in_dim.17
  131.1 19.6 %all_to_all.47.cot_ref = bf16[4,384,512]{2,1,0:T(8,128)(2,1)S(1)} all-to-all(bf16[4,384,512]{2,1,0:T(8,128)(2,1)S(1)} %broadcast_in_dim.17), channel_id=1, replica_groups=mesh['expert'=128,'dp'=4] {'dp'}, dimensions={0} | all-to-all | bytes 3145728 | tf_op jit(solution)/shard_map/all_to_all | solution.py:42
  150.6 5.0 %shard_map.80 = (bf16[4,384,512]{2,1,0:T(8,128)(2,1)S(1)}, bf16[384,384]{1,0:T(8,128)(2,1)S(1)}) custom-call(s32[2]{0:T(128)S(1)} %pad_add_fusion.where_ref, bf16[4,384,512]{2,1,0:T(8,128)(2,1)S(1)} %all_to_all.47.cot_ref, f32[384,384]{1,0:T(8,128)S(1)} %copy-done.5, bf16[384,2048]{1,0:T(8,128)(2,1)} %bitcast.5.in_ref, bf16[192,2048]{1,0:T(8,128)(2,1)S(1)} %bitcast.31, ...), custom_call_target="tpu_custom_call" | custom-call | tf_op jit(solution)/shard_map/pallas_call | solution.py:200
  155.6 0.0 copy-start.3
  155.6 1.1 copy-done.3
  156.7 4.3 %all-to-all-start.6 = ((bf16[4,384,512]{2,1,0:T(8,128)(2,1)}), bf16[4,384,512]{2,1,0:T(8,128)(2,1)}, u32[]{:S(2)}, u32[]{:S(2)}) async-start(bf16[4,384,512]{2,1,0:T(8,128)(2,1)} %copy-done.3), calls=%async_computation.6 | async-start | bytes 3145728 | tf_op jit(solution)/shard_map/all_to_all | solution.py:42
  161.1 2.8 %shard_map.82 = bf16[384,2048]{1,0:T(8,128)(2,1)} custom-call(s32[2]{0:T(128)S(1)} %pad_add_fusion.where_ref, bf16[4,384,512]{2,1,0:T(8,128)(2,1)S(1)} %all-to-all-done.1.rows_ref, bf16[384,384]{1,0:T(8,128)(2,1)S(1)} %get-tuple-element.15.pre_ref), custom_call_target="tpu_custom_call" | custom-call | tf_op jit(solution)/shard_map/pallas_call | solution.py:200
  163.9 1.9 collective-permute-start.2
  165.8 11.4 %all-to-all-done.6 = bf16[4,384,512]{2,1,0:T(8,128)(2,1)} async-done(((bf16[4,384,512]{2,1,0:T(8,128)(2,1)}), bf16[4,384,512]{2,1,0:T(8,128)(2,1)}, u32[]{:S(2)}, u32[]{:S(2)}) %all-to-all-start.6) | async-done | bytes 1572896 | tf_op jit(solution)/shard_map/all_to_all | solution.py:42
  177.2 1.6 add_convert_fusion
  178.8 0.1 add.45
  178.9 20.8 %all_to_all.48 = bf16[64,6,4,128]{3,2,1,0:T(4,128)(2,1)S(1)} all-to-all(bf16[64,6,4,128]{3,2,1,0:T(4,128)(2,1)S(1)} %add.45), channel_id=1, replica_groups={{0,8,16,24,32,40,48,56,64,72,80,88,96,104,112,120,128,136,144,152,160,1..., dimensions={0} | all-to-all | bytes 786432 | tf_op jit(solution)/shard_map/all_to_all | solution.py:30
  199.6 0.1 copy.18
  199.7 1.1 shard_map.81
  200.8 3.5 %all-to-all-start.8 = ((bf16[4,128,512]{2,1,0:T(8,128)(2,1)}), bf16[4,128,512]{2,1,0:T(8,128)(2,1)S(1)}, u32[]{:S(2)}, u32[]{:S(2)}) async-start(bf16[4,128,512]{2,1,0:T(8,128)(2,1)} %shard_map.81), calls=%async_computation.8 | async-start | bytes 1048576 | tf_op jit(solution)/shard_map/all_to_all | solution.py:42
  204.3 3.6 %shard_map.83._ = bf16[384,2048]{1,0:T(8,128)(2,1)} custom-call(s32[2]{0:T(128)S(1)} %pad_add_fusion.where_ref, bf16[4,384,512]{2,1,0:T(8,128)(2,1)S(1)} %all-to-all-done.1.rows_ref, bf16[384,384]{1,0:T(8,128)(2,1)S(1)} %get-tuple-element.15.pre_ref, bf16[384,2048]{1,0:T(8,128)(2,1)} %collective-permute-done.2.lent_ref), custom_call_target="tpu_custom_call" | custom-call | tf_op jit(solution)/shard_map/pallas_call | solution.py:200
  207.9 4.4 %all-to-all-done.8.parts_ref = bf16[4,128,512]{2,1,0:T(8,128)(2,1)S(1)} async-done(((bf16[4,128,512]{2,1,0:T(8,128)(2,1)}), bf16[4,128,512]{2,1,0:T(8,128)(2,1)S(1)}, u32[]{:S(2)}, u32[]{:S(2)}) %all-to-all-start.8) | async-done | bytes 524320 | tf_op jit(solution)/shard_map/all_to_all | solution.py:42
  212.3 1.4 copy-done.1
  213.7 0.8 shard_map.84
  (14 shorter events, 0.0 us)
Async XLA Ops:
  0.6 1.0 copy-start
  1.7 0.7 copy-start.6
  3.9 33.1 %all-to-all-start = ((bf16[64,6,4,128]{3,2,1,0:T(4,128)(2,1)}), bf16[64,6,4,128]{3,2,1,0:T(4,128)(2,1)S(1)}, u32[]{:S(2)}, u32[]{:S(2)}) async-start(bf16[64,6,4,128]{3,2,1,0:T(4,128)(2,1)} %reshape.57), calls=%async_computation | async-start | bytes 786432 | tf_op jit(solution)/shard_map/all_to_all | solution.py:30
  20.4 26.7 %collective-permute-start = (bf16[384,2048]{1,0:T(8,128)(2,1)}, bf16[384,2048]{1,0:T(8,128)(2,1)}, u32[]{:S(2)}, u32[]{:S(2)}) collective-permute-start(bf16[384,2048]{1,0:T(8,128)(2,1)} %bitcast.5.in_ref), channel_id=1, source_target_pairs={{0,4},{4,0},{8,12},{12,8},{16,20},{20,16},{24,28},{28,24},{32,36},... | collective-permute-start | bytes 4718600 | tf_op jit(solution)/shard_map/ppermute | solution.py:59
  38.3 4.4 %copy-start.2 = (bf16[1,192,2048]{2,1,0:T(8,128)(2,1)S(1)}, bf16[1,192,2048]{2,1,0:T(8,128)(2,1)}, u32[]{:S(2)}) copy-start(bf16[1,192,2048]{2,1,0:T(8,128)(2,1)} %param.11) | copy-start | bytes 2359300
  38.4 23.4 %all-to-all-start.1 = ((bf16[4,384,512]{2,1,0:T(8,128)(2,1)}), bf16[4,384,512]{2,1,0:T(8,128)(2,1)S(1)}, u32[]{:S(2)}, u32[]{:S(2)}) async-start(bf16[4,384,512]{2,1,0:T(8,128)(2,1)} %broadcast_in_dim.15), calls=%async_computation.1 | async-start | bytes 3145728 | tf_op jit(solution)/shard_map/all_to_all | solution.py:42
  42.8 4.3 %collective-permute-start.1 = (bf16[192,2048]{1,0:T(8,128)(2,1)S(1)}, bf16[192,2048]{1,0:T(8,128)(2,1)}, u32[]{:S(2)}, u32[]{:S(2)}) collective-permute-start(bf16[192,2048]{1,0:T(8,128)(2,1)S(1)} %bitcast.29), channel_id=1, source_target_pairs={{0,4},{4,0},{8,12},{12,8},{16,20},{20,16},{24,28},{28,24},{32,36},... | collective-permute-start | bytes 2359304 | tf_op jit(solution)/shard_map/ppermute | solution.py:59
  66.7 20.6 %copy-start.4 = (f32[384,384]{1,0:T(8,128)}, f32[384,384]{1,0:T(8,128)S(1)}, u32[]{:S(2)}) copy-start(f32[384,384]{1,0:T(8,128)S(1)} %get-tuple-element.13.proj_ref) | copy-start | bytes 1769476
  87.2 8.6 %copy-start.7 = (f32[128,2]{0,1:T(2,128)S(1)}, f32[128,2]{0,1:T(2,128)}, u32[]{:S(2)}) copy-start(f32[128,2]{0,1:T(2,128)} %param.8) | copy-start | bytes 3076
  87.2 8.7 %copy-start.8 = (f32[128]{0:T(128)S(1)}, f32[128]{0:T(128)}, u32[]{:S(2)}) copy-start(f32[128]{0:T(128)} %param.9) | copy-start | bytes 1540
  88.3 21.7 %all-to-all-start.3 = ((bf16[64,6,4,128]{3,2,1,0:T(4,128)(2,1)}), bf16[64,6,4,128]{3,2,1,0:T(4,128)(2,1)S(1)}, u32[]{:S(2)}, u32[]{:S(2)}) async-start(bf16[64,6,4,128]{3,2,1,0:T(4,128)(2,1)} %add.41), calls=%async_computation.3 | async-start | bytes 786432 | tf_op jit(solution)/shard_map/all_to_all | solution.py:30
  131.1 19.6 %copy-start.5 = (f32[384,384]{1,0:T(8,128)S(1)}, f32[384,384]{1,0:T(8,128)}, u32[]{:S(2)}) copy-start(f32[384,384]{1,0:T(8,128)} %copy-done.4) | copy-start | bytes 1769476
  155.6 1.1 copy-start.3
  156.7 20.5 %all-to-all-start.6 = ((bf16[4,384,512]{2,1,0:T(8,128)(2,1)}), bf16[4,384,512]{2,1,0:T(8,128)(2,1)}, u32[]{:S(2)}, u32[]{:S(2)}) async-start(bf16[4,384,512]{2,1,0:T(8,128)(2,1)} %copy-done.3), calls=%async_computation.6 | async-start | bytes 3145728 | tf_op jit(solution)/shard_map/all_to_all | solution.py:42
  163.9 40.4 %collective-permute-start.2 = (bf16[384,2048]{1,0:T(8,128)(2,1)}, bf16[384,2048]{1,0:T(8,128)(2,1)}, u32[]{:S(2)}, u32[]{:S(2)}) collective-permute-start(bf16[384,2048]{1,0:T(8,128)(2,1)} %shard_map.82), channel_id=1, source_target_pairs={{0,4},{4,0},{8,12},{12,8},{16,20},{20,16},{24,28},{28,24},{32,36},... | collective-permute-start | bytes 4718600 | tf_op jit(solution)/shard_map/ppermute | solution.py:59
  200.8 11.5 %all-to-all-start.8 = ((bf16[4,128,512]{2,1,0:T(8,128)(2,1)}), bf16[4,128,512]{2,1,0:T(8,128)(2,1)S(1)}, u32[]{:S(2)}, u32[]{:S(2)}) async-start(bf16[4,128,512]{2,1,0:T(8,128)(2,1)} %shard_map.81), calls=%async_computation.8 | async-start | bytes 1048576 | tf_op jit(solution)/shard_map/all_to_all | solution.py:42
  212.3 1.4 copy-start.1

commit v4 on v3

--- a/solution.py
+++ b/solution.py
@@ -15,7 +15,7 @@
 VMEM_BYTES = 20 * 1024 * 1024
 VMEM = pl.BlockSpec(memory_space=pltpu.VMEM)
 SMEM = pl.BlockSpec(memory_space=pltpu.SMEM)
-ANY = pl.BlockSpec(memory_space=pl.ANY)
+HBM = pl.BlockSpec(memory_space=pltpu.HBM)
 
 
 def swish_parts(preact):
@@ -24,7 +24,8 @@
 
 
 def over_chips(rows):
-    count, cols = rows.shape
+    count = rows.shape[0]
+    cols = rows.size // count
     experts = lax.axis_size("expert")
     chips = experts // CORES
     moved = lax.all_to_all(
@@ -84,45 +85,75 @@
     return jnp.where(lent, hot_core, at) == core
 
 
-def contract(blocks_ref, own_ref, other_ref, where_ref):
+def fetch(sources, targets, sems):
+    copies = [
+        pltpu.make_async_copy(source, target, sems.at[i])
+        for i, (source, target) in enumerate(zip(sources, targets))
+    ]
+    for copy in copies:
+        copy.start()
+    return [copy.wait for copy in copies]
+
+
+def contract(blocks_ref, own_ref, other_ref, where_ref, own_here, other_here):
     def product(weight_ref):
         return sum(mm_t(blocks_ref[q], weight_ref[:, span]) for q, span in column_blocks(blocks_ref))
 
+    own_here()
     own = product(own_ref)
-    return jnp.where(rows_of_core(where_ref, own.shape, where_ref[0]), own, product(other_ref))
-
-
-def expand(value, own_ref, other_ref, where_ref, out_ref):
+    other_here()
+    other = product(other_ref)
+    return jnp.where(rows_of_core(where_ref, own.shape, where_ref[0]), own, other)
+
+
+def expand(value, own_ref, other_ref, where_ref, out_ref, done=lambda q: None):
     owned = rows_of_core(where_ref, value.shape, where_ref[0])
     mine = jnp.where(owned, value, jnp.zeros_like(value))
     theirs = jnp.where(owned, jnp.zeros_like(value), value)
     for q, span in column_blocks(out_ref):
         out_ref[q] = (mm(mine, own_ref[:, span]) + mm(theirs, other_ref[:, span])).astype(BF)
-
-
-def forward_kernel(
-    where_ref, rows_ref, in_ref, out_ref, other_in_ref, other_out_ref, partial_ref, proj_ref
-):
+        done(q)
+
+
+def forward_kernel(where_ref, rows_ref, *refs):
+    sources, (partial_ref, proj_ref), held, sems = refs[:4], refs[4:6], refs[6:10], refs[10]
+    in_ref, other_in_ref, out_ref, other_out_ref = held
+    in_here, other_in_here, out_here, other_out_here = fetch(sources, held, sems)
     quarter = out_ref.shape[0]
-    projected = contract(rows_ref, in_ref, other_in_ref, where_ref)
+    projected = contract(rows_ref, in_ref, other_in_ref, where_ref, in_here, other_in_here)
     proj_ref[...] = projected
     swish_value, _ = swish_parts(projected[:, :quarter])
     hidden = (swish_value * projected[:, quarter:]).astype(BF)
+    out_here()
+    other_out_here()
     expand(hidden, out_ref, other_out_ref, where_ref, partial_ref)
 
 
-def backward_kernel(
-    where_ref, cot_ref, proj_ref, in_ref, out_ref, other_in_ref, other_out_ref, partial_ref, pre_ref
-):
+def backward_kernel(where_ref, cot_ref, proj_ref, *refs):
+    sources, (partial_ref, pre_ref), held, sems = refs[:4], refs[4:6], refs[6:10], refs[10]
+    block_ref, block_sems = refs[11:]
+    out_ref, other_out_ref, in_ref, other_in_ref = held
+    out_here, other_out_here, in_here, other_in_here = fetch(sources, held, sems)
     quarter = out_ref.shape[0]
-    back_hidden = contract(cot_ref, out_ref, other_out_ref, where_ref)
+    back_hidden = contract(cot_ref, out_ref, other_out_ref, where_ref, out_here, other_out_here)
     projected = proj_ref[...]
     swish_value, swish_slope = swish_parts(projected[:, :quarter])
     grad_pre = jnp.concatenate(
         [back_hidden * projected[:, quarter:] * swish_slope, back_hidden * swish_value], axis=1
     ).astype(BF)
     pre_ref[...] = grad_pre
-    expand(grad_pre, in_ref, other_in_ref, where_ref, partial_ref)
+    in_here()
+    other_in_here()
+    sent = []
+
+    def send(q):
+        copy = pltpu.make_async_copy(block_ref.at[q], partial_ref.at[q], block_sems.at[q])
+        copy.start()
+        sent.append(copy)
+
+    expand(grad_pre, in_ref, other_in_ref, where_ref, block_ref, send)
+    for copy in sent:
+        copy.wait()
 
 
 def lent_gradient_kernel(where_ref, rows_ref, pre_ref, out_ref):
@@ -133,12 +164,13 @@
         out_ref[:, span] = t_mm(theirs, rows_ref[q]).astype(BF)
 
 
-def gradient_kernel(where_ref, rows_ref, pre_ref, lent_ref, out_ref):
+def gradient_kernel(where_ref, rows_ref, pre_ref, lent_ref, out_ref, done_ref):
     pre = pre_ref[...]
     owned = rows_of_core(where_ref, pre.shape, where_ref[0])
     mine = jnp.where(owned, pre, jnp.zeros_like(pre))
     for q, span in column_blocks(rows_ref):
         out_ref[:, span] = (t_mm(mine, rows_ref[q]) + lent_ref[:, span].astype(F32)).astype(BF)
+    done_ref[...] = jnp.zeros_like(done_ref)
 
 
 def places(slot_ref, slots):
@@ -147,8 +179,14 @@
     return [(row == slot_ref[k : k + 1, :]).astype(BF) for k in range(slot_ref.shape[0])]
 
 
-def send_kernel(experts, routes_ref, tokens_ref, slot_ref, busiest_ref, out_ref):
+def send_kernel(
+    experts, part_ref, routes_ref, tokens_ref, slot_ref, busiest_ref, out_ref, held_ref, sem
+):
     choices, local_tokens = routes_ref.shape
+    cols = held_ref.shape[1]
+    span = pl.ds(pl.multiple_of(part_ref[0] * cols, cols), cols)
+    copy = pltpu.make_async_copy(tokens_ref.at[:, span], held_ref, sem)
+    copy.start()
     square = (local_tokens, local_tokens)
     earlier = (
         lax.broadcasted_iota(jnp.int32, square, 0) < lax.broadcasted_iota(jnp.int32, square, 1)
@@ -169,7 +207,8 @@
     busiest = jnp.sum(jnp.where(counts == most, ids, 0.0), axis=0, keepdims=True)
     busiest_ref[...] = busiest.astype(jnp.int32)
     both = sum(places(slot_ref, out_ref.shape[0]))
-    out_ref[...] = mm(both, tokens_ref[...]).astype(BF)
+    copy.wait()
+    out_ref[...] = mm(both, held_ref[...]).astype(BF).reshape(out_ref.shape)
 
 
 def combine_kernel(slot_ref, route_weight_ref, loss_weight_ref, returned_ref, out_ref):
@@ -181,7 +220,7 @@
     loss = loss_weight_ref[...]
     out_ref[...] = sum(
         mm(place[k], (loss * weights[k] * combined).astype(BF)) for k in range(choices)
-    ).astype(BF)
+    ).astype(BF).reshape(out_ref.shape)
 
 
 def collect_kernel(slot_ref, returned_ref, out_ref):
@@ -191,19 +230,21 @@
         out_ref[q] = collected
 
 
-def join_kernel(parts_ref, _, out_ref):
+def join_kernel(parts_ref, done_ref, out_ref):
+    del done_ref
     for q, span in column_blocks(parts_ref):
         out_ref[:, span] = parts_ref[q]
 
 
-def call(kernel, outs, args, scalars=0, after=()):
+def call(kernel, outs, args, ins=None, out_specs=None, scratch=()):
     return pl.pallas_call(
         kernel,
         out_shape=outs,
-        in_specs=[SMEM] * scalars + [VMEM] * (len(args) - scalars) + [ANY] * len(after),
-        out_specs=jax.tree.map(lambda _: VMEM, outs),
+        in_specs=ins or [VMEM] * len(args),
+        out_specs=out_specs or jax.tree.map(lambda _: VMEM, outs),
+        scratch_shapes=list(scratch),
         compiler_params=pltpu.CompilerParams(vmem_limit_bytes=VMEM_BYTES),
-    )(*args, *after)
+    )(*args)
 
 
 def local(tokens, routes, route_weights, loss_weights, gate_up, down_weight):
@@ -221,58 +262,62 @@
     def out(*shape, dtype=BF):
         return jax.ShapeDtypeStruct(shape, dtype)
 
-    mine = lax.dynamic_slice(
-        tokens, (jnp.int32(0), lax.axis_index("dp") * cols), (local_tokens, cols)
-    )
+    dma = pltpu.SemaphoreType.DMA
+    sent = out(slots, cols // LANES, LANES)
     slot, busiest, outgoing = call(
         functools.partial(send_kernel, experts),
-        [out(choices, local_tokens, dtype=jnp.int32), out(1, 1, dtype=jnp.int32), out(slots, cols)],
-        (routes.T, mine),
+        [out(choices, local_tokens, dtype=jnp.int32), out(1, 1, dtype=jnp.int32), sent],
+        (lax.axis_index("dp").reshape(1), routes.T, tokens),
+        ins=[SMEM, VMEM, HBM],
+        scratch=[pltpu.VMEM((local_tokens, cols), BF), dma],
     )
     busiest = busiest[0, 0]
     hot = jnp.where(busiest == index, 1, jnp.where(busiest == (index ^ 1), 2, 0))
     where = jnp.stack([index & 1, hot]).astype(jnp.int32)
 
     other_in, other_out = swap_cores(own_in), swap_cores(own_out)
-    weights = (own_in, own_out, other_in, other_out)
+    held = [pltpu.VMEM(w.shape, BF) for w in (own_in, own_in, own_out, own_out)]
     rows = gather_dp(over_chips(outgoing))
     partial, projected = call(
         forward_kernel,
         [out(parts, slots, cols), out(slots, 2 * quarter, dtype=F32)],
-        (where, rows, *weights),
-        scalars=1,
+        (where, rows, own_in, other_in, own_out, other_out),
+        ins=[SMEM, VMEM] + [HBM] * 4,
+        scratch=[*held, dma((4,))],
     )
     returned = over_chips(sum_dp(partial))
     cot_send = call(
         combine_kernel,
-        out(slots, cols),
+        sent,
         (slot, route_weights, loss_weights.reshape(local_tokens, 1), returned),
     )
     cot = gather_dp(over_chips(cot_send))
     input_partial, grad_pre = call(
         backward_kernel,
         [out(parts, slots, cols), out(slots, 2 * quarter)],
-        (where, cot, projected, *weights),
-        scalars=1,
+        (where, cot, projected, own_out, other_out, own_in, other_in),
+        ins=[SMEM, VMEM, VMEM] + [HBM] * 4,
+        out_specs=[HBM, VMEM],
+        scratch=[*held[2:], *held[:2], dma((4,)), pltpu.VMEM((parts, slots, cols), BF), dma((parts,))],
     )
     lent = call(
-        lent_gradient_kernel, out(2 * quarter, width), (where, rows, grad_pre), scalars=1
-    )
-    gradient = call(
+        lent_gradient_kernel,
+        out(2 * quarter, width),
+        (where, rows, grad_pre),
+        ins=[SMEM, VMEM, VMEM],
+    )
+    gradient, gradient_done = call(
         gradient_kernel,
-        out(2 * quarter, width),
+        [out(2 * quarter, width), out(8, LANES, dtype=F32)],
         (where, rows, grad_pre, swap_cores(lent)),
-        scalars=1,
+        ins=[SMEM, VMEM, VMEM, VMEM],
     )
     returned_in = over_chips(sum_dp(input_partial))
     collected = call(
         collect_kernel, out(parts, local_tokens, cols), (slot, returned_in)
     )
     input_gradient = call(
-        join_kernel,
-        out(local_tokens, width),
-        (over_dp(collected),),
-        after=(gradient,),
+        join_kernel, out(local_tokens, width), (over_dp(collected), gradient_done)
     )
     return (input_gradient, gradient.reshape(1, 2, quarter, width))
 

time: 215 us -> 219 us (1.019)
  blocking collectives: 80.2 us -> 83.7 us
    all_to_all x2, blocking collectives: 40.1 us -> 43.6 us  [over_chips(): lax.all_to_all(rows.reshape(chips, CORES * SLOTS, cols // LANES, LANES),...]
    unnamed x23 -> x25, local copies, waits for them, and re-layouts: 4.62 us -> 5.35 us
where the time goes in v4:
time: 219 us; the launch traced here: 218 us
  blocking collectives  83.7 us (38%)
  waiting for transfers between devices  60 us (27%)
  starting transfers between devices  41.4 us (19%)
  Pallas kernels  20.5 us (9%)
  local copies, waits for them, and re-layouts  8.78 us (4%)
    all_to_all x2, blocking collectives, over_chips(): lax.all_to_all(rows.reshape(chips, CORES * SLOTS, cols // LANES, LANES),...  43.6 us
    all_to_all x2, blocking collectives, over_dp(): return lax.all_to_all(blocks, 'dp', split_axis=0, concat_axis=0, tiled=True)  40.1 us
    all_to_all x3, waiting for transfers between devices, over_dp(): return lax.all_to_all(blocks, 'dp', split_axis=0, concat_axis=0, tiled=True)  30.2 us
    all_to_all x2, waiting for transfers between devices, over_chips(): lax.all_to_all(rows.reshape(chips, CORES * SLOTS, cols // LANES, LANES),...  28.5 us
    all_to_all x2, starting transfers between devices, over_chips(): lax.all_to_all(rows.reshape(chips, CORES * SLOTS, cols // LANES, LANES),...  24.2 us
    pallas_call x8, Pallas kernels, call(): pl.pallas_call(kernel, out_shape=outs, in_specs=ins or [VMEM] * len(args)...  20.5 us
    all_to_all x3, starting transfers between devices, over_dp(): return lax.all_to_all(blocks, 'dp', split_axis=0, concat_axis=0, tiled=True)  11.5 us
    ppermute x3, starting transfers between devices, swap_cores(): return lax.ppermute(value, 'expert', [(i, i ^ 1) for i in range(experts)])  5.74 us
  transfers between devices with their start and end apart: 8, of which 6 were waited for; matrix products, arithmetic and copies ran while one was open for 2% of the time, Pallas kernels for 3%

profile of v4, /device:TPU:16, one launch (start us, length us, event | category | flops | bytes accessed | tf_op | source)
XLA Modules:
  0.0 217.6 jit_solution(7300601031038575639)
XLA Ops:
  0.6 1.0 copy-done.6
  1.7 0.7 copy-done.7
  2.4 1.3 shard_map.77
  3.6 16.5 %all-to-all-start = ((bf16[64,6,4,128]{3,2,1,0:T(4,128)(2,1)}), bf16[64,6,4,128]{3,2,1,0:T(4,128)(2,1)S(1)}, u32[]{:S(2)}, u32[]{:S(2)}) async-start(bf16[64,6,4,128]{3,2,1,0:T(4,128)(2,1)} %bitcast.6), calls=%async_computation | async-start | bytes 786432 | tf_op jit(solution)/shard_map/all_to_all | solution.py:31
  20.1 1.9 collective-permute-start
  22.1 14.7 %all-to-all-done = bf16[64,6,4,128]{3,2,1,0:T(4,128)(2,1)S(1)} async-done(((bf16[64,6,4,128]{3,2,1,0:T(4,128)(2,1)}), bf16[64,6,4,128]{3,2,1,0:T(4,128)(2,1)S(1)}, u32[]{:S(2)}, u32[]{:S(2)}) %all-to-all-start) | async-done | bytes 393248 | tf_op jit(solution)/shard_map/all_to_all | solution.py:31
  36.8 0.1 copy.21
  36.8 1.3 broadcast_in_dim.15
  38.1 4.4 %all-to-all-start.1 = ((bf16[4,384,512]{2,1,0:T(8,128)(2,1)}), bf16[4,384,512]{2,1,0:T(8,128)(2,1)S(1)}, u32[]{:S(2)}, u32[]{:S(2)}) async-start(bf16[4,384,512]{2,1,0:T(8,128)(2,1)} %broadcast_in_dim.15), calls=%async_computation.1 | async-start | bytes 3145728 | tf_op jit(solution)/shard_map/all_to_all | solution.py:43
  42.5 1.9 collective-permute-start.1
  45.6 0.1 pad_add_fusion.where_ref
  45.7 1.4 collective-permute-done.1.refs_3_.refs_1_
  47.0 0.0 collective-permute-done.refs_1_.refs_3_
  47.0 14.5 %all-to-all-done.1.rows_ref = bf16[4,384,512]{2,1,0:T(8,128)(2,1)S(1)} async-done(((bf16[4,384,512]{2,1,0:T(8,128)(2,1)}), bf16[4,384,512]{2,1,0:T(8,128)(2,1)S(1)}, u32[]{:S(2)}, u32[]{:S(2)}) %all-to-all-start.1) | async-done | bytes 1572896 | tf_op jit(solution)/shard_map/all_to_all | solution.py:43
  61.6 1.1 copy-done.1
  62.7 4.2 %shard_map.78 = (bf16[4,384,512]{2,1,0:T(8,128)(2,1)S(1)}, f32[384,384]{1,0:T(8,128)S(1)}) custom-call(s32[2]{0:T(128)S(1)} %pad_add_fusion.where_ref, bf16[4,384,512]{2,1,0:T(8,128)(2,1)S(1)} %all-to-all-done.1.rows_ref, bf16[384,2048]{1,0:T(8,128)(2,1)S(1)} %bitcast.32, bf16[384,2048]{1,0:T(8,128)(2,1)} %collective-permute-done.refs_1_.refs_3_, ...), custom_call_target="tpu_custom_call" | custom-call | tf_op jit(solution)/shard_map/pallas_call | solution.py:240
  66.9 0.0 copy-start.4
  66.9 20.5 %all_to_all.45 = bf16[4,384,512]{2,1,0:T(8,128)(2,1)S(1)} all-to-all(bf16[4,384,512]{2,1,0:T(8,128)(2,1)S(1)} %get-tuple-element.14), channel_id=1, replica_groups=mesh['expert'=128,'dp'=4] {'dp'}, dimensions={0} | all-to-all | bytes 3145728 | tf_op jit(solution)/shard_map/all_to_all | solution.py:43
  87.4 0.2 add_convert_fusion.1
  87.6 0.8 add.37
  88.5 7.7 %all-to-all-start.3 = ((bf16[64,6,4,128]{3,2,1,0:T(4,128)(2,1)}), bf16[64,6,4,128]{3,2,1,0:T(4,128)(2,1)}, u32[]{:S(2)}, u32[]{:S(2)}) async-start(bf16[64,6,4,128]{3,2,1,0:T(4,128)(2,1)} %add.37), calls=%async_computation.3 | async-start | bytes 786432 | tf_op jit(solution)/shard_map/all_to_all | solution.py:31
  96.2 0.1 copy.8.route_weight_ref
  96.4 0.1 copy.9.loss_weight_ref
  96.5 13.8 %all-to-all-done.3 = bf16[64,6,4,128]{3,2,1,0:T(4,128)(2,1)} async-done(((bf16[64,6,4,128]{3,2,1,0:T(4,128)(2,1)}), bf16[64,6,4,128]{3,2,1,0:T(4,128)(2,1)}, u32[]{:S(2)}, u32[]{:S(2)}) %all-to-all-start.3) | async-done | bytes 393248 | tf_op jit(solution)/shard_map/all_to_all | solution.py:31
  110.3 1.1 copy.20
  111.3 0.7 shard_map.79
  112.0 19.2 %all_to_all.46 = bf16[64,6,4,128]{3,2,1,0:T(4,128)(2,1)S(1)} all-to-all(bf16[64,6,4,128]{3,2,1,0:T(4,128)(2,1)S(1)} %bitcast.38), channel_id=1, replica_groups={{0,8,16,24,32,40,48,56,64,72,80,88,96,104,112,120,128,136,144,152,160,1..., dimensions={0} | all-to-all | bytes 786432 | tf_op jit(solution)/shard_map/all_to_all | solution.py:31
  131.2 0.1 copy.19
  131.3 0.1 broadcast_in_dim.17
  131.4 0.0 copy-start.2
  131.4 0.0 copy-start.5
  131.4 19.5 %all_to_all.47.cot_ref = bf16[4,384,512]{2,1,0:T(8,128)(2,1)S(1)} all-to-all(bf16[4,384,512]{2,1,0:T(8,128)(2,1)S(1)} %broadcast_in_dim.17), channel_id=1, replica_groups=mesh['expert'=128,'dp'=4] {'dp'}, dimensions={0} | all-to-all | bytes 3145728 | tf_op jit(solution)/shard_map/all_to_all | solution.py:43
  150.9 6.0 %shard_map.80 = (bf16[4,384,512]{2,1,0:T(8,128)(2,1)S(1)}, bf16[384,384]{1,0:T(8,128)(2,1)S(1)}) custom-call(s32[2]{0:T(128)S(1)} %pad_add_fusion.where_ref, bf16[4,384,512]{2,1,0:T(8,128)(2,1)S(1)} %all_to_all.47.cot_ref, f32[384,384]{1,0:T(8,128)S(1)} %copy-done.5, bf16[192,2048]{1,0:T(8,128)(2,1)S(1)} %bitcast.36, ...), custom_call_target="tpu_custom_call" | custom-call | tf_op jit(solution)/shard_map/pallas_call | solution.py:240
  156.9 0.0 copy-start.3
  157.0 1.1 copy-done.3
  158.1 3.6 %all-to-all-start.6 = ((bf16[4,384,512]{2,1,0:T(8,128)(2,1)}), bf16[4,384,512]{2,1,0:T(8,128)(2,1)S(1)}, u32[]{:S(2)}, u32[]{:S(2)}) async-start(bf16[4,384,512]{2,1,0:T(8,128)(2,1)} %copy-done.3), calls=%async_computation.6 | async-start | bytes 3145728 | tf_op jit(solution)/shard_map/all_to_all | solution.py:43
  161.7 2.8 %shard_map.82 = bf16[384,2048]{1,0:T(8,128)(2,1)} custom-call(s32[2]{0:T(128)S(1)} %pad_add_fusion.where_ref, bf16[4,384,512]{2,1,0:T(8,128)(2,1)S(1)} %all-to-all-done.1.rows_ref, bf16[384,384]{1,0:T(8,128)(2,1)S(1)} %get-tuple-element.17.pre_ref), custom_call_target="tpu_custom_call" | custom-call | tf_op jit(solution)/shard_map/pallas_call | solution.py:240
  164.5 1.9 collective-permute-start.2
  166.4 11.3 %all-to-all-done.6 = bf16[4,384,512]{2,1,0:T(8,128)(2,1)S(1)} async-done(((bf16[4,384,512]{2,1,0:T(8,128)(2,1)}), bf16[4,384,512]{2,1,0:T(8,128)(2,1)S(1)}, u32[]{:S(2)}, u32[]{:S(2)}) %all-to-all-start.6) | async-done | bytes 1572896 | tf_op jit(solution)/shard_map/all_to_all | solution.py:43
  177.6 0.9 add_convert_fusion
  178.6 1.1 add.41
  179.7 24.5 %all_to_all.48 = bf16[64,6,4,128]{3,2,1,0:T(4,128)(2,1)S(1)} all-to-all(bf16[64,6,4,128]{3,2,1,0:T(4,128)(2,1)S(1)} %add.41), channel_id=1, replica_groups={{0,8,16,24,32,40,48,56,64,72,80,88,96,104,112,120,128,136,144,152,160,1..., dimensions={0} | all-to-all | bytes 786432 | tf_op jit(solution)/shard_map/all_to_all | solution.py:31
  204.1 0.1 copy.18
  204.2 1.1 shard_map.81
  205.3 3.5 %all-to-all-start.8 = ((bf16[4,128,512]{2,1,0:T(8,128)(2,1)}), bf16[4,128,512]{2,1,0:T(8,128)(2,1)S(1)}, u32[]{:S(2)}, u32[]{:S(2)}) async-start(bf16[4,128,512]{2,1,0:T(8,128)(2,1)} %shard_map.81), calls=%async_computation.8 | async-start | bytes 1048576 | tf_op jit(solution)/shard_map/all_to_all | solution.py:43
  208.8 3.6 %shard_map.83 = (bf16[384,2048]{1,0:T(8,128)(2,1)}, f32[8,128]{1,0:T(8,128)S(1)}) custom-call(s32[2]{0:T(128)S(1)} %pad_add_fusion.where_ref, bf16[4,384,512]{2,1,0:T(8,128)(2,1)S(1)} %all-to-all-done.1.rows_ref, bf16[384,384]{1,0:T(8,128)(2,1)S(1)} %get-tuple-element.17.pre_ref, bf16[384,2048]{1,0:T(8,128)(2,1)} %collective-permute-done.2.lent_ref), custom_call_target="tpu_custom_call" | custom-call | tf_op jit(solution)/shard_map/pallas_call | solution.py:240
  212.4 4.4 %all-to-all-done.8.parts_ref = bf16[4,128,512]{2,1,0:T(8,128)(2,1)S(1)} async-done(((bf16[4,128,512]{2,1,0:T(8,128)(2,1)}), bf16[4,128,512]{2,1,0:T(8,128)(2,1)S(1)}, u32[]{:S(2)}, u32[]{:S(2)}) %all-to-all-start.8) | async-done | bytes 524320 | tf_op jit(solution)/shard_map/all_to_all | solution.py:43
  216.8 0.8 shard_map.84
  (13 shorter events, 0.0 us)
Async XLA Ops:
  0.6 1.0 copy-start.6
  1.7 0.7 copy-start.7
  3.6 33.1 %all-to-all-start = ((bf16[64,6,4,128]{3,2,1,0:T(4,128)(2,1)}), bf16[64,6,4,128]{3,2,1,0:T(4,128)(2,1)S(1)}, u32[]{:S(2)}, u32[]{:S(2)}) async-start(bf16[64,6,4,128]{3,2,1,0:T(4,128)(2,1)} %bitcast.6), calls=%async_computation | async-start | bytes 786432 | tf_op jit(solution)/shard_map/all_to_all | solution.py:31
  20.1 26.9 %collective-permute-start = (bf16[384,2048]{1,0:T(8,128)(2,1)}, bf16[384,2048]{1,0:T(8,128)(2,1)}, u32[]{:S(2)}, u32[]{:S(2)}) collective-permute-start(bf16[384,2048]{1,0:T(8,128)(2,1)} %bitcast.31), channel_id=1, source_target_pairs={{0,4},{4,0},{8,12},{12,8},{16,20},{20,16},{24,28},{28,24},{32,36},... | collective-permute-start | bytes 4718600 | tf_op jit(solution)/shard_map/ppermute | solution.py:60
  38.1 23.4 %copy-start = (bf16[1,2,192,2048]{3,2,1,0:T(8,128)(2,1)S(1)}, bf16[1,2,192,2048]{3,2,1,0:T(8,128)(2,1)}, u32[]{:S(2)}) copy-start(bf16[1,2,192,2048]{3,2,1,0:T(8,128)(2,1)} %param.10) | copy-start | bytes 4718596
  38.1 23.4 %all-to-all-start.1 = ((bf16[4,384,512]{2,1,0:T(8,128)(2,1)}), bf16[4,384,512]{2,1,0:T(8,128)(2,1)S(1)}, u32[]{:S(2)}, u32[]{:S(2)}) async-start(bf16[4,384,512]{2,1,0:T(8,128)(2,1)} %broadcast_in_dim.15), calls=%async_computation.1 | async-start | bytes 3145728 | tf_op jit(solution)/shard_map/all_to_all | solution.py:43
  42.5 4.5 %collective-permute-start.1 = (bf16[192,2048]{1,0:T(8,128)(2,1)}, bf16[192,2048]{1,0:T(8,128)(2,1)}, u32[]{:S(2)}, u32[]{:S(2)}) collective-permute-start(bf16[192,2048]{1,0:T(8,128)(2,1)} %bitcast.34), channel_id=1, source_target_pairs={{0,4},{4,0},{8,12},{12,8},{16,20},{20,16},{24,28},{28,24},{32,36},... | collective-permute-start | bytes 2359304 | tf_op jit(solution)/shard_map/ppermute | solution.py:60
  61.6 1.1 copy-start.1
  66.9 20.6 %copy-start.4 = (f32[384,384]{1,0:T(8,128)}, f32[384,384]{1,0:T(8,128)S(1)}, u32[]{:S(2)}) copy-start(f32[384,384]{1,0:T(8,128)S(1)} %get-tuple-element.15.proj_ref) | copy-start | bytes 1769476
  87.4 8.8 %copy-start.8 = (f32[128,2]{0,1:T(2,128)S(1)}, f32[128,2]{0,1:T(2,128)}, u32[]{:S(2)}) copy-start(f32[128,2]{0,1:T(2,128)} %param.8) | copy-start | bytes 3076
  87.4 8.9 %copy-start.9 = (f32[128]{0:T(128)S(1)}, f32[128]{0:T(128)}, u32[]{:S(2)}) copy-start(f32[128]{0:T(128)} %param.9) | copy-start | bytes 1540
  88.5 21.8 %all-to-all-start.3 = ((bf16[64,6,4,128]{3,2,1,0:T(4,128)(2,1)}), bf16[64,6,4,128]{3,2,1,0:T(4,128)(2,1)}, u32[]{:S(2)}, u32[]{:S(2)}) async-start(bf16[64,6,4,128]{3,2,1,0:T(4,128)(2,1)} %add.37), calls=%async_computation.3 | async-start | bytes 786432 | tf_op jit(solution)/shard_map/all_to_all | solution.py:31
  131.4 19.5 %copy-start.2 = (bf16[1,192,2048]{2,1,0:T(8,128)(2,1)S(1)}, bf16[1,192,2048]{2,1,0:T(8,128)(2,1)}, u32[]{:S(2)}) copy-start(bf16[1,192,2048]{2,1,0:T(8,128)(2,1)} %param.11) | copy-start | bytes 2359300
  131.4 19.5 %copy-start.5 = (f32[384,384]{1,0:T(8,128)S(1)}, f32[384,384]{1,0:T(8,128)}, u32[]{:S(2)}) copy-start(f32[384,384]{1,0:T(8,128)} %copy-done.4) | copy-start | bytes 1769476
  156.9 1.1 copy-start.3
  158.1 19.5 %all-to-all-start.6 = ((bf16[4,384,512]{2,1,0:T(8,128)(2,1)}), bf16[4,384,512]{2,1,0:T(8,128)(2,1)S(1)}, u32[]{:S(2)}, u32[]{:S(2)}) async-start(bf16[4,384,512]{2,1,0:T(8,128)(2,1)} %copy-done.3), calls=%async_computation.6 | async-start | bytes 3145728 | tf_op jit(solution)/shard_map/all_to_all | solution.py:43
  164.5 44.3 %collective-permute-start.2 = (bf16[384,2048]{1,0:T(8,128)(2,1)}, bf16[384,2048]{1,0:T(8,128)(2,1)}, u32[]{:S(2)}, u32[]{:S(2)}) collective-permute-start(bf16[384,2048]{1,0:T(8,128)(2,1)} %shard_map.82), channel_id=1, source_target_pairs={{0,4},{4,0},{8,12},{12,8},{16,20},{20,16},{24,28},{28,24},{32,36},... | collective-permute-start | bytes 4718600 | tf_op jit(solution)/shard_map/ppermute | solution.py:60
  205.3 11.5 %all-to-all-start.8 = ((bf16[4,128,512]{2,1,0:T(8,128)(2,1)}), bf16[4,128,512]{2,1,0:T(8,128)(2,1)S(1)}, u32[]{:S(2)}, u32[]{:S(2)}) async-start(bf16[4,128,512]{2,1,0:T(8,128)(2,1)} %shard_map.81), calls=%async_computation.8 | async-start | bytes 1048576 | tf_op jit(solution)/shard_map/all_to_all | solution.py:43

commit v5 on v3

--- a/solution.py
+++ b/solution.py
@@ -15,7 +15,6 @@
 VMEM_BYTES = 20 * 1024 * 1024
 VMEM = pl.BlockSpec(memory_space=pltpu.VMEM)
 SMEM = pl.BlockSpec(memory_space=pltpu.SMEM)
-ANY = pl.BlockSpec(memory_space=pl.ANY)
 
 
 def swish_parts(preact):
@@ -24,7 +23,8 @@
 
 
 def over_chips(rows):
-    count, cols = rows.shape
+    count = rows.shape[0]
+    cols = rows.size // count
     experts = lax.axis_size("expert")
     chips = experts // CORES
     moved = lax.all_to_all(
@@ -44,14 +44,6 @@
 
 def gather_dp(block):
     return over_dp(jnp.broadcast_to(block[None], (lax.axis_size("dp"),) + block.shape))
-
-
-def sum_dp(blocks):
-    moved = over_dp(blocks)
-    total = moved[0].astype(F32)
-    for q in range(1, moved.shape[0]):
-        total = total + moved[q].astype(F32)
-    return total.astype(BF)
 
 
 def swap_cores(value):
@@ -133,12 +125,13 @@
         out_ref[:, span] = t_mm(theirs, rows_ref[q]).astype(BF)
 
 
-def gradient_kernel(where_ref, rows_ref, pre_ref, lent_ref, out_ref):
+def gradient_kernel(where_ref, rows_ref, pre_ref, lent_ref, out_ref, done_ref):
     pre = pre_ref[...]
     owned = rows_of_core(where_ref, pre.shape, where_ref[0])
     mine = jnp.where(owned, pre, jnp.zeros_like(pre))
     for q, span in column_blocks(rows_ref):
         out_ref[:, span] = (t_mm(mine, rows_ref[q]) + lent_ref[:, span].astype(F32)).astype(BF)
+    done_ref[...] = jnp.zeros_like(done_ref)
 
 
 def places(slot_ref, slots):
@@ -169,19 +162,24 @@
     busiest = jnp.sum(jnp.where(counts == most, ids, 0.0), axis=0, keepdims=True)
     busiest_ref[...] = busiest.astype(jnp.int32)
     both = sum(places(slot_ref, out_ref.shape[0]))
-    out_ref[...] = mm(both, tokens_ref[...]).astype(BF)
+    out_ref[...] = mm(both, tokens_ref[...]).astype(BF).reshape(out_ref.shape)
 
 
 def combine_kernel(slot_ref, route_weight_ref, loss_weight_ref, returned_ref, out_ref):
     place = places(slot_ref, out_ref.shape[0])
     choices = len(place)
-    weights = [route_weight_ref[:, k : k + 1] for k in range(choices)]
+    scales = jnp.transpose(
+        jnp.concatenate(
+            [route_weight_ref[...], loss_weight_ref[...], jnp.zeros((7 - choices, route_weight_ref.shape[1]), F32)], axis=0
+        )
+    )
+    weights = [scales[:, k : k + 1] for k in range(choices)]
     returned = returned_ref[...]
     combined = sum(weights[k] * t_mm(place[k], returned) for k in range(choices))
-    loss = loss_weight_ref[...]
+    loss = scales[:, choices : choices + 1]
     out_ref[...] = sum(
         mm(place[k], (loss * weights[k] * combined).astype(BF)) for k in range(choices)
-    ).astype(BF)
+    ).astype(BF).reshape(out_ref.shape)
 
 
 def collect_kernel(slot_ref, returned_ref, out_ref):
@@ -191,19 +189,27 @@
         out_ref[q] = collected
 
 
-def join_kernel(parts_ref, _, out_ref):
+def join_kernel(parts_ref, done_ref, out_ref):
+    del done_ref
     for q, span in column_blocks(parts_ref):
         out_ref[:, span] = parts_ref[q]
 
 
-def call(kernel, outs, args, scalars=0, after=()):
+def sum_kernel(blocks_ref, out_ref):
+    total = blocks_ref[0].astype(F32)
+    for q in range(1, blocks_ref.shape[0]):
+        total = total + blocks_ref[q].astype(F32)
+    out_ref[...] = total.astype(BF).reshape(out_ref.shape)
+
+
+def call(kernel, outs, args, scalars=0):
     return pl.pallas_call(
         kernel,
         out_shape=outs,
-        in_specs=[SMEM] * scalars + [VMEM] * (len(args) - scalars) + [ANY] * len(after),
+        in_specs=[SMEM] * scalars + [VMEM] * (len(args) - scalars),
         out_specs=jax.tree.map(lambda _: VMEM, outs),
         compiler_params=pltpu.CompilerParams(vmem_limit_bytes=VMEM_BYTES),
-    )(*args, *after)
+    )(*args)
 
 
 def local(tokens, routes, route_weights, loss_weights, gate_up, down_weight):
@@ -221,12 +227,13 @@
     def out(*shape, dtype=BF):
         return jax.ShapeDtypeStruct(shape, dtype)
 
+    sent = out(slots, cols // LANES, LANES)
     mine = lax.dynamic_slice(
         tokens, (jnp.int32(0), lax.axis_index("dp") * cols), (local_tokens, cols)
     )
     slot, busiest, outgoing = call(
         functools.partial(send_kernel, experts),
-        [out(choices, local_tokens, dtype=jnp.int32), out(1, 1, dtype=jnp.int32), out(slots, cols)],
+        [out(choices, local_tokens, dtype=jnp.int32), out(1, 1, dtype=jnp.int32), sent],
         (routes.T, mine),
     )
     busiest = busiest[0, 0]
@@ -242,11 +249,11 @@
         (where, rows, *weights),
         scalars=1,
     )
-    returned = over_chips(sum_dp(partial))
+    returned = over_chips(call(sum_kernel, sent, (over_dp(partial),)))
     cot_send = call(
         combine_kernel,
-        out(slots, cols),
-        (slot, route_weights, loss_weights.reshape(local_tokens, 1), returned),
+        sent,
+        (slot, route_weights.T, loss_weights.reshape(1, local_tokens), returned),
     )
     cot = gather_dp(over_chips(cot_send))
     input_partial, grad_pre = call(
@@ -258,21 +265,18 @@
     lent = call(
         lent_gradient_kernel, out(2 * quarter, width), (where, rows, grad_pre), scalars=1
     )
-    gradient = call(
+    gradient, gradient_done = call(
         gradient_kernel,
-        out(2 * quarter, width),
+        [out(2 * quarter, width), out(8, LANES, dtype=F32)],
         (where, rows, grad_pre, swap_cores(lent)),
         scalars=1,
     )
-    returned_in = over_chips(sum_dp(input_partial))
+    returned_in = over_chips(call(sum_kernel, sent, (over_dp(input_partial),)))
     collected = call(
         collect_kernel, out(parts, local_tokens, cols), (slot, returned_in)
     )
     input_gradient = call(
-        join_kernel,
-        out(local_tokens, width),
-        (over_dp(collected),),
-        after=(gradient,),
+        join_kernel, out(local_tokens, width), (over_dp(collected), gradient_done)
     )
     return (input_gradient, gradient.reshape(1, 2, quarter, width))
 

time: 215 us -> 213 us (level)
  blocking collectives: 80.2 us -> 103 us
  waiting for transfers between devices: 60.3 us -> 45.8 us
  starting transfers between devices: 42 us -> 34.5 us
  local copies, waits for them, and re-layouts: 8.74 us -> 5.9 us
    all_to_all x2 -> x3, blocking collectives: 40.1 us -> 62.7 us  [over_chips(): lax.all_to_all(rows.reshape(chips, CORES * SLOTS, cols // LANES, LANES),...]
    all_to_all x2 -> x1, waiting for transfers between devices: 28.6 us -> 14.7 us  [over_chips(): lax.all_to_all(rows.reshape(chips, CORES * SLOTS, cols // LANES, LANES),...]
    all_to_all x2 -> x1, starting transfers between devices: 24 us -> 16.5 us  [over_chips(): lax.all_to_all(rows.reshape(chips, CORES * SLOTS, cols // LANES, LANES),...]
    pallas_call x8 -> x10, Pallas kernels: 19.5 us -> 20.8 us  [call(): pl.pallas_call(kernel, out_shape=outs, in_specs=[SMEM] * scalars + [VMEM]...]
    unnamed x23 -> x20, local copies, waits for them, and re-layouts: 4.62 us -> 4.5 us
  transfers between devices with their start and end apart: 8 -> 7, of which waited for: 6 -> 5; matrix products, arithmetic and copies ran while one was open for 2% -> 1% of each run, Pallas kernels for 3% -> 4%
where the time goes in v5:
time: 213 us; the launch traced here: 212 us
  blocking collectives  103 us (48%)
  waiting for transfers between devices  45.8 us (22%)
  starting transfers between devices  34.5 us (16%)
  Pallas kernels  20.8 us (10%)
  local copies, waits for them, and re-layouts  5.9 us (3%)
  between operations  2.2 us (1%)
    all_to_all x3, blocking collectives, over_chips(): lax.all_to_all(rows.reshape(chips, CORES * SLOTS, cols // LANES, LANES),...  62.7 us
    all_to_all x2, blocking collectives, over_dp(): return lax.all_to_all(blocks, 'dp', split_axis=0, concat_axis=0, tiled=True)  40 us
    all_to_all x3, waiting for transfers between devices, over_dp(): return lax.all_to_all(blocks, 'dp', split_axis=0, concat_axis=0, tiled=True)  30.2 us
    pallas_call x10, Pallas kernels, call(): pl.pallas_call(kernel, out_shape=outs, in_specs=[SMEM] * scalars + [VMEM]...  20.8 us
    all_to_all x1, starting transfers between devices, over_chips(): lax.all_to_all(rows.reshape(chips, CORES * SLOTS, cols // LANES, LANES),...  16.5 us
    all_to_all x1, waiting for transfers between devices, over_chips(): lax.all_to_all(rows.reshape(chips, CORES * SLOTS, cols // LANES, LANES),...  14.7 us
    all_to_all x3, starting transfers between devices, over_dp(): return lax.all_to_all(blocks, 'dp', split_axis=0, concat_axis=0, tiled=True)  12.2 us
    ppermute x3, starting transfers between devices, swap_cores(): return lax.ppermute(value, 'expert', [(i, i ^ 1) for i in range(experts)])  5.74 us
  transfers between devices with their start and end apart: 7, of which 5 were waited for; matrix products, arithmetic and copies ran while one was open for 1% of the time, Pallas kernels for 4%

profile of v5, /device:TPU:16, one launch (start us, length us, event | category | flops | bytes accessed | tf_op | source)
XLA Modules:
  0.0 212.0 jit_solution(13563844776561172430)
XLA Ops:
  0.6 0.0 copy-start
  0.6 1.0 copy-done
  1.7 0.0 copy-start.5
  1.7 0.7 copy-done.5
  2.4 1.2 shard_map.77
  3.5 16.5 %all-to-all-start = ((bf16[64,6,4,128]{3,2,1,0:T(4,128)(2,1)}), bf16[64,6,4,128]{3,2,1,0:T(4,128)(2,1)S(1)}, u32[]{:S(2)}, u32[]{:S(2)}) async-start(bf16[64,6,4,128]{3,2,1,0:T(4,128)(2,1)} %bitcast.6), calls=%async_computation | async-start | bytes 786432 | tf_op jit(solution)/shard_map/all_to_all | solution.py:30
  20.0 1.9 collective-permute-start
  22.0 14.7 %all-to-all-done = bf16[64,6,4,128]{3,2,1,0:T(4,128)(2,1)S(1)} async-done(((bf16[64,6,4,128]{3,2,1,0:T(4,128)(2,1)}), bf16[64,6,4,128]{3,2,1,0:T(4,128)(2,1)S(1)}, u32[]{:S(2)}, u32[]{:S(2)}) %all-to-all-start) | async-done | bytes 393248 | tf_op jit(solution)/shard_map/all_to_all | solution.py:30
  36.7 0.1 copy.19
  36.7 1.3 broadcast_in_dim.15
  38.0 4.4 %all-to-all-start.1 = ((bf16[4,384,512]{2,1,0:T(8,128)(2,1)}), bf16[4,384,512]{2,1,0:T(8,128)(2,1)S(1)}, u32[]{:S(2)}, u32[]{:S(2)}) async-start(bf16[4,384,512]{2,1,0:T(8,128)(2,1)} %broadcast_in_dim.15), calls=%async_computation.1 | async-start | bytes 3145728 | tf_op jit(solution)/shard_map/all_to_all | solution.py:42
  42.4 0.0 copy-done.3
  42.4 1.9 collective-permute-start.1
  45.7 0.1 pad_add_fusion.where_ref
  45.8 0.9 collective-permute-done.1.other_out_ref
  46.7 0.0 collective-permute-done.other_in_ref
  46.7 14.7 %all-to-all-done.1.rows_ref = bf16[4,384,512]{2,1,0:T(8,128)(2,1)S(1)} async-done(((bf16[4,384,512]{2,1,0:T(8,128)(2,1)}), bf16[4,384,512]{2,1,0:T(8,128)(2,1)S(1)}, u32[]{:S(2)}, u32[]{:S(2)}) %all-to-all-start.1) | async-done | bytes 1572896 | tf_op jit(solution)/shard_map/all_to_all | solution.py:42
  61.4 1.4 copy-done.1
  62.9 4.4 %shard_map.78 = (bf16[4,384,512]{2,1,0:T(8,128)(2,1)S(1)}, f32[384,384]{1,0:T(8,128)S(1)}) custom-call(s32[2]{0:T(128)S(1)} %pad_add_fusion.where_ref, bf16[4,384,512]{2,1,0:T(8,128)(2,1)S(1)} %all-to-all-done.1.rows_ref, bf16[384,2048]{1,0:T(8,128)(2,1)S(1)} %bitcast.34, bf16[192,2048]{1,0:T(8,128)(2,1)S(1)} %bitcast.37, ...), custom_call_target="tpu_custom_call" | custom-call | tf_op jit(solution)/shard_map/pallas_call | solution.py:206
  67.3 20.5 %all_to_all.45.blocks_ref = bf16[4,384,512]{2,1,0:T(8,128)(2,1)S(1)} all-to-all(bf16[4,384,512]{2,1,0:T(8,128)(2,1)S(1)} %get-tuple-element.14), channel_id=1, replica_groups=mesh['expert'=128,'dp'=4] {'dp'}, dimensions={0} | all-to-all | bytes 3145728 | tf_op jit(solution)/shard_map/all_to_all | solution.py:42
  87.8 0.2 shard_map.79
  88.0 21.5 %all_to_all.46 = bf16[64,6,4,128]{3,2,1,0:T(4,128)(2,1)S(1)} all-to-all(bf16[64,6,4,128]{3,2,1,0:T(4,128)(2,1)S(1)} %bitcast.42), channel_id=1, replica_groups={{0,8,16,24,32,40,48,56,64,72,80,88,96,104,112,120,128,136,144,152,160,1..., dimensions={0} | all-to-all | bytes 786432 | tf_op jit(solution)/shard_map/all_to_all | solution.py:30
  109.5 0.1 copy.18
  109.6 0.0 copy-done.6
  109.6 0.0 copy-done.7
  109.6 0.7 shard_map.80
  110.3 19.0 %all_to_all.47 = bf16[64,6,4,128]{3,2,1,0:T(4,128)(2,1)S(1)} all-to-all(bf16[64,6,4,128]{3,2,1,0:T(4,128)(2,1)S(1)} %bitcast.41), channel_id=1, replica_groups={{0,8,16,24,32,40,48,56,64,72,80,88,96,104,112,120,128,136,144,152,160,1..., dimensions={0} | all-to-all | bytes 786432 | tf_op jit(solution)/shard_map/all_to_all | solution.py:30
  129.4 0.1 copy.17
  129.4 0.1 broadcast_in_dim.17
  129.5 0.0 copy-start.2
  129.6 19.5 %all_to_all.48.cot_ref = bf16[4,384,512]{2,1,0:T(8,128)(2,1)S(1)} all-to-all(bf16[4,384,512]{2,1,0:T(8,128)(2,1)S(1)} %broadcast_in_dim.17), channel_id=1, replica_groups=mesh['expert'=128,'dp'=4] {'dp'}, dimensions={0} | all-to-all | bytes 3145728 | tf_op jit(solution)/shard_map/all_to_all | solution.py:42
  149.0 0.0 copy-done.2
  149.0 4.5 %shard_map.81 = (bf16[4,384,512]{2,1,0:T(8,128)(2,1)S(1)}, bf16[384,384]{1,0:T(8,128)(2,1)S(1)}) custom-call(s32[2]{0:T(128)S(1)} %pad_add_fusion.where_ref, bf16[4,384,512]{2,1,0:T(8,128)(2,1)S(1)} %all_to_all.48.cot_ref, f32[384,384]{1,0:T(8,128)S(1)} %get-tuple-element.15.proj_ref, bf16[384,2048]{1,0:T(8,128)(2,1)S(1)} %bitcast.35, ...), custom_call_target="tpu_custom_call" | custom-call | tf_op jit(solution)/shard_map/pallas_call | solution.py:206
  153.5 0.0 copy-start.4
  153.5 1.1 copy-done.4
  154.6 4.4 %all-to-all-start.6 = ((bf16[4,384,512]{2,1,0:T(8,128)(2,1)}), bf16[4,384,512]{2,1,0:T(8,128)(2,1)}, u32[]{:S(2)}, u32[]{:S(2)}) async-start(bf16[4,384,512]{2,1,0:T(8,128)(2,1)} %copy-done.4), calls=%async_computation.6 | async-start | bytes 3145728 | tf_op jit(solution)/shard_map/all_to_all | solution.py:42
  159.0 2.8 %shard_map.84 = bf16[384,2048]{1,0:T(8,128)(2,1)} custom-call(s32[2]{0:T(128)S(1)} %pad_add_fusion.where_ref, bf16[4,384,512]{2,1,0:T(8,128)(2,1)S(1)} %all-to-all-done.1.rows_ref, bf16[384,384]{1,0:T(8,128)(2,1)S(1)} %get-tuple-element.17.pre_ref), custom_call_target="tpu_custom_call" | custom-call | tf_op jit(solution)/shard_map/pallas_call | solution.py:206
  161.8 1.9 collective-permute-start.2
  163.7 11.1 %all-to-all-done.6.blocks_ref = bf16[4,384,512]{2,1,0:T(8,128)(2,1)} async-done(((bf16[4,384,512]{2,1,0:T(8,128)(2,1)}), bf16[4,384,512]{2,1,0:T(8,128)(2,1)}, u32[]{:S(2)}, u32[]{:S(2)}) %all-to-all-start.6) | async-done | bytes 1572896 | tf_op jit(solution)/shard_map/all_to_all | solution.py:42
  174.8 1.6 shard_map.82
  176.4 22.2 %all_to_all.49 = bf16[64,6,4,128]{3,2,1,0:T(4,128)(2,1)S(1)} all-to-all(bf16[64,6,4,128]{3,2,1,0:T(4,128)(2,1)S(1)} %bitcast.43), channel_id=1, replica_groups={{0,8,16,24,32,40,48,56,64,72,80,88,96,104,112,120,128,136,144,152,160,1..., dimensions={0} | all-to-all | bytes 786432 | tf_op jit(solution)/shard_map/all_to_all | solution.py:30
  198.6 0.1 copy.16
  198.6 1.1 shard_map.83
  199.7 3.5 %all-to-all-start.8 = ((bf16[4,128,512]{2,1,0:T(8,128)(2,1)}), bf16[4,128,512]{2,1,0:T(8,128)(2,1)S(1)}, u32[]{:S(2)}, u32[]{:S(2)}) async-start(bf16[4,128,512]{2,1,0:T(8,128)(2,1)} %shard_map.83), calls=%async_computation.8 | async-start | bytes 1048576 | tf_op jit(solution)/shard_map/all_to_all | solution.py:42
  203.2 0.0 collective-permute-done.2.lent_ref
  203.2 3.7 %shard_map.85 = (bf16[384,2048]{1,0:T(8,128)(2,1)}, f32[8,128]{1,0:T(8,128)S(1)}) custom-call(s32[2]{0:T(128)S(1)} %pad_add_fusion.where_ref, bf16[4,384,512]{2,1,0:T(8,128)(2,1)S(1)} %all-to-all-done.1.rows_ref, bf16[384,384]{1,0:T(8,128)(2,1)S(1)} %get-tuple-element.17.pre_ref, bf16[384,2048]{1,0:T(8,128)(2,1)} %collective-permute-done.2.lent_ref), custom_call_target="tpu_custom_call" | custom-call | tf_op jit(solution)/shard_map/pallas_call | solution.py:206
  206.8 4.4 %all-to-all-done.8.parts_ref = bf16[4,128,512]{2,1,0:T(8,128)(2,1)S(1)} async-done(((bf16[4,128,512]{2,1,0:T(8,128)(2,1)}), bf16[4,128,512]{2,1,0:T(8,128)(2,1)S(1)}, u32[]{:S(2)}, u32[]{:S(2)}) %all-to-all-start.8) | async-done | bytes 524320 | tf_op jit(solution)/shard_map/all_to_all | solution.py:42
  211.2 0.8 shard_map.86
  (5 shorter events, 0.0 us)
Async XLA Ops:
  0.6 1.0 copy-start
  1.7 0.7 copy-start.5
  3.5 33.1 %all-to-all-start = ((bf16[64,6,4,128]{3,2,1,0:T(4,128)(2,1)}), bf16[64,6,4,128]{3,2,1,0:T(4,128)(2,1)S(1)}, u32[]{:S(2)}, u32[]{:S(2)}) async-start(bf16[64,6,4,128]{3,2,1,0:T(4,128)(2,1)} %bitcast.6), calls=%async_computation | async-start | bytes 786432 | tf_op jit(solution)/shard_map/all_to_all | solution.py:30
  20.0 26.7 %collective-permute-start = (bf16[384,2048]{1,0:T(8,128)(2,1)}, bf16[384,2048]{1,0:T(8,128)(2,1)}, u32[]{:S(2)}, u32[]{:S(2)}) collective-permute-start(bf16[384,2048]{1,0:T(8,128)(2,1)} %bitcast.33), channel_id=1, source_target_pairs={{0,4},{4,0},{8,12},{12,8},{16,20},{20,16},{24,28},{28,24},{32,36},... | collective-permute-start | bytes 4718600 | tf_op jit(solution)/shard_map/ppermute | solution.py:51
  38.0 4.4 %copy-start.3 = (bf16[1,192,2048]{2,1,0:T(8,128)(2,1)S(1)}, bf16[1,192,2048]{2,1,0:T(8,128)(2,1)}, u32[]{:S(2)}) copy-start(bf16[1,192,2048]{2,1,0:T(8,128)(2,1)} %param.11) | copy-start | bytes 2359300
  38.0 23.4 %all-to-all-start.1 = ((bf16[4,384,512]{2,1,0:T(8,128)(2,1)}), bf16[4,384,512]{2,1,0:T(8,128)(2,1)S(1)}, u32[]{:S(2)}, u32[]{:S(2)}) async-start(bf16[4,384,512]{2,1,0:T(8,128)(2,1)} %broadcast_in_dim.15), calls=%async_computation.1 | async-start | bytes 3145728 | tf_op jit(solution)/shard_map/all_to_all | solution.py:42
  42.4 4.3 %collective-permute-start.1 = (bf16[192,2048]{1,0:T(8,128)(2,1)S(1)}, bf16[192,2048]{1,0:T(8,128)(2,1)}, u32[]{:S(2)}, u32[]{:S(2)}) collective-permute-start(bf16[192,2048]{1,0:T(8,128)(2,1)S(1)} %bitcast.36), channel_id=1, source_target_pairs={{0,4},{4,0},{8,12},{12,8},{16,20},{20,16},{24,28},{28,24},{32,36},... | collective-permute-start | bytes 2359304 | tf_op jit(solution)/shard_map/ppermute | solution.py:51
  61.4 1.4 copy-start.1
  87.8 21.8 %copy-start.6 = (f32[128,2]{0,1:T(2,128)S(1)}, f32[128,2]{0,1:T(2,128)}, u32[]{:S(2)}) copy-start(f32[128,2]{0,1:T(2,128)} %param.8) | copy-start | bytes 3076
  87.8 21.8 %copy-start.7 = (f32[128]{0:T(128)S(1)}, f32[128]{0:T(128)}, u32[]{:S(2)}) copy-start(f32[128]{0:T(128)} %param.9) | copy-start | bytes 1540
  129.5 19.5 %copy-start.2 = (bf16[1,2,192,2048]{3,2,1,0:T(8,128)(2,1)S(1)}, bf16[1,2,192,2048]{3,2,1,0:T(8,128)(2,1)}, u32[]{:S(2)}) copy-start(bf16[1,2,192,2048]{3,2,1,0:T(8,128)(2,1)} %param.10) | copy-start | bytes 4718596
  153.5 1.1 copy-start.4
  154.6 20.1 %all-to-all-start.6 = ((bf16[4,384,512]{2,1,0:T(8,128)(2,1)}), bf16[4,384,512]{2,1,0:T(8,128)(2,1)}, u32[]{:S(2)}, u32[]{:S(2)}) async-start(bf16[4,384,512]{2,1,0:T(8,128)(2,1)} %copy-done.4), calls=%async_computation.6 | async-start | bytes 3145728 | tf_op jit(solution)/shard_map/all_to_all | solution.py:42
  161.8 41.4 %collective-permute-start.2 = (bf16[384,2048]{1,0:T(8,128)(2,1)}, bf16[384,2048]{1,0:T(8,128)(2,1)}, u32[]{:S(2)}, u32[]{:S(2)}) collective-permute-start(bf16[384,2048]{1,0:T(8,128)(2,1)} %shard_map.84), channel_id=1, source_target_pairs={{0,4},{4,0},{8,12},{12,8},{16,20},{20,16},{24,28},{28,24},{32,36},... | collective-permute-start | bytes 4718600 | tf_op jit(solution)/shard_map/ppermute | solution.py:51
  199.7 11.5 %all-to-all-start.8 = ((bf16[4,128,512]{2,1,0:T(8,128)(2,1)}), bf16[4,128,512]{2,1,0:T(8,128)(2,1)S(1)}, u32[]{:S(2)}, u32[]{:S(2)}) async-start(bf16[4,128,512]{2,1,0:T(8,128)(2,1)} %shard_map.83), calls=%async_computation.8 | async-start | bytes 1048576 | tf_op jit(solution)/shard_map/all_to_all | solution.py:42

commit v6 on v5

--- a/solution.py
+++ b/solution.py
@@ -182,15 +182,15 @@
     ).astype(BF).reshape(out_ref.shape)
 
 
-def collect_kernel(slot_ref, returned_ref, out_ref):
+def collect_kernel(slot_ref, returned_ref, done_ref, out_ref):
+    del done_ref
     both = sum(places(slot_ref, returned_ref.shape[0]))
     collected = t_mm(both, returned_ref[...]).astype(BF)
     for q in range(out_ref.shape[0]):
         out_ref[q] = collected
 
 
-def join_kernel(parts_ref, done_ref, out_ref):
-    del done_ref
+def join_kernel(parts_ref, out_ref):
     for q, span in column_blocks(parts_ref):
         out_ref[:, span] = parts_ref[q]
 
@@ -273,10 +273,10 @@
     )
     returned_in = over_chips(call(sum_kernel, sent, (over_dp(input_partial),)))
     collected = call(
-        collect_kernel, out(parts, local_tokens, cols), (slot, returned_in)
+        collect_kernel, out(parts, local_tokens, cols), (slot, returned_in, gradient_done)
     )
     input_gradient = call(
-        join_kernel, out(local_tokens, width), (over_dp(collected), gradient_done)
+        join_kernel, out(local_tokens, width), (over_dp(collected),)
     )
     return (input_gradient, gradient.reshape(1, 2, quarter, width))
 

time: 213 us -> 212 us (level)
  blocking collectives: 103 us -> 91 us
  waiting for transfers between devices: 45.8 us -> 51.6 us
  starting transfers between devices: 34.5 us -> 39.7 us
    all_to_all x3 -> x2, blocking collectives: 62.7 us -> 40.6 us  [over_chips(): lax.all_to_all(rows.reshape(chips, CORES * SLOTS, cols // LANES, LANES),...]
    all_to_all x2 -> x3, blocking collectives: 40 us -> 50.5 us  [over_dp(): return lax.all_to_all(blocks, 'dp', split_axis=0, concat_axis=0, tiled=True)]
    all_to_all x1 -> x2, waiting for transfers between devices: 14.7 us -> 25 us  [over_chips(): lax.all_to_all(rows.reshape(chips, CORES * SLOTS, cols // LANES, LANES),...]
    all_to_all x1 -> x2, starting transfers between devices: 16.5 us -> 25.2 us  [over_chips(): lax.all_to_all(rows.reshape(chips, CORES * SLOTS, cols // LANES, LANES),...]
    all_to_all x3 -> x2, waiting for transfers between devices: 30.2 us -> 25.8 us  [over_dp(): return lax.all_to_all(blocks, 'dp', split_axis=0, concat_axis=0, tiled=True)]
    all_to_all x3 -> x2, starting transfers between devices: 12.2 us -> 8.77 us  [over_dp(): return lax.all_to_all(blocks, 'dp', split_axis=0, concat_axis=0, tiled=True)]
where the time goes in v6:
time: 212 us; the launch traced here: 211 us
  blocking collectives  91 us (43%)
  waiting for transfers between devices  51.6 us (24%)
  starting transfers between devices  39.7 us (19%)
  Pallas kernels  20.8 us (10%)
  local copies, waits for them, and re-layouts  5.9 us (3%)
  between operations  2.2 us (1%)
    all_to_all x3, blocking collectives, over_dp(): return lax.all_to_all(blocks, 'dp', split_axis=0, concat_axis=0, tiled=True)  50.5 us
    all_to_all x2, blocking collectives, over_chips(): lax.all_to_all(rows.reshape(chips, CORES * SLOTS, cols // LANES, LANES),...  40.6 us
    all_to_all x2, waiting for transfers between devices, over_dp(): return lax.all_to_all(blocks, 'dp', split_axis=0, concat_axis=0, tiled=True)  25.8 us
    all_to_all x2, starting transfers between devices, over_chips(): lax.all_to_all(rows.reshape(chips, CORES * SLOTS, cols // LANES, LANES),...  25.2 us
    all_to_all x2, waiting for transfers between devices, over_chips(): lax.all_to_all(rows.reshape(chips, CORES * SLOTS, cols // LANES, LANES),...  25 us
    pallas_call x10, Pallas kernels, call(): pl.pallas_call(kernel, out_shape=outs, in_specs=[SMEM] * scalars + [VMEM]...  20.8 us
    all_to_all x2, starting transfers between devices, over_dp(): return lax.all_to_all(blocks, 'dp', split_axis=0, concat_axis=0, tiled=True)  8.77 us
    ppermute x3, starting transfers between devices, swap_cores(): return lax.ppermute(value, 'expert', [(i, i ^ 1) for i in range(experts)])  5.74 us
  transfers between devices with their start and end apart: 7, of which 5 were waited for; matrix products, arithmetic and copies ran while one was open for 1% of the time, Pallas kernels for 4%

profile of v6, /device:TPU:16, one launch (start us, length us, event | category | flops | bytes accessed | tf_op | source)
XLA Modules:
  0.0 211.4 jit_solution(1483675743386406654)
XLA Ops:
  0.6 0.0 copy-start
  0.6 1.0 copy-done
  1.7 0.0 copy-start.5
  1.7 0.7 copy-done.5
  2.4 1.2 shard_map.77
  3.5 16.5 %all-to-all-start = ((bf16[64,6,4,128]{3,2,1,0:T(4,128)(2,1)}), bf16[64,6,4,128]{3,2,1,0:T(4,128)(2,1)S(1)}, u32[]{:S(2)}, u32[]{:S(2)}) async-start(bf16[64,6,4,128]{3,2,1,0:T(4,128)(2,1)} %bitcast.6), calls=%async_computation | async-start | bytes 786432 | tf_op jit(solution)/shard_map/all_to_all | solution.py:30
  20.0 1.9 collective-permute-start
  22.0 14.7 %all-to-all-done = bf16[64,6,4,128]{3,2,1,0:T(4,128)(2,1)S(1)} async-done(((bf16[64,6,4,128]{3,2,1,0:T(4,128)(2,1)}), bf16[64,6,4,128]{3,2,1,0:T(4,128)(2,1)S(1)}, u32[]{:S(2)}, u32[]{:S(2)}) %all-to-all-start) | async-done | bytes 393248 | tf_op jit(solution)/shard_map/all_to_all | solution.py:30
  36.7 0.1 copy.19
  36.7 1.3 broadcast_in_dim.15
  38.0 4.4 %all-to-all-start.1 = ((bf16[4,384,512]{2,1,0:T(8,128)(2,1)}), bf16[4,384,512]{2,1,0:T(8,128)(2,1)S(1)}, u32[]{:S(2)}, u32[]{:S(2)}) async-start(bf16[4,384,512]{2,1,0:T(8,128)(2,1)} %broadcast_in_dim.15), calls=%async_computation.1 | async-start | bytes 3145728 | tf_op jit(solution)/shard_map/all_to_all | solution.py:42
  42.4 0.0 copy-done.3
  42.4 1.9 collective-permute-start.1
  45.7 0.1 pad_add_fusion.where_ref
  45.8 0.9 collective-permute-done.1.other_out_ref
  46.7 0.0 collective-permute-done.other_in_ref
  46.7 14.7 %all-to-all-done.1.rows_ref = bf16[4,384,512]{2,1,0:T(8,128)(2,1)S(1)} async-done(((bf16[4,384,512]{2,1,0:T(8,128)(2,1)}), bf16[4,384,512]{2,1,0:T(8,128)(2,1)S(1)}, u32[]{:S(2)}, u32[]{:S(2)}) %all-to-all-start.1) | async-done | bytes 1572896 | tf_op jit(solution)/shard_map/all_to_all | solution.py:42
  61.4 1.4 copy-done.1
  62.9 4.4 %shard_map.78 = (bf16[4,384,512]{2,1,0:T(8,128)(2,1)S(1)}, f32[384,384]{1,0:T(8,128)S(1)}) custom-call(s32[2]{0:T(128)S(1)} %pad_add_fusion.where_ref, bf16[4,384,512]{2,1,0:T(8,128)(2,1)S(1)} %all-to-all-done.1.rows_ref, bf16[384,2048]{1,0:T(8,128)(2,1)S(1)} %bitcast.34, bf16[192,2048]{1,0:T(8,128)(2,1)S(1)} %bitcast.37, ...), custom_call_target="tpu_custom_call" | custom-call | tf_op jit(solution)/shard_map/pallas_call | solution.py:206
  67.3 20.5 %all_to_all.45.blocks_ref = bf16[4,384,512]{2,1,0:T(8,128)(2,1)S(1)} all-to-all(bf16[4,384,512]{2,1,0:T(8,128)(2,1)S(1)} %get-tuple-element.14), channel_id=1, replica_groups=mesh['expert'=128,'dp'=4] {'dp'}, dimensions={0} | all-to-all | bytes 3145728 | tf_op jit(solution)/shard_map/all_to_all | solution.py:42
  87.8 0.2 shard_map.79
  88.0 21.5 %all_to_all.46 = bf16[64,6,4,128]{3,2,1,0:T(4,128)(2,1)S(1)} all-to-all(bf16[64,6,4,128]{3,2,1,0:T(4,128)(2,1)S(1)} %bitcast.42), channel_id=1, replica_groups={{0,8,16,24,32,40,48,56,64,72,80,88,96,104,112,120,128,136,144,152,160,1..., dimensions={0} | all-to-all | bytes 786432 | tf_op jit(solution)/shard_map/all_to_all | solution.py:30
  109.5 0.1 copy.18
  109.6 0.0 copy-done.6
  109.6 0.0 copy-done.7
  109.6 0.7 shard_map.80
  110.3 19.1 %all_to_all.47 = bf16[64,6,4,128]{3,2,1,0:T(4,128)(2,1)S(1)} all-to-all(bf16[64,6,4,128]{3,2,1,0:T(4,128)(2,1)S(1)} %bitcast.41), channel_id=1, replica_groups={{0,8,16,24,32,40,48,56,64,72,80,88,96,104,112,120,128,136,144,152,160,1..., dimensions={0} | all-to-all | bytes 786432 | tf_op jit(solution)/shard_map/all_to_all | solution.py:30
  129.4 0.1 copy.17
  129.4 0.1 broadcast_in_dim.17
  129.6 0.0 copy-start.2
  129.6 19.4 %all_to_all.48.cot_ref = bf16[4,384,512]{2,1,0:T(8,128)(2,1)S(1)} all-to-all(bf16[4,384,512]{2,1,0:T(8,128)(2,1)S(1)} %broadcast_in_dim.17), channel_id=1, replica_groups=mesh['expert'=128,'dp'=4] {'dp'}, dimensions={0} | all-to-all | bytes 3145728 | tf_op jit(solution)/shard_map/all_to_all | solution.py:42
  149.0 0.0 copy-done.2
  149.0 4.5 %shard_map.81 = (bf16[4,384,512]{2,1,0:T(8,128)(2,1)S(1)}, bf16[384,384]{1,0:T(8,128)(2,1)S(1)}) custom-call(s32[2]{0:T(128)S(1)} %pad_add_fusion.where_ref, bf16[4,384,512]{2,1,0:T(8,128)(2,1)S(1)} %all_to_all.48.cot_ref, f32[384,384]{1,0:T(8,128)S(1)} %get-tuple-element.15.proj_ref, bf16[384,2048]{1,0:T(8,128)(2,1)S(1)} %bitcast.35, ...), custom_call_target="tpu_custom_call" | custom-call | tf_op jit(solution)/shard_map/pallas_call | solution.py:206
  153.5 0.0 copy-start.4
  153.5 1.1 copy-done.4
  154.7 4.4 %all-to-all-start.6 = ((bf16[4,384,512]{2,1,0:T(8,128)(2,1)}), bf16[4,384,512]{2,1,0:T(8,128)(2,1)}, u32[]{:S(2)}, u32[]{:S(2)}) async-start(bf16[4,384,512]{2,1,0:T(8,128)(2,1)} %copy-done.4), calls=%async_computation.6 | async-start | bytes 3145728 | tf_op jit(solution)/shard_map/all_to_all | solution.py:42
  159.0 2.8 %shard_map.83 = bf16[384,2048]{1,0:T(8,128)(2,1)} custom-call(s32[2]{0:T(128)S(1)} %pad_add_fusion.where_ref, bf16[4,384,512]{2,1,0:T(8,128)(2,1)S(1)} %all-to-all-done.1.rows_ref, bf16[384,384]{1,0:T(8,128)(2,1)S(1)} %get-tuple-element.17.pre_ref), custom_call_target="tpu_custom_call" | custom-call | tf_op jit(solution)/shard_map/pallas_call | solution.py:206
  161.8 1.9 collective-permute-start.2
  163.7 11.1 %all-to-all-done.6.blocks_ref = bf16[4,384,512]{2,1,0:T(8,128)(2,1)} async-done(((bf16[4,384,512]{2,1,0:T(8,128)(2,1)}), bf16[4,384,512]{2,1,0:T(8,128)(2,1)}, u32[]{:S(2)}, u32[]{:S(2)}) %all-to-all-start.6) | async-done | bytes 1572896 | tf_op jit(solution)/shard_map/all_to_all | solution.py:42
  174.8 2.3 %shard_map.82 = bf16[384,4,128]{2,1,0:T(4,128)(2,1)} custom-call(bf16[4,384,512]{2,1,0:T(8,128)(2,1)} %all-to-all-done.6.blocks_ref), custom_call_target="tpu_custom_call" | custom-call | tf_op jit(solution)/shard_map/pallas_call | solution.py:206
  177.1 8.7 %all-to-all-start.7 = ((bf16[64,6,4,128]{3,2,1,0:T(4,128)(2,1)}), bf16[64,6,4,128]{3,2,1,0:T(4,128)(2,1)S(1)}, u32[]{:S(2)}, u32[]{:S(2)}) async-start(bf16[64,6,4,128]{3,2,1,0:T(4,128)(2,1)} %bitcast.11), calls=%async_computation.7 | async-start | bytes 786432 | tf_op jit(solution)/shard_map/all_to_all | solution.py:30
  185.8 0.0 collective-permute-done.2.lent_ref
  185.8 3.6 %shard_map.84 = (bf16[384,2048]{1,0:T(8,128)(2,1)}, f32[8,128]{1,0:T(8,128)S(1)}) custom-call(s32[2]{0:T(128)S(1)} %pad_add_fusion.where_ref, bf16[4,384,512]{2,1,0:T(8,128)(2,1)S(1)} %all-to-all-done.1.rows_ref, bf16[384,384]{1,0:T(8,128)(2,1)S(1)} %get-tuple-element.17.pre_ref, bf16[384,2048]{1,0:T(8,128)(2,1)} %collective-permute-done.2.lent_ref), custom_call_target="tpu_custom_call" | custom-call | tf_op jit(solution)/shard_map/pallas_call | solution.py:206
  189.5 10.2 %all-to-all-done.7 = bf16[64,6,4,128]{3,2,1,0:T(4,128)(2,1)S(1)} async-done(((bf16[64,6,4,128]{3,2,1,0:T(4,128)(2,1)}), bf16[64,6,4,128]{3,2,1,0:T(4,128)(2,1)S(1)}, u32[]{:S(2)}, u32[]{:S(2)}) %all-to-all-start.7) | async-done | bytes 393248 | tf_op jit(solution)/shard_map/all_to_all | solution.py:30
  199.7 0.1 copy.16
  199.8 0.3 shard_map.85
  200.1 10.5 %all_to_all.49.parts_ref = bf16[4,128,512]{2,1,0:T(8,128)(2,1)S(1)} all-to-all(bf16[4,128,512]{2,1,0:T(8,128)(2,1)S(1)} %shard_map.85), channel_id=1, replica_groups=mesh['expert'=128,'dp'=4] {'dp'}, dimensions={0} | all-to-all | bytes 1048576 | tf_op jit(solution)/shard_map/all_to_all | solution.py:42
  210.5 0.8 shard_map.86
  (5 shorter events, 0.0 us)
Async XLA Ops:
  0.6 1.0 copy-start
  1.7 0.7 copy-start.5
  3.5 33.1 %all-to-all-start = ((bf16[64,6,4,128]{3,2,1,0:T(4,128)(2,1)}), bf16[64,6,4,128]{3,2,1,0:T(4,128)(2,1)S(1)}, u32[]{:S(2)}, u32[]{:S(2)}) async-start(bf16[64,6,4,128]{3,2,1,0:T(4,128)(2,1)} %bitcast.6), calls=%async_computation | async-start | bytes 786432 | tf_op jit(solution)/shard_map/all_to_all | solution.py:30
  20.0 26.7 %collective-permute-start = (bf16[384,2048]{1,0:T(8,128)(2,1)}, bf16[384,2048]{1,0:T(8,128)(2,1)}, u32[]{:S(2)}, u32[]{:S(2)}) collective-permute-start(bf16[384,2048]{1,0:T(8,128)(2,1)} %bitcast.33), channel_id=1, source_target_pairs={{0,4},{4,0},{8,12},{12,8},{16,20},{20,16},{24,28},{28,24},{32,36},... | collective-permute-start | bytes 4718600 | tf_op jit(solution)/shard_map/ppermute | solution.py:51
  38.0 4.4 %copy-start.3 = (bf16[1,192,2048]{2,1,0:T(8,128)(2,1)S(1)}, bf16[1,192,2048]{2,1,0:T(8,128)(2,1)}, u32[]{:S(2)}) copy-start(bf16[1,192,2048]{2,1,0:T(8,128)(2,1)} %param.11) | copy-start | bytes 2359300
  38.0 23.4 %all-to-all-start.1 = ((bf16[4,384,512]{2,1,0:T(8,128)(2,1)}), bf16[4,384,512]{2,1,0:T(8,128)(2,1)S(1)}, u32[]{:S(2)}, u32[]{:S(2)}) async-start(bf16[4,384,512]{2,1,0:T(8,128)(2,1)} %broadcast_in_dim.15), calls=%async_computation.1 | async-start | bytes 3145728 | tf_op jit(solution)/shard_map/all_to_all | solution.py:42
  42.4 4.3 %collective-permute-start.1 = (bf16[192,2048]{1,0:T(8,128)(2,1)S(1)}, bf16[192,2048]{1,0:T(8,128)(2,1)}, u32[]{:S(2)}, u32[]{:S(2)}) collective-permute-start(bf16[192,2048]{1,0:T(8,128)(2,1)S(1)} %bitcast.36), channel_id=1, source_target_pairs={{0,4},{4,0},{8,12},{12,8},{16,20},{20,16},{24,28},{28,24},{32,36},... | collective-permute-start | bytes 2359304 | tf_op jit(solution)/shard_map/ppermute | solution.py:51
  61.4 1.4 copy-start.1
  87.8 21.8 %copy-start.6 = (f32[128,2]{0,1:T(2,128)S(1)}, f32[128,2]{0,1:T(2,128)}, u32[]{:S(2)}) copy-start(f32[128,2]{0,1:T(2,128)} %param.8) | copy-start | bytes 3076
  87.8 21.8 %copy-start.7 = (f32[128]{0:T(128)S(1)}, f32[128]{0:T(128)}, u32[]{:S(2)}) copy-start(f32[128]{0:T(128)} %param.9) | copy-start | bytes 1540
  129.6 19.5 %copy-start.2 = (bf16[1,2,192,2048]{3,2,1,0:T(8,128)(2,1)S(1)}, bf16[1,2,192,2048]{3,2,1,0:T(8,128)(2,1)}, u32[]{:S(2)}) copy-start(bf16[1,2,192,2048]{3,2,1,0:T(8,128)(2,1)} %param.10) | copy-start | bytes 4718596
  153.5 1.1 copy-start.4
  154.7 20.1 %all-to-all-start.6 = ((bf16[4,384,512]{2,1,0:T(8,128)(2,1)}), bf16[4,384,512]{2,1,0:T(8,128)(2,1)}, u32[]{:S(2)}, u32[]{:S(2)}) async-start(bf16[4,384,512]{2,1,0:T(8,128)(2,1)} %copy-done.4), calls=%async_computation.6 | async-start | bytes 3145728 | tf_op jit(solution)/shard_map/all_to_all | solution.py:42
  161.8 24.0 %collective-permute-start.2 = (bf16[384,2048]{1,0:T(8,128)(2,1)}, bf16[384,2048]{1,0:T(8,128)(2,1)}, u32[]{:S(2)}, u32[]{:S(2)}) collective-permute-start(bf16[384,2048]{1,0:T(8,128)(2,1)} %shard_map.83), channel_id=1, source_target_pairs={{0,4},{4,0},{8,12},{12,8},{16,20},{20,16},{24,28},{28,24},{32,36},... | collective-permute-start | bytes 4718600 | tf_op jit(solution)/shard_map/ppermute | solution.py:51
  177.1 22.6 %all-to-all-start.7 = ((bf16[64,6,4,128]{3,2,1,0:T(4,128)(2,1)}), bf16[64,6,4,128]{3,2,1,0:T(4,128)(2,1)S(1)}, u32[]{:S(2)}, u32[]{:S(2)}) async-start(bf16[64,6,4,128]{3,2,1,0:T(4,128)(2,1)} %bitcast.11), calls=%async_computation.7 | async-start | bytes 786432 | tf_op jit(solution)/shard_map/all_to_all | solution.py:30

commit v7 on v6

--- a/solution.py
+++ b/solution.py
@@ -44,6 +44,14 @@
 
 def gather_dp(block):
     return over_dp(jnp.broadcast_to(block[None], (lax.axis_size("dp"),) + block.shape))
+
+
+def sum_dp(blocks):
+    moved = over_dp(blocks)
+    total = moved[0].astype(F32)
+    for q in range(1, moved.shape[0]):
+        total = total + moved[q].astype(F32)
+    return total.astype(BF)
 
 
 def swap_cores(value):
@@ -271,7 +279,7 @@
         (where, rows, grad_pre, swap_cores(lent)),
         scalars=1,
     )
-    returned_in = over_chips(call(sum_kernel, sent, (over_dp(input_partial),)))
+    returned_in = over_chips(sum_dp(input_partial))
     collected = call(
         collect_kernel, out(parts, local_tokens, cols), (slot, returned_in, gradient_done)
     )

time: 212 us -> 212 us (level)
  Pallas kernels: 20.8 us -> 18.5 us
    pallas_call x10 -> x9, Pallas kernels: 20.8 us -> 18.5 us  [call(): pl.pallas_call(kernel, out_shape=outs, in_specs=[SMEM] * scalars + [VMEM]...]
  transfers between devices with their start and end apart: 7 -> 7, of which waited for: 5 -> 5; matrix products, arithmetic and copies ran while one was open for 1% -> 2% of each run, Pallas kernels for 4% -> 3%
where the time goes in v7:
time: 212 us; the launch traced here: 211 us
  blocking collectives  91 us (43%)
  waiting for transfers between devices  51.6 us (24%)
  starting transfers between devices  39.7 us (19%)
  Pallas kernels  18.5 us (9%)
  local copies, waits for them, and re-layouts  6.73 us (3%)
  between operations  2.21 us (1%)
    all_to_all x3, blocking collectives, over_dp(): return lax.all_to_all(blocks, 'dp', split_axis=0, concat_axis=0, tiled=True)  50.5 us
    all_to_all x2, blocking collectives, over_chips(): lax.all_to_all(rows.reshape(chips, CORES * SLOTS, cols // LANES, LANES),...  40.6 us
    all_to_all x2, waiting for transfers between devices, over_dp(): return lax.all_to_all(blocks, 'dp', split_axis=0, concat_axis=0, tiled=True)  25.8 us
    all_to_all x2, starting transfers between devices, over_chips(): lax.all_to_all(rows.reshape(chips, CORES * SLOTS, cols // LANES, LANES),...  25.2 us
    all_to_all x2, waiting for transfers between devices, over_chips(): lax.all_to_all(rows.reshape(chips, CORES * SLOTS, cols // LANES, LANES),...  24.9 us
    pallas_call x9, Pallas kernels, call(): pl.pallas_call(kernel, out_shape=outs, in_specs=[SMEM] * scalars + [VMEM]...  18.5 us
    all_to_all x2, starting transfers between devices, over_dp(): return lax.all_to_all(blocks, 'dp', split_axis=0, concat_axis=0, tiled=True)  8.77 us
    ppermute x3, starting transfers between devices, swap_cores(): return lax.ppermute(value, 'expert', [(i, i ^ 1) for i in range(experts)])  5.74 us
  transfers between devices with their start and end apart: 7, of which 5 were waited for; matrix products, arithmetic and copies ran while one was open for 2% of the time, Pallas kernels for 3%

profile of v7, /device:TPU:16, one launch (start us, length us, event | category | flops | bytes accessed | tf_op | source)
XLA Modules:
  0.0 211.4 jit_solution(7308698083771286896)
XLA Ops:
  0.6 0.0 copy-start
  0.6 1.0 copy-done
  1.7 0.0 copy-start.5
  1.7 0.7 copy-done.5
  2.4 1.2 shard_map.77
  3.5 16.5 %all-to-all-start = ((bf16[64,6,4,128]{3,2,1,0:T(4,128)(2,1)}), bf16[64,6,4,128]{3,2,1,0:T(4,128)(2,1)S(1)}, u32[]{:S(2)}, u32[]{:S(2)}) async-start(bf16[64,6,4,128]{3,2,1,0:T(4,128)(2,1)} %bitcast.6), calls=%async_computation | async-start | bytes 786432 | tf_op jit(solution)/shard_map/all_to_all | solution.py:30
  20.0 1.9 collective-permute-start
  22.0 14.7 %all-to-all-done = bf16[64,6,4,128]{3,2,1,0:T(4,128)(2,1)S(1)} async-done(((bf16[64,6,4,128]{3,2,1,0:T(4,128)(2,1)}), bf16[64,6,4,128]{3,2,1,0:T(4,128)(2,1)S(1)}, u32[]{:S(2)}, u32[]{:S(2)}) %all-to-all-start) | async-done | bytes 393248 | tf_op jit(solution)/shard_map/all_to_all | solution.py:30
  36.7 0.1 copy.19
  36.7 1.3 broadcast_in_dim.15
  38.0 4.4 %all-to-all-start.1 = ((bf16[4,384,512]{2,1,0:T(8,128)(2,1)}), bf16[4,384,512]{2,1,0:T(8,128)(2,1)S(1)}, u32[]{:S(2)}, u32[]{:S(2)}) async-start(bf16[4,384,512]{2,1,0:T(8,128)(2,1)} %broadcast_in_dim.15), calls=%async_computation.1 | async-start | bytes 3145728 | tf_op jit(solution)/shard_map/all_to_all | solution.py:42
  42.4 0.0 copy-done.3
  42.4 1.9 collective-permute-start.1
  45.7 0.1 pad_add_fusion.where_ref
  45.8 0.9 collective-permute-done.1.other_out_ref
  46.7 0.0 collective-permute-done.other_in_ref
  46.7 14.7 %all-to-all-done.1.rows_ref = bf16[4,384,512]{2,1,0:T(8,128)(2,1)S(1)} async-done(((bf16[4,384,512]{2,1,0:T(8,128)(2,1)}), bf16[4,384,512]{2,1,0:T(8,128)(2,1)S(1)}, u32[]{:S(2)}, u32[]{:S(2)}) %all-to-all-start.1) | async-done | bytes 1572896 | tf_op jit(solution)/shard_map/all_to_all | solution.py:42
  61.4 1.4 copy-done.1
  62.9 4.4 %shard_map.78 = (bf16[4,384,512]{2,1,0:T(8,128)(2,1)S(1)}, f32[384,384]{1,0:T(8,128)S(1)}) custom-call(s32[2]{0:T(128)S(1)} %pad_add_fusion.where_ref, bf16[4,384,512]{2,1,0:T(8,128)(2,1)S(1)} %all-to-all-done.1.rows_ref, bf16[384,2048]{1,0:T(8,128)(2,1)S(1)} %bitcast.33, bf16[192,2048]{1,0:T(8,128)(2,1)S(1)} %bitcast.36, ...), custom_call_target="tpu_custom_call" | custom-call | tf_op jit(solution)/shard_map/pallas_call | solution.py:214
  67.3 20.5 %all_to_all.45.blocks_ref = bf16[4,384,512]{2,1,0:T(8,128)(2,1)S(1)} all-to-all(bf16[4,384,512]{2,1,0:T(8,128)(2,1)S(1)} %get-tuple-element.14), channel_id=1, replica_groups=mesh['expert'=128,'dp'=4] {'dp'}, dimensions={0} | all-to-all | bytes 3145728 | tf_op jit(solution)/shard_map/all_to_all | solution.py:42
  87.8 0.2 shard_map.79
  88.0 21.5 %all_to_all.46 = bf16[64,6,4,128]{3,2,1,0:T(4,128)(2,1)S(1)} all-to-all(bf16[64,6,4,128]{3,2,1,0:T(4,128)(2,1)S(1)} %bitcast.41), channel_id=1, replica_groups={{0,8,16,24,32,40,48,56,64,72,80,88,96,104,112,120,128,136,144,152,160,1..., dimensions={0} | all-to-all | bytes 786432 | tf_op jit(solution)/shard_map/all_to_all | solution.py:30
  109.5 0.1 copy.18
  109.6 0.0 copy-done.6
  109.6 0.0 copy-done.7
  109.6 0.7 shard_map.80
  110.3 19.1 %all_to_all.47 = bf16[64,6,4,128]{3,2,1,0:T(4,128)(2,1)S(1)} all-to-all(bf16[64,6,4,128]{3,2,1,0:T(4,128)(2,1)S(1)} %bitcast.40), channel_id=1, replica_groups={{0,8,16,24,32,40,48,56,64,72,80,88,96,104,112,120,128,136,144,152,160,1..., dimensions={0} | all-to-all | bytes 786432 | tf_op jit(solution)/shard_map/all_to_all | solution.py:30
  129.4 0.1 copy.17
  129.4 0.1 broadcast_in_dim.17
  129.6 0.0 copy-start.2
  129.6 19.4 %all_to_all.48.cot_ref = bf16[4,384,512]{2,1,0:T(8,128)(2,1)S(1)} all-to-all(bf16[4,384,512]{2,1,0:T(8,128)(2,1)S(1)} %broadcast_in_dim.17), channel_id=1, replica_groups=mesh['expert'=128,'dp'=4] {'dp'}, dimensions={0} | all-to-all | bytes 3145728 | tf_op jit(solution)/shard_map/all_to_all | solution.py:42
  149.0 4.5 %shard_map.81 = (bf16[4,384,512]{2,1,0:T(8,128)(2,1)S(1)}, bf16[384,384]{1,0:T(8,128)(2,1)S(1)}) custom-call(s32[2]{0:T(128)S(1)} %pad_add_fusion.where_ref, bf16[4,384,512]{2,1,0:T(8,128)(2,1)S(1)} %all_to_all.48.cot_ref, f32[384,384]{1,0:T(8,128)S(1)} %get-tuple-element.15.proj_ref, bf16[384,2048]{1,0:T(8,128)(2,1)S(1)} %bitcast.34, ...), custom_call_target="tpu_custom_call" | custom-call | tf_op jit(solution)/shard_map/pallas_call | solution.py:214
  153.5 0.0 copy-start.4
  153.5 1.1 copy-done.4
  154.7 4.4 %all-to-all-start.6 = ((bf16[4,384,512]{2,1,0:T(8,128)(2,1)}), bf16[4,384,512]{2,1,0:T(8,128)(2,1)}, u32[]{:S(2)}, u32[]{:S(2)}) async-start(bf16[4,384,512]{2,1,0:T(8,128)(2,1)} %copy-done.4), calls=%async_computation.6 | async-start | bytes 3145728 | tf_op jit(solution)/shard_map/all_to_all | solution.py:42
  159.0 2.8 %shard_map.82 = bf16[384,2048]{1,0:T(8,128)(2,1)} custom-call(s32[2]{0:T(128)S(1)} %pad_add_fusion.where_ref, bf16[4,384,512]{2,1,0:T(8,128)(2,1)S(1)} %all-to-all-done.1.rows_ref, bf16[384,384]{1,0:T(8,128)(2,1)S(1)} %get-tuple-element.17.pre_ref), custom_call_target="tpu_custom_call" | custom-call | tf_op jit(solution)/shard_map/pallas_call | solution.py:214
  161.8 1.9 collective-permute-start.2
  163.7 11.1 %all-to-all-done.6 = bf16[4,384,512]{2,1,0:T(8,128)(2,1)} async-done(((bf16[4,384,512]{2,1,0:T(8,128)(2,1)}), bf16[4,384,512]{2,1,0:T(8,128)(2,1)}, u32[]{:S(2)}, u32[]{:S(2)}) %all-to-all-start.6) | async-done | bytes 1572896 | tf_op jit(solution)/shard_map/all_to_all | solution.py:42
  174.8 1.6 add_convert_fusion
  176.3 0.8 add.24
  177.1 8.7 %all-to-all-start.7 = ((bf16[64,6,4,128]{3,2,1,0:T(4,128)(2,1)}), bf16[64,6,4,128]{3,2,1,0:T(4,128)(2,1)S(1)}, u32[]{:S(2)}, u32[]{:S(2)}) async-start(bf16[64,6,4,128]{3,2,1,0:T(4,128)(2,1)} %add.24), calls=%async_computation.7 | async-start | bytes 786432 | tf_op jit(solution)/shard_map/all_to_all | solution.py:30
  185.9 0.0 collective-permute-done.2.lent_ref
  185.9 3.6 %shard_map.83 = (bf16[384,2048]{1,0:T(8,128)(2,1)}, f32[8,128]{1,0:T(8,128)S(1)}) custom-call(s32[2]{0:T(128)S(1)} %pad_add_fusion.where_ref, bf16[4,384,512]{2,1,0:T(8,128)(2,1)S(1)} %all-to-all-done.1.rows_ref, bf16[384,384]{1,0:T(8,128)(2,1)S(1)} %get-tuple-element.17.pre_ref, bf16[384,2048]{1,0:T(8,128)(2,1)} %collective-permute-done.2.lent_ref), custom_call_target="tpu_custom_call" | custom-call | tf_op jit(solution)/shard_map/pallas_call | solution.py:214
  189.5 10.2 %all-to-all-done.7 = bf16[64,6,4,128]{3,2,1,0:T(4,128)(2,1)S(1)} async-done(((bf16[64,6,4,128]{3,2,1,0:T(4,128)(2,1)}), bf16[64,6,4,128]{3,2,1,0:T(4,128)(2,1)S(1)}, u32[]{:S(2)}, u32[]{:S(2)}) %all-to-all-start.7) | async-done | bytes 393248 | tf_op jit(solution)/shard_map/all_to_all | solution.py:30
  199.8 0.1 copy.16
  199.8 0.3 shard_map.84
  200.1 10.5 %all_to_all.49.parts_ref = bf16[4,128,512]{2,1,0:T(8,128)(2,1)S(1)} all-to-all(bf16[4,128,512]{2,1,0:T(8,128)(2,1)S(1)} %shard_map.84), channel_id=1, replica_groups=mesh['expert'=128,'dp'=4] {'dp'}, dimensions={0} | all-to-all | bytes 1048576 | tf_op jit(solution)/shard_map/all_to_all | solution.py:42
  210.6 0.8 shard_map.85
  (6 shorter events, 0.0 us)
Async XLA Ops:
  0.6 1.0 copy-start
  1.7 0.7 copy-start.5
  3.5 33.1 %all-to-all-start = ((bf16[64,6,4,128]{3,2,1,0:T(4,128)(2,1)}), bf16[64,6,4,128]{3,2,1,0:T(4,128)(2,1)S(1)}, u32[]{:S(2)}, u32[]{:S(2)}) async-start(bf16[64,6,4,128]{3,2,1,0:T(4,128)(2,1)} %bitcast.6), calls=%async_computation | async-start | bytes 786432 | tf_op jit(solution)/shard_map/all_to_all | solution.py:30
  20.0 26.7 %collective-permute-start = (bf16[384,2048]{1,0:T(8,128)(2,1)}, bf16[384,2048]{1,0:T(8,128)(2,1)}, u32[]{:S(2)}, u32[]{:S(2)}) collective-permute-start(bf16[384,2048]{1,0:T(8,128)(2,1)} %bitcast.32), channel_id=1, source_target_pairs={{0,4},{4,0},{8,12},{12,8},{16,20},{20,16},{24,28},{28,24},{32,36},... | collective-permute-start | bytes 4718600 | tf_op jit(solution)/shard_map/ppermute | solution.py:59
  38.0 4.4 %copy-start.3 = (bf16[1,192,2048]{2,1,0:T(8,128)(2,1)S(1)}, bf16[1,192,2048]{2,1,0:T(8,128)(2,1)}, u32[]{:S(2)}) copy-start(bf16[1,192,2048]{2,1,0:T(8,128)(2,1)} %param.11) | copy-start | bytes 2359300
  38.0 23.4 %all-to-all-start.1 = ((bf16[4,384,512]{2,1,0:T(8,128)(2,1)}), bf16[4,384,512]{2,1,0:T(8,128)(2,1)S(1)}, u32[]{:S(2)}, u32[]{:S(2)}) async-start(bf16[4,384,512]{2,1,0:T(8,128)(2,1)} %broadcast_in_dim.15), calls=%async_computation.1 | async-start | bytes 3145728 | tf_op jit(solution)/shard_map/all_to_all | solution.py:42
  42.4 4.3 %collective-permute-start.1 = (bf16[192,2048]{1,0:T(8,128)(2,1)S(1)}, bf16[192,2048]{1,0:T(8,128)(2,1)}, u32[]{:S(2)}, u32[]{:S(2)}) collective-permute-start(bf16[192,2048]{1,0:T(8,128)(2,1)S(1)} %bitcast.35), channel_id=1, source_target_pairs={{0,4},{4,0},{8,12},{12,8},{16,20},{20,16},{24,28},{28,24},{32,36},... | collective-permute-start | bytes 2359304 | tf_op jit(solution)/shard_map/ppermute | solution.py:59
  61.4 1.4 copy-start.1
  87.8 21.8 %copy-start.6 = (f32[128,2]{0,1:T(2,128)S(1)}, f32[128,2]{0,1:T(2,128)}, u32[]{:S(2)}) copy-start(f32[128,2]{0,1:T(2,128)} %param.8) | copy-start | bytes 3076
  87.8 21.8 %copy-start.7 = (f32[128]{0:T(128)S(1)}, f32[128]{0:T(128)}, u32[]{:S(2)}) copy-start(f32[128]{0:T(128)} %param.9) | copy-start | bytes 1540
  129.6 19.5 %copy-start.2 = (bf16[1,2,192,2048]{3,2,1,0:T(8,128)(2,1)S(1)}, bf16[1,2,192,2048]{3,2,1,0:T(8,128)(2,1)}, u32[]{:S(2)}) copy-start(bf16[1,2,192,2048]{3,2,1,0:T(8,128)(2,1)} %param.10) | copy-start | bytes 4718596
  153.5 1.1 copy-start.4
  154.7 20.1 %all-to-all-start.6 = ((bf16[4,384,512]{2,1,0:T(8,128)(2,1)}), bf16[4,384,512]{2,1,0:T(8,128)(2,1)}, u32[]{:S(2)}, u32[]{:S(2)}) async-start(bf16[4,384,512]{2,1,0:T(8,128)(2,1)} %copy-done.4), calls=%async_computation.6 | async-start | bytes 3145728 | tf_op jit(solution)/shard_map/all_to_all | solution.py:42
  161.8 24.1 %collective-permute-start.2 = (bf16[384,2048]{1,0:T(8,128)(2,1)}, bf16[384,2048]{1,0:T(8,128)(2,1)}, u32[]{:S(2)}, u32[]{:S(2)}) collective-permute-start(bf16[384,2048]{1,0:T(8,128)(2,1)} %shard_map.82), channel_id=1, source_target_pairs={{0,4},{4,0},{8,12},{12,8},{16,20},{20,16},{24,28},{28,24},{32,36},... | collective-permute-start | bytes 4718600 | tf_op jit(solution)/shard_map/ppermute | solution.py:59
  177.1 22.6 %all-to-all-start.7 = ((bf16[64,6,4,128]{3,2,1,0:T(4,128)(2,1)}), bf16[64,6,4,128]{3,2,1,0:T(4,128)(2,1)S(1)}, u32[]{:S(2)}, u32[]{:S(2)}) async-start(bf16[64,6,4,128]{3,2,1,0:T(4,128)(2,1)} %add.24), calls=%async_computation.7 | async-start | bytes 786432 | tf_op jit(solution)/shard_map/all_to_all | solution.py:30

commit v8 on v7

--- a/solution.py
+++ b/solution.py
@@ -15,6 +15,7 @@
 VMEM_BYTES = 20 * 1024 * 1024
 VMEM = pl.BlockSpec(memory_space=pltpu.VMEM)
 SMEM = pl.BlockSpec(memory_space=pltpu.SMEM)
+HBM = pl.BlockSpec(memory_space=pltpu.HBM)
 
 
 def swish_parts(preact):
@@ -84,11 +85,22 @@
     return jnp.where(lent, hot_core, at) == core
 
 
-def contract(blocks_ref, own_ref, other_ref, where_ref):
+def fetch(sources, targets, sems):
+    copies = [
+        pltpu.make_async_copy(source, target, sems.at[i])
+        for i, (source, target) in enumerate(zip(sources, targets))
+    ]
+    for copy in copies:
+        copy.start()
+    return copies
+
+
+def contract(blocks_ref, own_ref, other_ref, where_ref, other_copy):
     def product(weight_ref):
         return sum(mm_t(blocks_ref[q], weight_ref[:, span]) for q, span in column_blocks(blocks_ref))
 
     own = product(own_ref)
+    other_copy.wait()
     return jnp.where(rows_of_core(where_ref, own.shape, where_ref[0]), own, product(other_ref))
 
 
@@ -101,27 +113,33 @@
 
 
 def forward_kernel(
-    where_ref, rows_ref, in_ref, out_ref, other_in_ref, other_out_ref, partial_ref, proj_ref
+    where_ref, rows_ref, in_ref, out_ref, in_far, out_far, partial_ref, proj_ref, *held
 ):
+    other_in_ref, other_out_ref, sems = held
+    in_copy, out_copy = fetch((in_far, out_far), (other_in_ref, other_out_ref), sems)
     quarter = out_ref.shape[0]
-    projected = contract(rows_ref, in_ref, other_in_ref, where_ref)
+    projected = contract(rows_ref, in_ref, other_in_ref, where_ref, in_copy)
     proj_ref[...] = projected
     swish_value, _ = swish_parts(projected[:, :quarter])
     hidden = (swish_value * projected[:, quarter:]).astype(BF)
+    out_copy.wait()
     expand(hidden, out_ref, other_out_ref, where_ref, partial_ref)
 
 
 def backward_kernel(
-    where_ref, cot_ref, proj_ref, in_ref, out_ref, other_in_ref, other_out_ref, partial_ref, pre_ref
+    where_ref, cot_ref, proj_ref, in_ref, out_ref, in_far, out_far, partial_ref, pre_ref, *held
 ):
+    other_in_ref, other_out_ref, sems = held
+    out_copy, in_copy = fetch((out_far, in_far), (other_out_ref, other_in_ref), sems)
     quarter = out_ref.shape[0]
-    back_hidden = contract(cot_ref, out_ref, other_out_ref, where_ref)
+    back_hidden = contract(cot_ref, out_ref, other_out_ref, where_ref, out_copy)
     projected = proj_ref[...]
     swish_value, swish_slope = swish_parts(projected[:, :quarter])
     grad_pre = jnp.concatenate(
         [back_hidden * projected[:, quarter:] * swish_slope, back_hidden * swish_value], axis=1
     ).astype(BF)
     pre_ref[...] = grad_pre
+    in_copy.wait()
     expand(grad_pre, in_ref, other_in_ref, where_ref, partial_ref)
 
 
@@ -210,12 +228,14 @@
     out_ref[...] = total.astype(BF).reshape(out_ref.shape)
 
 
-def call(kernel, outs, args, scalars=0):
+def call(kernel, outs, args, scalars=0, far=0, scratch=()):
+    near = len(args) - scalars - far
     return pl.pallas_call(
         kernel,
         out_shape=outs,
-        in_specs=[SMEM] * scalars + [VMEM] * (len(args) - scalars),
+        in_specs=[SMEM] * scalars + [VMEM] * near + [HBM] * far,
         out_specs=jax.tree.map(lambda _: VMEM, outs),
+        scratch_shapes=list(scratch),
         compiler_params=pltpu.CompilerParams(vmem_limit_bytes=VMEM_BYTES),
     )(*args)
 
@@ -250,12 +270,19 @@
 
     other_in, other_out = swap_cores(own_in), swap_cores(own_out)
     weights = (own_in, own_out, other_in, other_out)
+    held = [
+        pltpu.VMEM(own_in.shape, BF),
+        pltpu.VMEM(own_out.shape, BF),
+        pltpu.SemaphoreType.DMA((2,)),
+    ]
     rows = gather_dp(over_chips(outgoing))
     partial, projected = call(
         forward_kernel,
         [out(parts, slots, cols), out(slots, 2 * quarter, dtype=F32)],
         (where, rows, *weights),
         scalars=1,
+        far=2,
+        scratch=held,
     )
     returned = over_chips(call(sum_kernel, sent, (over_dp(partial),)))
     cot_send = call(
@@ -269,6 +296,8 @@
         [out(parts, slots, cols), out(slots, 2 * quarter)],
         (where, cot, projected, *weights),
         scalars=1,
+        far=2,
+        scratch=held,
     )
     lent = call(
         lent_gradient_kernel, out(2 * quarter, width), (where, rows, grad_pre), scalars=1

time: 212 us -> 213 us (level)
  no operation moved by 1% of the time
where the time goes in v8:
time: 213 us; the launch traced here: 212 us
  blocking collectives  91.1 us (43%)
  waiting for transfers between devices  51.7 us (24%)
  starting transfers between devices  39.5 us (19%)
  Pallas kernels  19 us (9%)
  local copies, waits for them, and re-layouts  6.73 us (3%)
  between operations  2.21 us (1%)
    all_to_all x3, blocking collectives, over_dp(): return lax.all_to_all(blocks, 'dp', split_axis=0, concat_axis=0, tiled=True)  50.5 us
    all_to_all x2, blocking collectives, over_chips(): lax.all_to_all(rows.reshape(chips, CORES * SLOTS, cols // LANES, LANES),...  40.5 us
    all_to_all x2, waiting for transfers between devices, over_dp(): return lax.all_to_all(blocks, 'dp', split_axis=0, concat_axis=0, tiled=True)  25.8 us
    all_to_all x2, waiting for transfers between devices, over_chips(): lax.all_to_all(rows.reshape(chips, CORES * SLOTS, cols // LANES, LANES),...  24.9 us
    all_to_all x2, starting transfers between devices, over_chips(): lax.all_to_all(rows.reshape(chips, CORES * SLOTS, cols // LANES, LANES),...  24.9 us
    pallas_call x9, Pallas kernels, call(): pl.pallas_call(kernel, out_shape=outs, in_specs=[SMEM] * scalars + [VMEM]...  19 us
    all_to_all x2, starting transfers between devices, over_dp(): return lax.all_to_all(blocks, 'dp', split_axis=0, concat_axis=0, tiled=True)  8.77 us
    ppermute x3, starting transfers between devices, swap_cores(): return lax.ppermute(value, 'expert', [(i, i ^ 1) for i in range(experts)])  5.74 us
  transfers between devices with their start and end apart: 7, of which 5 were waited for; matrix products, arithmetic and copies ran while one was open for 2% of the time, Pallas kernels for 3%

profile of v8, /device:TPU:16, one launch (start us, length us, event | category | flops | bytes accessed | tf_op | source)
XLA Modules:
  0.0 211.7 jit_solution(17760672881886929198)
XLA Ops:
  0.6 0.0 copy-start
  0.6 1.0 copy-done
  1.7 0.0 copy-start.5
  1.7 0.7 copy-done.5
  2.4 1.2 shard_map.77
  3.5 16.5 %all-to-all-start = ((bf16[64,6,4,128]{3,2,1,0:T(4,128)(2,1)}), bf16[64,6,4,128]{3,2,1,0:T(4,128)(2,1)S(1)}, u32[]{:S(2)}, u32[]{:S(2)}) async-start(bf16[64,6,4,128]{3,2,1,0:T(4,128)(2,1)} %bitcast.6), calls=%async_computation | async-start | bytes 786432 | tf_op jit(solution)/shard_map/all_to_all | solution.py:31
  20.0 1.9 collective-permute-start
  22.0 14.7 %all-to-all-done = bf16[64,6,4,128]{3,2,1,0:T(4,128)(2,1)S(1)} async-done(((bf16[64,6,4,128]{3,2,1,0:T(4,128)(2,1)}), bf16[64,6,4,128]{3,2,1,0:T(4,128)(2,1)S(1)}, u32[]{:S(2)}, u32[]{:S(2)}) %all-to-all-start) | async-done | bytes 393248 | tf_op jit(solution)/shard_map/all_to_all | solution.py:31
  36.7 0.1 copy.19
  36.7 1.3 broadcast_in_dim.15
  38.0 4.4 %all-to-all-start.1 = ((bf16[4,384,512]{2,1,0:T(8,128)(2,1)}), bf16[4,384,512]{2,1,0:T(8,128)(2,1)S(1)}, u32[]{:S(2)}, u32[]{:S(2)}) async-start(bf16[4,384,512]{2,1,0:T(8,128)(2,1)} %broadcast_in_dim.15), calls=%async_computation.1 | async-start | bytes 3145728 | tf_op jit(solution)/shard_map/all_to_all | solution.py:43
  42.4 0.0 copy-done.3
  42.4 1.9 collective-permute-start.1
  45.7 0.1 pad_add_fusion.where_ref
  45.8 0.9 collective-permute-done.1.out_far
  46.7 0.0 collective-permute-done.in_far
  46.7 14.7 %all-to-all-done.1.rows_ref = bf16[4,384,512]{2,1,0:T(8,128)(2,1)S(1)} async-done(((bf16[4,384,512]{2,1,0:T(8,128)(2,1)}), bf16[4,384,512]{2,1,0:T(8,128)(2,1)S(1)}, u32[]{:S(2)}, u32[]{:S(2)}) %all-to-all-start.1) | async-done | bytes 1572896 | tf_op jit(solution)/shard_map/all_to_all | solution.py:43
  61.4 1.4 copy-done.1
  62.9 4.1 %shard_map.78 = (bf16[4,384,512]{2,1,0:T(8,128)(2,1)S(1)}, f32[384,384]{1,0:T(8,128)S(1)}) custom-call(s32[2]{0:T(128)S(1)} %pad_add_fusion.where_ref, bf16[4,384,512]{2,1,0:T(8,128)(2,1)S(1)} %all-to-all-done.1.rows_ref, bf16[384,2048]{1,0:T(8,128)(2,1)S(1)} %bitcast.33, bf16[192,2048]{1,0:T(8,128)(2,1)S(1)} %bitcast.36, ...), custom_call_target="tpu_custom_call" | custom-call | tf_op jit(solution)/shard_map/pallas_call | solution.py:233
  66.9 20.5 %all_to_all.45.blocks_ref = bf16[4,384,512]{2,1,0:T(8,128)(2,1)S(1)} all-to-all(bf16[4,384,512]{2,1,0:T(8,128)(2,1)S(1)} %get-tuple-element.14), channel_id=1, replica_groups=mesh['expert'=128,'dp'=4] {'dp'}, dimensions={0} | all-to-all | bytes 3145728 | tf_op jit(solution)/shard_map/all_to_all | solution.py:43
  87.5 0.2 shard_map.79
  87.6 21.5 %all_to_all.46 = bf16[64,6,4,128]{3,2,1,0:T(4,128)(2,1)S(1)} all-to-all(bf16[64,6,4,128]{3,2,1,0:T(4,128)(2,1)S(1)} %bitcast.41), channel_id=1, replica_groups={{0,8,16,24,32,40,48,56,64,72,80,88,96,104,112,120,128,136,144,152,160,1..., dimensions={0} | all-to-all | bytes 786432 | tf_op jit(solution)/shard_map/all_to_all | solution.py:31
  109.1 0.1 copy.18
  109.2 0.0 copy-done.6
  109.2 0.0 copy-done.7
  109.2 0.7 shard_map.80
  110.0 19.0 %all_to_all.47 = bf16[64,6,4,128]{3,2,1,0:T(4,128)(2,1)S(1)} all-to-all(bf16[64,6,4,128]{3,2,1,0:T(4,128)(2,1)S(1)} %bitcast.40), channel_id=1, replica_groups={{0,8,16,24,32,40,48,56,64,72,80,88,96,104,112,120,128,136,144,152,160,1..., dimensions={0} | all-to-all | bytes 786432 | tf_op jit(solution)/shard_map/all_to_all | solution.py:31
  129.0 0.1 copy.17
  129.1 0.1 broadcast_in_dim.17
  129.2 0.0 copy-start.2
  129.2 19.5 %all_to_all.48.cot_ref = bf16[4,384,512]{2,1,0:T(8,128)(2,1)S(1)} all-to-all(bf16[4,384,512]{2,1,0:T(8,128)(2,1)S(1)} %broadcast_in_dim.17), channel_id=1, replica_groups=mesh['expert'=128,'dp'=4] {'dp'}, dimensions={0} | all-to-all | bytes 3145728 | tf_op jit(solution)/shard_map/all_to_all | solution.py:43
  148.7 5.3 %shard_map.81 = (bf16[4,384,512]{2,1,0:T(8,128)(2,1)S(1)}, bf16[384,384]{1,0:T(8,128)(2,1)S(1)}) custom-call(s32[2]{0:T(128)S(1)} %pad_add_fusion.where_ref, bf16[4,384,512]{2,1,0:T(8,128)(2,1)S(1)} %all_to_all.48.cot_ref, f32[384,384]{1,0:T(8,128)S(1)} %get-tuple-element.15.proj_ref, bf16[384,2048]{1,0:T(8,128)(2,1)S(1)} %bitcast.34, ...), custom_call_target="tpu_custom_call" | custom-call | tf_op jit(solution)/shard_map/pallas_call | solution.py:233
  154.0 0.0 copy-start.4
  154.1 1.1 copy-done.4
  155.2 4.4 %all-to-all-start.6 = ((bf16[4,384,512]{2,1,0:T(8,128)(2,1)}), bf16[4,384,512]{2,1,0:T(8,128)(2,1)}, u32[]{:S(2)}, u32[]{:S(2)}) async-start(bf16[4,384,512]{2,1,0:T(8,128)(2,1)} %copy-done.4), calls=%async_computation.6 | async-start | bytes 3145728 | tf_op jit(solution)/shard_map/all_to_all | solution.py:43
  159.5 2.8 %shard_map.82 = bf16[384,2048]{1,0:T(8,128)(2,1)} custom-call(s32[2]{0:T(128)S(1)} %pad_add_fusion.where_ref, bf16[4,384,512]{2,1,0:T(8,128)(2,1)S(1)} %all-to-all-done.1.rows_ref, bf16[384,384]{1,0:T(8,128)(2,1)S(1)} %get-tuple-element.17.pre_ref), custom_call_target="tpu_custom_call" | custom-call | tf_op jit(solution)/shard_map/pallas_call | solution.py:233
  162.3 1.9 collective-permute-start.2
  164.2 11.1 %all-to-all-done.6 = bf16[4,384,512]{2,1,0:T(8,128)(2,1)} async-done(((bf16[4,384,512]{2,1,0:T(8,128)(2,1)}), bf16[4,384,512]{2,1,0:T(8,128)(2,1)}, u32[]{:S(2)}, u32[]{:S(2)}) %all-to-all-start.6) | async-done | bytes 1572896 | tf_op jit(solution)/shard_map/all_to_all | solution.py:43
  175.3 1.6 add_convert_fusion
  176.9 0.8 add.24
  177.7 8.5 %all-to-all-start.7 = ((bf16[64,6,4,128]{3,2,1,0:T(4,128)(2,1)}), bf16[64,6,4,128]{3,2,1,0:T(4,128)(2,1)S(1)}, u32[]{:S(2)}, u32[]{:S(2)}) async-start(bf16[64,6,4,128]{3,2,1,0:T(4,128)(2,1)} %add.24), calls=%async_computation.7 | async-start | bytes 786432 | tf_op jit(solution)/shard_map/all_to_all | solution.py:31
  186.2 0.0 collective-permute-done.2.lent_ref
  186.2 3.6 %shard_map.83 = (bf16[384,2048]{1,0:T(8,128)(2,1)}, f32[8,128]{1,0:T(8,128)S(1)}) custom-call(s32[2]{0:T(128)S(1)} %pad_add_fusion.where_ref, bf16[4,384,512]{2,1,0:T(8,128)(2,1)S(1)} %all-to-all-done.1.rows_ref, bf16[384,384]{1,0:T(8,128)(2,1)S(1)} %get-tuple-element.17.pre_ref, bf16[384,2048]{1,0:T(8,128)(2,1)} %collective-permute-done.2.lent_ref), custom_call_target="tpu_custom_call" | custom-call | tf_op jit(solution)/shard_map/pallas_call | solution.py:233
  189.8 10.2 %all-to-all-done.7 = bf16[64,6,4,128]{3,2,1,0:T(4,128)(2,1)S(1)} async-done(((bf16[64,6,4,128]{3,2,1,0:T(4,128)(2,1)}), bf16[64,6,4,128]{3,2,1,0:T(4,128)(2,1)S(1)}, u32[]{:S(2)}, u32[]{:S(2)}) %all-to-all-start.7) | async-done | bytes 393248 | tf_op jit(solution)/shard_map/all_to_all | solution.py:31
  200.1 0.1 copy.16
  200.1 0.3 shard_map.84
  200.4 10.5 %all_to_all.49.parts_ref = bf16[4,128,512]{2,1,0:T(8,128)(2,1)S(1)} all-to-all(bf16[4,128,512]{2,1,0:T(8,128)(2,1)S(1)} %shard_map.84), channel_id=1, replica_groups=mesh['expert'=128,'dp'=4] {'dp'}, dimensions={0} | all-to-all | bytes 1048576 | tf_op jit(solution)/shard_map/all_to_all | solution.py:43
  210.9 0.8 shard_map.85
  (6 shorter events, 0.0 us)
Async XLA Ops:
  0.6 1.0 copy-start
  1.7 0.7 copy-start.5
  3.5 33.1 %all-to-all-start = ((bf16[64,6,4,128]{3,2,1,0:T(4,128)(2,1)}), bf16[64,6,4,128]{3,2,1,0:T(4,128)(2,1)S(1)}, u32[]{:S(2)}, u32[]{:S(2)}) async-start(bf16[64,6,4,128]{3,2,1,0:T(4,128)(2,1)} %bitcast.6), calls=%async_computation | async-start | bytes 786432 | tf_op jit(solution)/shard_map/all_to_all | solution.py:31
  20.0 26.7 %collective-permute-start = (bf16[384,2048]{1,0:T(8,128)(2,1)}, bf16[384,2048]{1,0:T(8,128)(2,1)}, u32[]{:S(2)}, u32[]{:S(2)}) collective-permute-start(bf16[384,2048]{1,0:T(8,128)(2,1)} %bitcast.32), channel_id=1, source_target_pairs={{0,4},{4,0},{8,12},{12,8},{16,20},{20,16},{24,28},{28,24},{32,36},... | collective-permute-start | bytes 4718600 | tf_op jit(solution)/shard_map/ppermute | solution.py:60
  38.0 4.4 %copy-start.3 = (bf16[1,192,2048]{2,1,0:T(8,128)(2,1)S(1)}, bf16[1,192,2048]{2,1,0:T(8,128)(2,1)}, u32[]{:S(2)}) copy-start(bf16[1,192,2048]{2,1,0:T(8,128)(2,1)} %param.11) | copy-start | bytes 2359300
  38.0 23.4 %all-to-all-start.1 = ((bf16[4,384,512]{2,1,0:T(8,128)(2,1)}), bf16[4,384,512]{2,1,0:T(8,128)(2,1)S(1)}, u32[]{:S(2)}, u32[]{:S(2)}) async-start(bf16[4,384,512]{2,1,0:T(8,128)(2,1)} %broadcast_in_dim.15), calls=%async_computation.1 | async-start | bytes 3145728 | tf_op jit(solution)/shard_map/all_to_all | solution.py:43
  42.4 4.3 %collective-permute-start.1 = (bf16[192,2048]{1,0:T(8,128)(2,1)S(1)}, bf16[192,2048]{1,0:T(8,128)(2,1)}, u32[]{:S(2)}, u32[]{:S(2)}) collective-permute-start(bf16[192,2048]{1,0:T(8,128)(2,1)S(1)} %bitcast.35), channel_id=1, source_target_pairs={{0,4},{4,0},{8,12},{12,8},{16,20},{20,16},{24,28},{28,24},{32,36},... | collective-permute-start | bytes 2359304 | tf_op jit(solution)/shard_map/ppermute | solution.py:60
  61.4 1.4 copy-start.1
  87.4 21.8 %copy-start.6 = (f32[128,2]{0,1:T(2,128)S(1)}, f32[128,2]{0,1:T(2,128)}, u32[]{:S(2)}) copy-start(f32[128,2]{0,1:T(2,128)} %param.8) | copy-start | bytes 3076
  87.4 21.8 %copy-start.7 = (f32[128]{0:T(128)S(1)}, f32[128]{0:T(128)}, u32[]{:S(2)}) copy-start(f32[128]{0:T(128)} %param.9) | copy-start | bytes 1540
  129.2 19.5 %copy-start.2 = (bf16[1,2,192,2048]{3,2,1,0:T(8,128)(2,1)S(1)}, bf16[1,2,192,2048]{3,2,1,0:T(8,128)(2,1)}, u32[]{:S(2)}) copy-start(bf16[1,2,192,2048]{3,2,1,0:T(8,128)(2,1)} %param.10) | copy-start | bytes 4718596
  154.0 1.1 copy-start.4
  155.2 20.1 %all-to-all-start.6 = ((bf16[4,384,512]{2,1,0:T(8,128)(2,1)}), bf16[4,384,512]{2,1,0:T(8,128)(2,1)}, u32[]{:S(2)}, u32[]{:S(2)}) async-start(bf16[4,384,512]{2,1,0:T(8,128)(2,1)} %copy-done.4), calls=%async_computation.6 | async-start | bytes 3145728 | tf_op jit(solution)/shard_map/all_to_all | solution.py:43
  162.3 23.9 %collective-permute-start.2 = (bf16[384,2048]{1,0:T(8,128)(2,1)}, bf16[384,2048]{1,0:T(8,128)(2,1)}, u32[]{:S(2)}, u32[]{:S(2)}) collective-permute-start(bf16[384,2048]{1,0:T(8,128)(2,1)} %shard_map.82), channel_id=1, source_target_pairs={{0,4},{4,0},{8,12},{12,8},{16,20},{20,16},{24,28},{28,24},{32,36},... | collective-permute-start | bytes 4718600 | tf_op jit(solution)/shard_map/ppermute | solution.py:60
  177.7 22.4 %all-to-all-start.7 = ((bf16[64,6,4,128]{3,2,1,0:T(4,128)(2,1)}), bf16[64,6,4,128]{3,2,1,0:T(4,128)(2,1)S(1)}, u32[]{:S(2)}, u32[]{:S(2)}) async-start(bf16[64,6,4,128]{3,2,1,0:T(4,128)(2,1)} %add.24), calls=%async_computation.7 | async-start | bytes 786432 | tf_op jit(solution)/shard_map/all_to_all | solution.py:31

commit v9 on v8

--- a/solution.py
+++ b/solution.py
@@ -95,12 +95,13 @@
     return copies
 
 
-def contract(blocks_ref, own_ref, other_ref, where_ref, other_copy):
+def contract(blocks_ref, own_ref, other_ref, where_ref, other_copy=None):
     def product(weight_ref):
         return sum(mm_t(blocks_ref[q], weight_ref[:, span]) for q, span in column_blocks(blocks_ref))
 
     own = product(own_ref)
-    other_copy.wait()
+    if other_copy is not None:
+        other_copy.wait()
     return jnp.where(rows_of_core(where_ref, own.shape, where_ref[0]), own, product(other_ref))
 
 
@@ -127,19 +128,16 @@
 
 
 def backward_kernel(
-    where_ref, cot_ref, proj_ref, in_ref, out_ref, in_far, out_far, partial_ref, pre_ref, *held
+    where_ref, cot_ref, proj_ref, in_ref, out_ref, other_in_ref, other_out_ref, partial_ref, pre_ref
 ):
-    other_in_ref, other_out_ref, sems = held
-    out_copy, in_copy = fetch((out_far, in_far), (other_out_ref, other_in_ref), sems)
     quarter = out_ref.shape[0]
-    back_hidden = contract(cot_ref, out_ref, other_out_ref, where_ref, out_copy)
+    back_hidden = contract(cot_ref, out_ref, other_out_ref, where_ref)
     projected = proj_ref[...]
     swish_value, swish_slope = swish_parts(projected[:, :quarter])
     grad_pre = jnp.concatenate(
         [back_hidden * projected[:, quarter:] * swish_slope, back_hidden * swish_value], axis=1
     ).astype(BF)
     pre_ref[...] = grad_pre
-    in_copy.wait()
     expand(grad_pre, in_ref, other_in_ref, where_ref, partial_ref)
 
 
@@ -296,8 +294,6 @@
         [out(parts, slots, cols), out(slots, 2 * quarter)],
         (where, cot, projected, *weights),
         scalars=1,
-        far=2,
-        scratch=held,
     )
     lent = call(
         lent_gradient_kernel, out(2 * quarter, width), (where, rows, grad_pre), scalars=1

time: 213 us -> 212 us (level)
  no operation moved by 1% of the time
where the time goes in v9:
time: 212 us; the launch traced here: 211 us
  blocking collectives  91.1 us (43%)
  waiting for transfers between devices  51.7 us (24%)
  starting transfers between devices  39.5 us (19%)
  Pallas kernels  18.1 us (9%)
  local copies, waits for them, and re-layouts  6.73 us (3%)
  between operations  2.21 us (1%)
    all_to_all x3, blocking collectives, over_dp(): return lax.all_to_all(blocks, 'dp', split_axis=0, concat_axis=0, tiled=True)  50.5 us
    all_to_all x2, blocking collectives, over_chips(): lax.all_to_all(rows.reshape(chips, CORES * SLOTS, cols // LANES, LANES),...  40.5 us
    all_to_all x2, waiting for transfers between devices, over_dp(): return lax.all_to_all(blocks, 'dp', split_axis=0, concat_axis=0, tiled=True)  25.8 us
    all_to_all x2, waiting for transfers between devices, over_chips(): lax.all_to_all(rows.reshape(chips, CORES * SLOTS, cols // LANES, LANES),...  24.9 us
    all_to_all x2, starting transfers between devices, over_chips(): lax.all_to_all(rows.reshape(chips, CORES * SLOTS, cols // LANES, LANES),...  24.9 us
    pallas_call x9, Pallas kernels, call(): pl.pallas_call(kernel, out_shape=outs, in_specs=[SMEM] * scalars + [VMEM]...  18.1 us
    all_to_all x2, starting transfers between devices, over_dp(): return lax.all_to_all(blocks, 'dp', split_axis=0, concat_axis=0, tiled=True)  8.77 us
    ppermute x3, starting transfers between devices, swap_cores(): return lax.ppermute(value, 'expert', [(i, i ^ 1) for i in range(experts)])  5.74 us
  transfers between devices with their start and end apart: 7, of which 5 were waited for; matrix products, arithmetic and copies ran while one was open for 2% of the time, Pallas kernels for 3%

profile of v9, /device:TPU:16, one launch (start us, length us, event | category | flops | bytes accessed | tf_op | source)
XLA Modules:
  0.0 210.9 jit_solution(8750847861851391862)
XLA Ops:
  0.6 0.0 copy-start
  0.6 1.0 copy-done
  1.7 0.0 copy-start.5
  1.7 0.7 copy-done.5
  2.4 1.2 shard_map.77
  3.5 16.5 %all-to-all-start = ((bf16[64,6,4,128]{3,2,1,0:T(4,128)(2,1)}), bf16[64,6,4,128]{3,2,1,0:T(4,128)(2,1)S(1)}, u32[]{:S(2)}, u32[]{:S(2)}) async-start(bf16[64,6,4,128]{3,2,1,0:T(4,128)(2,1)} %bitcast.6), calls=%async_computation | async-start | bytes 786432 | tf_op jit(solution)/shard_map/all_to_all | solution.py:31
  20.0 1.9 collective-permute-start
  22.0 14.7 %all-to-all-done = bf16[64,6,4,128]{3,2,1,0:T(4,128)(2,1)S(1)} async-done(((bf16[64,6,4,128]{3,2,1,0:T(4,128)(2,1)}), bf16[64,6,4,128]{3,2,1,0:T(4,128)(2,1)S(1)}, u32[]{:S(2)}, u32[]{:S(2)}) %all-to-all-start) | async-done | bytes 393248 | tf_op jit(solution)/shard_map/all_to_all | solution.py:31
  36.7 0.1 copy.19
  36.7 1.3 broadcast_in_dim.15
  38.0 4.4 %all-to-all-start.1 = ((bf16[4,384,512]{2,1,0:T(8,128)(2,1)}), bf16[4,384,512]{2,1,0:T(8,128)(2,1)S(1)}, u32[]{:S(2)}, u32[]{:S(2)}) async-start(bf16[4,384,512]{2,1,0:T(8,128)(2,1)} %broadcast_in_dim.15), calls=%async_computation.1 | async-start | bytes 3145728 | tf_op jit(solution)/shard_map/all_to_all | solution.py:43
  42.4 0.0 copy-done.3
  42.4 1.9 collective-permute-start.1
  45.7 0.1 pad_add_fusion.where_ref
  45.8 0.9 collective-permute-done.1.out_far.other_out_ref
  46.7 0.0 collective-permute-done.in_far.other_in_ref
  46.7 14.7 %all-to-all-done.1.rows_ref = bf16[4,384,512]{2,1,0:T(8,128)(2,1)S(1)} async-done(((bf16[4,384,512]{2,1,0:T(8,128)(2,1)}), bf16[4,384,512]{2,1,0:T(8,128)(2,1)S(1)}, u32[]{:S(2)}, u32[]{:S(2)}) %all-to-all-start.1) | async-done | bytes 1572896 | tf_op jit(solution)/shard_map/all_to_all | solution.py:43
  61.4 1.4 copy-done.1
  62.9 4.1 %shard_map.78 = (bf16[4,384,512]{2,1,0:T(8,128)(2,1)S(1)}, f32[384,384]{1,0:T(8,128)S(1)}) custom-call(s32[2]{0:T(128)S(1)} %pad_add_fusion.where_ref, bf16[4,384,512]{2,1,0:T(8,128)(2,1)S(1)} %all-to-all-done.1.rows_ref, bf16[384,2048]{1,0:T(8,128)(2,1)S(1)} %bitcast.33, bf16[192,2048]{1,0:T(8,128)(2,1)S(1)} %bitcast.36, ...), custom_call_target="tpu_custom_call" | custom-call | tf_op jit(solution)/shard_map/pallas_call | solution.py:231
  66.9 20.5 %all_to_all.45.blocks_ref = bf16[4,384,512]{2,1,0:T(8,128)(2,1)S(1)} all-to-all(bf16[4,384,512]{2,1,0:T(8,128)(2,1)S(1)} %get-tuple-element.14), channel_id=1, replica_groups=mesh['expert'=128,'dp'=4] {'dp'}, dimensions={0} | all-to-all | bytes 3145728 | tf_op jit(solution)/shard_map/all_to_all | solution.py:43
  87.5 0.2 shard_map.79
  87.6 21.5 %all_to_all.46 = bf16[64,6,4,128]{3,2,1,0:T(4,128)(2,1)S(1)} all-to-all(bf16[64,6,4,128]{3,2,1,0:T(4,128)(2,1)S(1)} %bitcast.41), channel_id=1, replica_groups={{0,8,16,24,32,40,48,56,64,72,80,88,96,104,112,120,128,136,144,152,160,1..., dimensions={0} | all-to-all | bytes 786432 | tf_op jit(solution)/shard_map/all_to_all | solution.py:31
  109.1 0.1 copy.18
  109.2 0.0 copy-done.6
  109.2 0.0 copy-done.7
  109.2 0.7 shard_map.80
  110.0 19.0 %all_to_all.47 = bf16[64,6,4,128]{3,2,1,0:T(4,128)(2,1)S(1)} all-to-all(bf16[64,6,4,128]{3,2,1,0:T(4,128)(2,1)S(1)} %bitcast.40), channel_id=1, replica_groups={{0,8,16,24,32,40,48,56,64,72,80,88,96,104,112,120,128,136,144,152,160,1..., dimensions={0} | all-to-all | bytes 786432 | tf_op jit(solution)/shard_map/all_to_all | solution.py:31
  129.0 0.1 copy.17
  129.1 0.1 broadcast_in_dim.17
  129.2 0.0 copy-start.2
  129.2 19.5 %all_to_all.48.cot_ref = bf16[4,384,512]{2,1,0:T(8,128)(2,1)S(1)} all-to-all(bf16[4,384,512]{2,1,0:T(8,128)(2,1)S(1)} %broadcast_in_dim.17), channel_id=1, replica_groups=mesh['expert'=128,'dp'=4] {'dp'}, dimensions={0} | all-to-all | bytes 3145728 | tf_op jit(solution)/shard_map/all_to_all | solution.py:43
  148.7 4.5 %shard_map.81 = (bf16[4,384,512]{2,1,0:T(8,128)(2,1)S(1)}, bf16[384,384]{1,0:T(8,128)(2,1)S(1)}) custom-call(s32[2]{0:T(128)S(1)} %pad_add_fusion.where_ref, bf16[4,384,512]{2,1,0:T(8,128)(2,1)S(1)} %all_to_all.48.cot_ref, f32[384,384]{1,0:T(8,128)S(1)} %get-tuple-element.15.proj_ref, bf16[384,2048]{1,0:T(8,128)(2,1)S(1)} %bitcast.34, ...), custom_call_target="tpu_custom_call" | custom-call | tf_op jit(solution)/shard_map/pallas_call | solution.py:231
  153.2 0.0 copy-start.4
  153.2 1.1 copy-done.4
  154.4 4.4 %all-to-all-start.6 = ((bf16[4,384,512]{2,1,0:T(8,128)(2,1)}), bf16[4,384,512]{2,1,0:T(8,128)(2,1)}, u32[]{:S(2)}, u32[]{:S(2)}) async-start(bf16[4,384,512]{2,1,0:T(8,128)(2,1)} %copy-done.4), calls=%async_computation.6 | async-start | bytes 3145728 | tf_op jit(solution)/shard_map/all_to_all | solution.py:43
  158.7 2.8 %shard_map.82 = bf16[384,2048]{1,0:T(8,128)(2,1)} custom-call(s32[2]{0:T(128)S(1)} %pad_add_fusion.where_ref, bf16[4,384,512]{2,1,0:T(8,128)(2,1)S(1)} %all-to-all-done.1.rows_ref, bf16[384,384]{1,0:T(8,128)(2,1)S(1)} %get-tuple-element.17.pre_ref), custom_call_target="tpu_custom_call" | custom-call | tf_op jit(solution)/shard_map/pallas_call | solution.py:231
  161.5 1.9 collective-permute-start.2
  163.4 11.1 %all-to-all-done.6 = bf16[4,384,512]{2,1,0:T(8,128)(2,1)} async-done(((bf16[4,384,512]{2,1,0:T(8,128)(2,1)}), bf16[4,384,512]{2,1,0:T(8,128)(2,1)}, u32[]{:S(2)}, u32[]{:S(2)}) %all-to-all-start.6) | async-done | bytes 1572896 | tf_op jit(solution)/shard_map/all_to_all | solution.py:43
  174.5 1.6 add_convert_fusion
  176.0 0.8 add.24
  176.9 8.5 %all-to-all-start.7 = ((bf16[64,6,4,128]{3,2,1,0:T(4,128)(2,1)}), bf16[64,6,4,128]{3,2,1,0:T(4,128)(2,1)S(1)}, u32[]{:S(2)}, u32[]{:S(2)}) async-start(bf16[64,6,4,128]{3,2,1,0:T(4,128)(2,1)} %add.24), calls=%async_computation.7 | async-start | bytes 786432 | tf_op jit(solution)/shard_map/all_to_all | solution.py:31
  185.4 0.0 collective-permute-done.2.lent_ref
  185.4 3.6 %shard_map.83 = (bf16[384,2048]{1,0:T(8,128)(2,1)}, f32[8,128]{1,0:T(8,128)S(1)}) custom-call(s32[2]{0:T(128)S(1)} %pad_add_fusion.where_ref, bf16[4,384,512]{2,1,0:T(8,128)(2,1)S(1)} %all-to-all-done.1.rows_ref, bf16[384,384]{1,0:T(8,128)(2,1)S(1)} %get-tuple-element.17.pre_ref, bf16[384,2048]{1,0:T(8,128)(2,1)} %collective-permute-done.2.lent_ref), custom_call_target="tpu_custom_call" | custom-call | tf_op jit(solution)/shard_map/pallas_call | solution.py:231
  189.0 10.2 %all-to-all-done.7 = bf16[64,6,4,128]{3,2,1,0:T(4,128)(2,1)S(1)} async-done(((bf16[64,6,4,128]{3,2,1,0:T(4,128)(2,1)}), bf16[64,6,4,128]{3,2,1,0:T(4,128)(2,1)S(1)}, u32[]{:S(2)}, u32[]{:S(2)}) %all-to-all-start.7) | async-done | bytes 393248 | tf_op jit(solution)/shard_map/all_to_all | solution.py:31
  199.2 0.1 copy.16
  199.3 0.3 shard_map.84
  199.6 10.5 %all_to_all.49.parts_ref = bf16[4,128,512]{2,1,0:T(8,128)(2,1)S(1)} all-to-all(bf16[4,128,512]{2,1,0:T(8,128)(2,1)S(1)} %shard_map.84), channel_id=1, replica_groups=mesh['expert'=128,'dp'=4] {'dp'}, dimensions={0} | all-to-all | bytes 1048576 | tf_op jit(solution)/shard_map/all_to_all | solution.py:43
  210.1 0.8 shard_map.85
  (6 shorter events, 0.0 us)
Async XLA Ops:
  0.6 1.0 copy-start
  1.7 0.7 copy-start.5
  3.5 33.1 %all-to-all-start = ((bf16[64,6,4,128]{3,2,1,0:T(4,128)(2,1)}), bf16[64,6,4,128]{3,2,1,0:T(4,128)(2,1)S(1)}, u32[]{:S(2)}, u32[]{:S(2)}) async-start(bf16[64,6,4,128]{3,2,1,0:T(4,128)(2,1)} %bitcast.6), calls=%async_computation | async-start | bytes 786432 | tf_op jit(solution)/shard_map/all_to_all | solution.py:31
  20.0 26.7 %collective-permute-start = (bf16[384,2048]{1,0:T(8,128)(2,1)}, bf16[384,2048]{1,0:T(8,128)(2,1)}, u32[]{:S(2)}, u32[]{:S(2)}) collective-permute-start(bf16[384,2048]{1,0:T(8,128)(2,1)} %bitcast.32), channel_id=1, source_target_pairs={{0,4},{4,0},{8,12},{12,8},{16,20},{20,16},{24,28},{28,24},{32,36},... | collective-permute-start | bytes 4718600 | tf_op jit(solution)/shard_map/ppermute | solution.py:60
  38.0 4.4 %copy-start.3 = (bf16[1,192,2048]{2,1,0:T(8,128)(2,1)S(1)}, bf16[1,192,2048]{2,1,0:T(8,128)(2,1)}, u32[]{:S(2)}) copy-start(bf16[1,192,2048]{2,1,0:T(8,128)(2,1)} %param.11) | copy-start | bytes 2359300
  38.0 23.4 %all-to-all-start.1 = ((bf16[4,384,512]{2,1,0:T(8,128)(2,1)}), bf16[4,384,512]{2,1,0:T(8,128)(2,1)S(1)}, u32[]{:S(2)}, u32[]{:S(2)}) async-start(bf16[4,384,512]{2,1,0:T(8,128)(2,1)} %broadcast_in_dim.15), calls=%async_computation.1 | async-start | bytes 3145728 | tf_op jit(solution)/shard_map/all_to_all | solution.py:43
  42.4 4.3 %collective-permute-start.1 = (bf16[192,2048]{1,0:T(8,128)(2,1)S(1)}, bf16[192,2048]{1,0:T(8,128)(2,1)}, u32[]{:S(2)}, u32[]{:S(2)}) collective-permute-start(bf16[192,2048]{1,0:T(8,128)(2,1)S(1)} %bitcast.35), channel_id=1, source_target_pairs={{0,4},{4,0},{8,12},{12,8},{16,20},{20,16},{24,28},{28,24},{32,36},... | collective-permute-start | bytes 2359304 | tf_op jit(solution)/shard_map/ppermute | solution.py:60
  61.4 1.4 copy-start.1
  87.4 21.8 %copy-start.6 = (f32[128,2]{0,1:T(2,128)S(1)}, f32[128,2]{0,1:T(2,128)}, u32[]{:S(2)}) copy-start(f32[128,2]{0,1:T(2,128)} %param.8) | copy-start | bytes 3076
  87.4 21.8 %copy-start.7 = (f32[128]{0:T(128)S(1)}, f32[128]{0:T(128)}, u32[]{:S(2)}) copy-start(f32[128]{0:T(128)} %param.9) | copy-start | bytes 1540
  129.2 19.5 %copy-start.2 = (bf16[1,2,192,2048]{3,2,1,0:T(8,128)(2,1)S(1)}, bf16[1,2,192,2048]{3,2,1,0:T(8,128)(2,1)}, u32[]{:S(2)}) copy-start(bf16[1,2,192,2048]{3,2,1,0:T(8,128)(2,1)} %param.10) | copy-start | bytes 4718596
  153.2 1.1 copy-start.4
  154.4 20.1 %all-to-all-start.6 = ((bf16[4,384,512]{2,1,0:T(8,128)(2,1)}), bf16[4,384,512]{2,1,0:T(8,128)(2,1)}, u32[]{:S(2)}, u32[]{:S(2)}) async-start(bf16[4,384,512]{2,1,0:T(8,128)(2,1)} %copy-done.4), calls=%async_computation.6 | async-start | bytes 3145728 | tf_op jit(solution)/shard_map/all_to_all | solution.py:43
  161.5 23.9 %collective-permute-start.2 = (bf16[384,2048]{1,0:T(8,128)(2,1)}, bf16[384,2048]{1,0:T(8,128)(2,1)}, u32[]{:S(2)}, u32[]{:S(2)}) collective-permute-start(bf16[384,2048]{1,0:T(8,128)(2,1)} %shard_map.82), channel_id=1, source_target_pairs={{0,4},{4,0},{8,12},{12,8},{16,20},{20,16},{24,28},{28,24},{32,36},... | collective-permute-start | bytes 4718600 | tf_op jit(solution)/shard_map/ppermute | solution.py:60
  176.9 22.4 %all-to-all-start.7 = ((bf16[64,6,4,128]{3,2,1,0:T(4,128)(2,1)}), bf16[64,6,4,128]{3,2,1,0:T(4,128)(2,1)S(1)}, u32[]{:S(2)}, u32[]{:S(2)}) async-start(bf16[64,6,4,128]{3,2,1,0:T(4,128)(2,1)} %add.24), calls=%async_computation.7 | async-start | bytes 786432 | tf_op jit(solution)/shard_map/all_to_all | solution.py:31

commit v10 on v9

--- a/solution.py
+++ b/solution.py
@@ -128,8 +128,10 @@
 
 
 def backward_kernel(
-    where_ref, cot_ref, proj_ref, in_ref, out_ref, other_in_ref, other_out_ref, partial_ref, pre_ref
+    where_ref, cot_ref, proj_ref, in_ref, out_ref, other_out_ref, in_far, partial_ref, pre_ref, *held
 ):
+    other_in_ref, sems = held
+    (in_copy,) = fetch((in_far,), (other_in_ref,), sems)
     quarter = out_ref.shape[0]
     back_hidden = contract(cot_ref, out_ref, other_out_ref, where_ref)
     projected = proj_ref[...]
@@ -138,6 +140,7 @@
         [back_hidden * projected[:, quarter:] * swish_slope, back_hidden * swish_value], axis=1
     ).astype(BF)
     pre_ref[...] = grad_pre
+    in_copy.wait()
     expand(grad_pre, in_ref, other_in_ref, where_ref, partial_ref)
 
 
@@ -292,8 +295,10 @@
     input_partial, grad_pre = call(
         backward_kernel,
         [out(parts, slots, cols), out(slots, 2 * quarter)],
-        (where, cot, projected, *weights),
+        (where, cot, projected, own_in, own_out, other_out, other_in),
         scalars=1,
+        far=1,
+        scratch=[held[0], pltpu.SemaphoreType.DMA((1,))],
     )
     lent = call(
         lent_gradient_kernel, out(2 * quarter, width), (where, rows, grad_pre), scalars=1

time: 212 us -> 212 us (level)
  no operation moved by 1% of the time
where the time goes in v10:
time: 212 us; the launch traced here: 211 us
  blocking collectives  91.1 us (43%)
  waiting for transfers between devices  51.7 us (24%)
  starting transfers between devices  39.5 us (19%)
  Pallas kernels  18 us (8%)
  local copies, waits for them, and re-layouts  6.73 us (3%)
  between operations  2.21 us (1%)
    all_to_all x3, blocking collectives, over_dp(): return lax.all_to_all(blocks, 'dp', split_axis=0, concat_axis=0, tiled=True)  50.5 us
    all_to_all x2, blocking collectives, over_chips(): lax.all_to_all(rows.reshape(chips, CORES * SLOTS, cols // LANES, LANES),...  40.5 us
    all_to_all x2, waiting for transfers between devices, over_dp(): return lax.all_to_all(blocks, 'dp', split_axis=0, concat_axis=0, tiled=True)  25.8 us
    all_to_all x2, waiting for transfers between devices, over_chips(): lax.all_to_all(rows.reshape(chips, CORES * SLOTS, cols // LANES, LANES),...  25 us
    all_to_all x2, starting transfers between devices, over_chips(): lax.all_to_all(rows.reshape(chips, CORES * SLOTS, cols // LANES, LANES),...  24.9 us
    pallas_call x9, Pallas kernels, call(): pl.pallas_call(kernel, out_shape=outs, in_specs=[SMEM] * scalars + [VMEM]...  18 us
    all_to_all x2, starting transfers between devices, over_dp(): return lax.all_to_all(blocks, 'dp', split_axis=0, concat_axis=0, tiled=True)  8.77 us
    ppermute x3, starting transfers between devices, swap_cores(): return lax.ppermute(value, 'expert', [(i, i ^ 1) for i in range(experts)])  5.74 us
  transfers between devices with their start and end apart: 7, of which 5 were waited for; matrix products, arithmetic and copies ran while one was open for 2% of the time, Pallas kernels for 3%

profile of v10, /device:TPU:16, one launch (start us, length us, event | category | flops | bytes accessed | tf_op | source)
XLA Modules:
  0.0 210.8 jit_solution(8757008209665698636)
XLA Ops:
  0.6 0.0 copy-start
  0.6 1.0 copy-done
  1.7 0.0 copy-start.5
  1.7 0.7 copy-done.5
  2.4 1.2 shard_map.77
  3.5 16.5 %all-to-all-start = ((bf16[64,6,4,128]{3,2,1,0:T(4,128)(2,1)}), bf16[64,6,4,128]{3,2,1,0:T(4,128)(2,1)S(1)}, u32[]{:S(2)}, u32[]{:S(2)}) async-start(bf16[64,6,4,128]{3,2,1,0:T(4,128)(2,1)} %bitcast.6), calls=%async_computation | async-start | bytes 786432 | tf_op jit(solution)/shard_map/all_to_all | solution.py:31
  20.0 1.9 collective-permute-start
  22.0 14.7 %all-to-all-done = bf16[64,6,4,128]{3,2,1,0:T(4,128)(2,1)S(1)} async-done(((bf16[64,6,4,128]{3,2,1,0:T(4,128)(2,1)}), bf16[64,6,4,128]{3,2,1,0:T(4,128)(2,1)S(1)}, u32[]{:S(2)}, u32[]{:S(2)}) %all-to-all-start) | async-done | bytes 393248 | tf_op jit(solution)/shard_map/all_to_all | solution.py:31
  36.7 0.1 copy.19
  36.7 1.3 broadcast_in_dim.15
  38.0 4.4 %all-to-all-start.1 = ((bf16[4,384,512]{2,1,0:T(8,128)(2,1)}), bf16[4,384,512]{2,1,0:T(8,128)(2,1)S(1)}, u32[]{:S(2)}, u32[]{:S(2)}) async-start(bf16[4,384,512]{2,1,0:T(8,128)(2,1)} %broadcast_in_dim.15), calls=%async_computation.1 | async-start | bytes 3145728 | tf_op jit(solution)/shard_map/all_to_all | solution.py:43
  42.4 0.0 copy-done.3
  42.4 1.9 collective-permute-start.1
  45.7 0.1 pad_add_fusion.where_ref
  45.8 0.9 collective-permute-done.1.out_far.other_out_ref
  46.7 0.0 collective-permute-done.in_far
  46.7 14.7 %all-to-all-done.1.rows_ref = bf16[4,384,512]{2,1,0:T(8,128)(2,1)S(1)} async-done(((bf16[4,384,512]{2,1,0:T(8,128)(2,1)}), bf16[4,384,512]{2,1,0:T(8,128)(2,1)S(1)}, u32[]{:S(2)}, u32[]{:S(2)}) %all-to-all-start.1) | async-done | bytes 1572896 | tf_op jit(solution)/shard_map/all_to_all | solution.py:43
  61.4 1.4 copy-done.1
  62.9 4.1 %shard_map.78 = (bf16[4,384,512]{2,1,0:T(8,128)(2,1)S(1)}, f32[384,384]{1,0:T(8,128)S(1)}) custom-call(s32[2]{0:T(128)S(1)} %pad_add_fusion.where_ref, bf16[4,384,512]{2,1,0:T(8,128)(2,1)S(1)} %all-to-all-done.1.rows_ref, bf16[384,2048]{1,0:T(8,128)(2,1)S(1)} %bitcast.33, bf16[192,2048]{1,0:T(8,128)(2,1)S(1)} %bitcast.36, ...), custom_call_target="tpu_custom_call" | custom-call | tf_op jit(solution)/shard_map/pallas_call | solution.py:234
  66.9 20.5 %all_to_all.45.blocks_ref = bf16[4,384,512]{2,1,0:T(8,128)(2,1)S(1)} all-to-all(bf16[4,384,512]{2,1,0:T(8,128)(2,1)S(1)} %get-tuple-element.14), channel_id=1, replica_groups=mesh['expert'=128,'dp'=4] {'dp'}, dimensions={0} | all-to-all | bytes 3145728 | tf_op jit(solution)/shard_map/all_to_all | solution.py:43
  87.5 0.2 shard_map.79
  87.6 21.5 %all_to_all.46 = bf16[64,6,4,128]{3,2,1,0:T(4,128)(2,1)S(1)} all-to-all(bf16[64,6,4,128]{3,2,1,0:T(4,128)(2,1)S(1)} %bitcast.41), channel_id=1, replica_groups={{0,8,16,24,32,40,48,56,64,72,80,88,96,104,112,120,128,136,144,152,160,1..., dimensions={0} | all-to-all | bytes 786432 | tf_op jit(solution)/shard_map/all_to_all | solution.py:31
  109.1 0.1 copy.18
  109.2 0.0 copy-done.6
  109.2 0.0 copy-done.7
  109.2 0.7 shard_map.80
  110.0 19.0 %all_to_all.47 = bf16[64,6,4,128]{3,2,1,0:T(4,128)(2,1)S(1)} all-to-all(bf16[64,6,4,128]{3,2,1,0:T(4,128)(2,1)S(1)} %bitcast.40), channel_id=1, replica_groups={{0,8,16,24,32,40,48,56,64,72,80,88,96,104,112,120,128,136,144,152,160,1..., dimensions={0} | all-to-all | bytes 786432 | tf_op jit(solution)/shard_map/all_to_all | solution.py:31
  129.0 0.1 copy.17
  129.1 0.1 broadcast_in_dim.17
  129.2 0.0 copy-start.2
  129.2 19.5 %all_to_all.48.cot_ref = bf16[4,384,512]{2,1,0:T(8,128)(2,1)S(1)} all-to-all(bf16[4,384,512]{2,1,0:T(8,128)(2,1)S(1)} %broadcast_in_dim.17), channel_id=1, replica_groups=mesh['expert'=128,'dp'=4] {'dp'}, dimensions={0} | all-to-all | bytes 3145728 | tf_op jit(solution)/shard_map/all_to_all | solution.py:43
  148.7 4.4 %shard_map.81 = (bf16[4,384,512]{2,1,0:T(8,128)(2,1)S(1)}, bf16[384,384]{1,0:T(8,128)(2,1)S(1)}) custom-call(s32[2]{0:T(128)S(1)} %pad_add_fusion.where_ref, bf16[4,384,512]{2,1,0:T(8,128)(2,1)S(1)} %all_to_all.48.cot_ref, f32[384,384]{1,0:T(8,128)S(1)} %get-tuple-element.15.proj_ref, bf16[384,2048]{1,0:T(8,128)(2,1)S(1)} %bitcast.34, ...), custom_call_target="tpu_custom_call" | custom-call | tf_op jit(solution)/shard_map/pallas_call | solution.py:234
  153.1 0.0 copy-start.4
  153.1 1.1 copy-done.4
  154.2 4.4 %all-to-all-start.6 = ((bf16[4,384,512]{2,1,0:T(8,128)(2,1)}), bf16[4,384,512]{2,1,0:T(8,128)(2,1)}, u32[]{:S(2)}, u32[]{:S(2)}) async-start(bf16[4,384,512]{2,1,0:T(8,128)(2,1)} %copy-done.4), calls=%async_computation.6 | async-start | bytes 3145728 | tf_op jit(solution)/shard_map/all_to_all | solution.py:43
  158.6 2.8 %shard_map.82 = bf16[384,2048]{1,0:T(8,128)(2,1)} custom-call(s32[2]{0:T(128)S(1)} %pad_add_fusion.where_ref, bf16[4,384,512]{2,1,0:T(8,128)(2,1)S(1)} %all-to-all-done.1.rows_ref, bf16[384,384]{1,0:T(8,128)(2,1)S(1)} %get-tuple-element.17.pre_ref), custom_call_target="tpu_custom_call" | custom-call | tf_op jit(solution)/shard_map/pallas_call | solution.py:234
  161.3 1.9 collective-permute-start.2
  163.3 11.1 %all-to-all-done.6 = bf16[4,384,512]{2,1,0:T(8,128)(2,1)} async-done(((bf16[4,384,512]{2,1,0:T(8,128)(2,1)}), bf16[4,384,512]{2,1,0:T(8,128)(2,1)}, u32[]{:S(2)}, u32[]{:S(2)}) %all-to-all-start.6) | async-done | bytes 1572896 | tf_op jit(solution)/shard_map/all_to_all | solution.py:43
  174.4 1.6 add_convert_fusion
  175.9 0.8 add.24
  176.7 8.5 %all-to-all-start.7 = ((bf16[64,6,4,128]{3,2,1,0:T(4,128)(2,1)}), bf16[64,6,4,128]{3,2,1,0:T(4,128)(2,1)S(1)}, u32[]{:S(2)}, u32[]{:S(2)}) async-start(bf16[64,6,4,128]{3,2,1,0:T(4,128)(2,1)} %add.24), calls=%async_computation.7 | async-start | bytes 786432 | tf_op jit(solution)/shard_map/all_to_all | solution.py:31
  185.2 0.0 collective-permute-done.2.lent_ref
  185.2 3.6 %shard_map.83 = (bf16[384,2048]{1,0:T(8,128)(2,1)}, f32[8,128]{1,0:T(8,128)S(1)}) custom-call(s32[2]{0:T(128)S(1)} %pad_add_fusion.where_ref, bf16[4,384,512]{2,1,0:T(8,128)(2,1)S(1)} %all-to-all-done.1.rows_ref, bf16[384,384]{1,0:T(8,128)(2,1)S(1)} %get-tuple-element.17.pre_ref, bf16[384,2048]{1,0:T(8,128)(2,1)} %collective-permute-done.2.lent_ref), custom_call_target="tpu_custom_call" | custom-call | tf_op jit(solution)/shard_map/pallas_call | solution.py:234
  188.9 10.2 %all-to-all-done.7 = bf16[64,6,4,128]{3,2,1,0:T(4,128)(2,1)S(1)} async-done(((bf16[64,6,4,128]{3,2,1,0:T(4,128)(2,1)}), bf16[64,6,4,128]{3,2,1,0:T(4,128)(2,1)S(1)}, u32[]{:S(2)}, u32[]{:S(2)}) %all-to-all-start.7) | async-done | bytes 393248 | tf_op jit(solution)/shard_map/all_to_all | solution.py:31
  199.1 0.1 copy.16
  199.2 0.3 shard_map.84
  199.5 10.5 %all_to_all.49.parts_ref = bf16[4,128,512]{2,1,0:T(8,128)(2,1)S(1)} all-to-all(bf16[4,128,512]{2,1,0:T(8,128)(2,1)S(1)} %shard_map.84), channel_id=1, replica_groups=mesh['expert'=128,'dp'=4] {'dp'}, dimensions={0} | all-to-all | bytes 1048576 | tf_op jit(solution)/shard_map/all_to_all | solution.py:43
  209.9 0.8 shard_map.85
  (6 shorter events, 0.0 us)
Async XLA Ops:
  0.6 1.0 copy-start
  1.7 0.7 copy-start.5
  3.5 33.1 %all-to-all-start = ((bf16[64,6,4,128]{3,2,1,0:T(4,128)(2,1)}), bf16[64,6,4,128]{3,2,1,0:T(4,128)(2,1)S(1)}, u32[]{:S(2)}, u32[]{:S(2)}) async-start(bf16[64,6,4,128]{3,2,1,0:T(4,128)(2,1)} %bitcast.6), calls=%async_computation | async-start | bytes 786432 | tf_op jit(solution)/shard_map/all_to_all | solution.py:31
  20.0 26.7 %collective-permute-start = (bf16[384,2048]{1,0:T(8,128)(2,1)}, bf16[384,2048]{1,0:T(8,128)(2,1)}, u32[]{:S(2)}, u32[]{:S(2)}) collective-permute-start(bf16[384,2048]{1,0:T(8,128)(2,1)} %bitcast.32), channel_id=1, source_target_pairs={{0,4},{4,0},{8,12},{12,8},{16,20},{20,16},{24,28},{28,24},{32,36},... | collective-permute-start | bytes 4718600 | tf_op jit(solution)/shard_map/ppermute | solution.py:60
  38.0 4.4 %copy-start.3 = (bf16[1,192,2048]{2,1,0:T(8,128)(2,1)S(1)}, bf16[1,192,2048]{2,1,0:T(8,128)(2,1)}, u32[]{:S(2)}) copy-start(bf16[1,192,2048]{2,1,0:T(8,128)(2,1)} %param.11) | copy-start | bytes 2359300
  38.0 23.4 %all-to-all-start.1 = ((bf16[4,384,512]{2,1,0:T(8,128)(2,1)}), bf16[4,384,512]{2,1,0:T(8,128)(2,1)S(1)}, u32[]{:S(2)}, u32[]{:S(2)}) async-start(bf16[4,384,512]{2,1,0:T(8,128)(2,1)} %broadcast_in_dim.15), calls=%async_computation.1 | async-start | bytes 3145728 | tf_op jit(solution)/shard_map/all_to_all | solution.py:43
  42.4 4.3 %collective-permute-start.1 = (bf16[192,2048]{1,0:T(8,128)(2,1)S(1)}, bf16[192,2048]{1,0:T(8,128)(2,1)}, u32[]{:S(2)}, u32[]{:S(2)}) collective-permute-start(bf16[192,2048]{1,0:T(8,128)(2,1)S(1)} %bitcast.35), channel_id=1, source_target_pairs={{0,4},{4,0},{8,12},{12,8},{16,20},{20,16},{24,28},{28,24},{32,36},... | collective-permute-start | bytes 2359304 | tf_op jit(solution)/shard_map/ppermute | solution.py:60
  61.4 1.4 copy-start.1
  87.4 21.8 %copy-start.6 = (f32[128,2]{0,1:T(2,128)S(1)}, f32[128,2]{0,1:T(2,128)}, u32[]{:S(2)}) copy-start(f32[128,2]{0,1:T(2,128)} %param.8) | copy-start | bytes 3076
  87.4 21.8 %copy-start.7 = (f32[128]{0:T(128)S(1)}, f32[128]{0:T(128)}, u32[]{:S(2)}) copy-start(f32[128]{0:T(128)} %param.9) | copy-start | bytes 1540
  129.2 19.5 %copy-start.2 = (bf16[1,2,192,2048]{3,2,1,0:T(8,128)(2,1)S(1)}, bf16[1,2,192,2048]{3,2,1,0:T(8,128)(2,1)}, u32[]{:S(2)}) copy-start(bf16[1,2,192,2048]{3,2,1,0:T(8,128)(2,1)} %param.10) | copy-start | bytes 4718596
  153.1 1.1 copy-start.4
  154.2 20.1 %all-to-all-start.6 = ((bf16[4,384,512]{2,1,0:T(8,128)(2,1)}), bf16[4,384,512]{2,1,0:T(8,128)(2,1)}, u32[]{:S(2)}, u32[]{:S(2)}) async-start(bf16[4,384,512]{2,1,0:T(8,128)(2,1)} %copy-done.4), calls=%async_computation.6 | async-start | bytes 3145728 | tf_op jit(solution)/shard_map/all_to_all | solution.py:43
  161.3 23.9 %collective-permute-start.2 = (bf16[384,2048]{1,0:T(8,128)(2,1)}, bf16[384,2048]{1,0:T(8,128)(2,1)}, u32[]{:S(2)}, u32[]{:S(2)}) collective-permute-start(bf16[384,2048]{1,0:T(8,128)(2,1)} %shard_map.82), channel_id=1, source_target_pairs={{0,4},{4,0},{8,12},{12,8},{16,20},{20,16},{24,28},{28,24},{32,36},... | collective-permute-start | bytes 4718600 | tf_op jit(solution)/shard_map/ppermute | solution.py:60
  176.7 22.4 %all-to-all-start.7 = ((bf16[64,6,4,128]{3,2,1,0:T(4,128)(2,1)}), bf16[64,6,4,128]{3,2,1,0:T(4,128)(2,1)S(1)}, u32[]{:S(2)}, u32[]{:S(2)}) async-start(bf16[64,6,4,128]{3,2,1,0:T(4,128)(2,1)} %add.24), calls=%async_computation.7 | async-start | bytes 786432 | tf_op jit(solution)/shard_map/all_to_all | solution.py:31
